TPU v7x, 32 devices: a whole 2x2x4 slice. The times are simulated.
32 devices in a mesh: groups: 2 (over x), dp: 8 (over z, y), tile: 2 (over core).
Axes of the slice: x: 2, y: 2, z: 4, core: 2. Of those that a mesh axis runs over, the one named last changes fastest.
Arguments:
- coords: bfloat16 [80512, 3, 256], P(('groups', 'dp', 'tile')), parts along dimension 0, may hold values from -4 to 4
- lengths: int32 [32], P('groups'), parts along dimension 0, may hold values from 501 to 2516, as said below
- atom_pairs: int32 [2, 1024], replicated, may hold values from 0 to 255, as said below
Outputs:
- cov_zero: float32 [2048, 1024], P(('groups', 'dp'), 'tile'), parts along dimension 0
- cov_lag: float32 [2048, 1024], P(('groups', 'dp'), 'tile'), parts along dimension 0
There are 2 independent parts, one for each index of `groups`. A program takes and returns all parts, laid end to end along the dimension named above; an argument that names none is the same for every part. Nothing has to cross between parts.
Inputs may be any that keep to these rules, and one draw needn't show every extreme that they name: `lengths`: each trajectory's pair starts, grouped 32 to a block from its first frame, fill 1 to 63 blocks; all trajectories together fill exactly 512 blocks, and one fills 63. `atom_pairs`: each feature names two different atoms.
All inputs are finite; a program needn't handle non-finite values.
Results may differ from a plain program's by a relative error of at most 0.00045.
Values may be sent and summed in bfloat16 or wider, within the bound.
No kernel may reach another device: no remote copies, remote signals or barrier semaphores. Data moves between devices by JAX's collectives and lax.ppermute only.
A program may use at most 128 MiB of HBM per device.

v0:
```python
import jax
import jax.numpy as jnp
from jax import lax
from jax.sharding import PartitionSpec as P

FEATS = 1024
ATOMS = 256
LAG = 500
BLOCK = 32
OUTB = 32
HOMEB = 63


def difference_table(atom_pairs, atom_count):
    atom_ids = jnp.arange(atom_count, dtype=jnp.int32)[:, None]
    first_hit = (atom_ids == atom_pairs[0][None, :]).astype(jnp.float32)
    second_hit = (atom_ids == atom_pairs[1][None, :]).astype(jnp.float32)
    return (first_hit - second_hit).astype(jnp.bfloat16)


def contacts(frames, table):
    number = frames.shape[0]
    flattened = frames.reshape(number * 3, frames.shape[2])
    separation = jnp.dot(flattened, table, preferred_element_type=jnp.float32)
    separation = separation.reshape(number, 3, table.shape[1])
    distance = jnp.sqrt(jnp.sum(separation * separation, axis=1))
    return jax.nn.sigmoid(6.0 * (1.0 - distance)).astype(jnp.bfloat16)


def block_contacts(frames, table):
    number = frames.shape[0]
    portion_rows = min(512, number)
    rounds = -(-number // portion_rows)
    padded = frames
    padded = padded.reshape(rounds, portion_rows, frames.shape[1], frames.shape[2])
    result = lax.map(lambda portion: contacts(portion, table), padded)
    return result.reshape(rounds * portion_rows, -1)


def contract(left_rows, right_rows):
    return lax.dot_general(
        left_rows, right_rows, (((0,), (0,)), ((), ())), preferred_element_type=jnp.float32
    )


def local(coords, lengths, atom_pairs):
    members = lengths.shape[0]
    own_index = lax.axis_index(("dp", "tile"))
    table = difference_table(atom_pairs, coords.shape[2])
    peer_slots = (2 * OUTB + members - 2) // members
    live_blocks = (lengths - LAG + BLOCK - 1) // BLOCK
    offsets = jnp.cumsum(live_blocks) - live_blocks
    peer_ids = jnp.arange(members, dtype=jnp.int32)
    slot_ids = jnp.arange(peer_slots, dtype=jnp.int32)
    sent_blocks = ((peer_ids - offsets[own_index]) % members)[:, None] + members * slot_ids[None, :]
    sent_blocks = jnp.minimum(sent_blocks, HOMEB - 1)
    lag_shift = jnp.array([0, LAG], jnp.int32)
    frame_index = (
        sent_blocks[:, :, None, None] * BLOCK
        + lag_shift[None, None, :, None]
        + jnp.arange(BLOCK, dtype=jnp.int32)[None, None, None, :]
    )
    outgoing = jnp.take(coords, frame_index, axis=0)
    arrived = lax.all_to_all(outgoing, ("dp", "tile"), split_axis=0, concat_axis=0, tiled=True)
    got_blocks = ((own_index - offsets) % members)[:, None] + members * slot_ids[None, :]
    usable = (got_blocks < live_blocks[:, None]).reshape(-1)
    row_limit = jnp.clip(lengths[:, None] - LAG - got_blocks * BLOCK, 0, BLOCK).reshape(-1)
    position = jnp.cumsum(usable.astype(jnp.int32)) - 1
    sources = jnp.arange(members * peer_slots, dtype=jnp.int32)
    targets = jnp.arange(OUTB, dtype=jnp.int32)
    matches = usable[None, :] & (position[None, :] == targets[:, None])
    picked = jnp.sum(jnp.where(matches, sources[None, :], 0), axis=1)
    chosen = jnp.take(arrived.reshape(members * peer_slots, 2 * BLOCK, 3, ATOMS), picked, axis=0)
    features = block_contacts(chosen.reshape(OUTB * 2 * BLOCK, 3, ATOMS), table)
    features = features.reshape(OUTB, 2, BLOCK, FEATS)
    kept_rows = jnp.take(row_limit, picked)
    live_rows = (jnp.arange(BLOCK, dtype=jnp.int32)[None, :] < kept_rows[:, None]).astype(
        jnp.bfloat16
    )[:, :, None]
    leading = (features[:, 0] * live_rows).reshape(OUTB * BLOCK, FEATS)
    lagged = (features[:, 1] * live_rows).reshape(OUTB * BLOCK, FEATS)
    totals = lax.psum(
        (jnp.sum(leading, axis=0, dtype=jnp.float32), jnp.sum(lagged, axis=0, dtype=jnp.float32)),
        ("dp", "tile"),
    )
    pair_total = jnp.sum(lengths - LAG).astype(jnp.float32)
    rows_here = FEATS // lax.axis_size("dp")
    banded = lax.psum_scatter(
        jnp.concatenate([contract(leading, leading), contract(leading, lagged)], axis=1),
        "dp",
        scatter_dimension=0,
        tiled=True,
    )
    halves = lax.psum_scatter(
        banded.reshape(rows_here, 2, FEATS), "tile", scatter_dimension=2, tiled=True
    )
    gram_zero = halves[:, 0, :]
    gram_lag = halves[:, 1, :]
    row_count = gram_zero.shape[0]
    column_count = gram_zero.shape[1]
    row_start = lax.axis_index("dp") * row_count
    column_start = lax.axis_index("tile") * column_count
    mean_lead = totals[0] / pair_total
    mean_lag = totals[1] / pair_total
    row_mean = lax.dynamic_slice_in_dim(mean_lead, row_start, row_count)
    column_lead = lax.dynamic_slice_in_dim(mean_lead, column_start, column_count)
    column_lag = lax.dynamic_slice_in_dim(mean_lag, column_start, column_count)
    cov_zero = gram_zero / pair_total - row_mean[:, None] * column_lead[None, :]
    cov_lag = gram_lag / pair_total - row_mean[:, None] * column_lag[None, :]
    return (cov_zero, cov_lag)


def solution(mesh):
    placed = (P(("groups", "dp", "tile"), None, None), P("groups"), P())
    return jax.shard_map(
        local,
        mesh=mesh,
        in_specs=placed,
        out_specs=(P(("groups", "dp"), "tile"), P(("groups", "dp"), "tile")),
        check_vma=False,
    )
```

profile of v0, /device:TPU:0, one launch (start us, length us, event | category | flops | bytes accessed | tf_op | source)
XLA Modules:
  0.0 483.9 jit_solution(5634615157488448726)
XLA Ops:
  7.2 1.3 fusion.30
  8.5 0.1 copy.34
  8.6 0.1 reduce.2
  8.7 0.6 dynamic_slice.16
  9.3 0.7 and_select_fusion.1
  10.0 0.1 fusion.26
  10.1 0.1 broadcast_add_fusion
  10.2 0.1 compare_select_fusion
  10.3 0.2 compare_and_fusion
  10.5 0.1 reshape.350
  10.6 88.2 %gather_fusion = bf16[4096,3,256]{2,0,1:T(8,128)(2,1)} fusion(bf16[2516,3,256]{2,0,1:T(8,128)(2,1)} %param.6, s32[4096]{0:T(1024)S(1)} %broadcast_clamp_fusion), kind=kCustom, calls=%fused_computation | custom fusion | bytes 12599296 | tf_op jit(solution)/shard_map/jit(_take)/gather | solution.py:63
  98.7 6.1 %copy_select_fusion = bf16[16,4,2,32,3,256]{5,3,2,1,4,0:T(8,128)(2,1)} fusion(bf16[16,4,2,32,3,256]{5,3,2,1,0,4:T(8,128)(2,1)} %bitcast.74, pred[16,4,2,32]{3,2,1,0:T(4,128)(4,1)S(1)} %compare_and_fusion), kind=kLoop, calls=%fused_computation.17 | loop fusion | flops 3145728 | bytes 12587008 | tf_op jit(solution)/shard_map/jit(_take)/select_n | solution.py:63
  104.8 0.0 copy-start
  104.8 7.6 %all-to-all-start = ((bf16[16,4,2,32,3,256]{5,3,2,1,4,0:T(8,128)(2,1)}), bf16[16,4,2,32,3,256]{5,3,2,1,4,0:T(8,128)(2,1)}, u32[]{:S(2)}, u32[]{:S(2)}) async-start(bf16[16,4,2,32,3,256]{5,3,2,1,4,0:T(8,128)(2,1)} %copy_select_fusion), calls=%async_computation | async-start | bytes 12582912 | tf_op jit(solution)/shard_map/all_to_all | solution.py:64
  112.4 0.2 reduce-scatter.3.cloned.1.call-start
  112.6 0.1 add_compare_fusion
  112.7 0.1 reshape.377
  112.8 0.1 reduce-window.18
  112.9 0.1 lt.123
  113.0 0.1 add_reduce_fusion
  113.1 0.1 select_reduce_fusion
  113.2 0.1 reduce_sum.50
  113.3 0.1 broadcast_in_dim.70
  113.4 0.1 broadcast_in_dim.71
  113.5 0.1 min.21
  113.6 0.7 gather_fusion.2
  114.3 0.1 fusion.24
  114.4 0.0 copy-done
  114.4 112.2 %all-to-all-done = bf16[16,4,2,32,3,256]{5,3,2,1,4,0:T(8,128)(2,1)} async-done(((bf16[16,4,2,32,3,256]{5,3,2,1,4,0:T(8,128)(2,1)}), bf16[16,4,2,32,3,256]{5,3,2,1,4,0:T(8,128)(2,1)}, u32[]{:S(2)}, u32[]{:S(2)}) %all-to-all-start) | async-done | bytes 6291488 | tf_op jit(solution)/shard_map/all_to_all | solution.py:64
  226.6 6.8 %copy.37 = bf16[16,4,2,32,3,256]{5,3,2,4,1,0:T(8,128)(2,1)} copy(bf16[16,4,2,32,3,256]{5,3,2,1,4,0:T(8,128)(2,1)} %all-to-all-done) | data formatting | bytes 12582912 | tf_op jit(solution)/shard_map/all_to_all | solution.py:64
  233.4 3.5 gather_fusion.1
  237.0 0.2 copy.38
  237.2 0.5 bitcast_select_fusion
  237.7 12.3 %while.11 = (s32[]{:T(128)}, bf16[4,512,1024]{2,1,0:T(8,128)(2,1)}, bf16[4,512,3,256]{3,1,0,2:T(8,128)(2,1)S(1)}, s32[1024]{0:T(1024)S(1)}, s32[1024]{0:T(1024)S(1)}, /*index=5*/s32[]{:T(128)}) while((s32[]{:T(128)}, bf16[4,512,1024]{2,1,0:T(8,128)(2,1)}, bf16[4,512,3,256]{3,1,0,2:T(8,128)(2,1)S(1)}, s32[1024]{0:T(1024)S(1)}, ...), condition=%wide.region_5.6_spmd.clone, body=%wide.region_3.5_spmd.clone.sunk | while | flops 812646400 | bytes 6038089 | solution.py:36
  237.7 1.1 multiply_reduce_fusion.2
  238.8 2.1 bitcast_dynamic-update-slice_fusion.2
  240.8 1.1 multiply_reduce_fusion.2
  241.9 2.0 bitcast_dynamic-update-slice_fusion.2
  243.9 1.1 multiply_reduce_fusion.2
  244.9 2.0 bitcast_dynamic-update-slice_fusion.2
  246.9 1.1 multiply_reduce_fusion.2
  248.0 2.0 bitcast_dynamic-update-slice_fusion.2
  250.0 4.7 convolution_bitcast_fusion.1
  254.7 4.7 convolution_bitcast_fusion
  259.4 4.1 pad_maximum_fusion
  263.5 0.0 reduce-scatter.3.cloned.1.call-update
  263.5 0.0 reduce-scatter.5.cloned.1.call-start
  263.6 172.9 %reduce-scatter.3.cloned.1.call-done = f32[128,2048]{0,1:T(8,128)} async-done(((f32[1024,2048]{0,1:T(8,128)}), f32[128,2048]{0,1:T(8,128)}) %reduce-scatter.3.cloned.1.call-update) | async-done | bytes 1048592 | tf_op jit(solution)/shard_map/reduce_scatter | solution.py:88
  436.5 2.5 copy.42
  439.0 0.0 reduce-scatter.5.cloned.1.call-update
  439.7 3.1 convert_reduce_fusion
  442.8 32.0 %all-reduce = (f32[1024]{0:T(1024)S(1)}, f32[1024]{0:T(1024)S(1)}) all-reduce(f32[1024]{0:T(1024)S(1)} %get-tuple-element.60, f32[1024]{0:T(1024)S(1)} %get-tuple-element.59), channel_id=1, replica_groups=mesh['groups'=2,'dp'=8,'tile'=2] {'dp','tile'}, use_global_device_ids=true, to_apply=%region_10.11 | all-reduce | flops 2048 | bytes 16384 | tf_op jit(solution)/shard_map/psum | solution.py:82
  474.9 0.1 dynamic_slice.18
  475.0 0.1 dynamic_slice.17
  475.0 0.1 dynamic_slice.19
  475.1 0.0 reduce-scatter.5.cloned.1.call-done
  475.1 1.9 fusion.20
  (12 shorter events, 0.1 us)
Async XLA Ops:
  104.8 9.6 %copy-start = (s32[2,1024]{1,0:T(2,128)S(1)}, s32[2,1024]{1,0:T(2,128)}, u32[]{:S(2)}) copy-start(s32[2,1024]{1,0:T(2,128)} %param.8) | copy-start | bytes 24580
  104.8 121.8 %all-to-all-start = ((bf16[16,4,2,32,3,256]{5,3,2,1,4,0:T(8,128)(2,1)}), bf16[16,4,2,32,3,256]{5,3,2,1,4,0:T(8,128)(2,1)}, u32[]{:S(2)}, u32[]{:S(2)}) async-start(bf16[16,4,2,32,3,256]{5,3,2,1,4,0:T(8,128)(2,1)} %copy_select_fusion), calls=%async_computation | async-start | bytes 12582912 | tf_op jit(solution)/shard_map/all_to_all | solution.py:64
  112.4 324.1 %reduce-scatter.3.cloned.1.call-start = ((), (), s32[]{:S(2)}) async-start(), calls=%async_computation.3 | async-start | bytes 9437184 | tf_op jit(solution)/shard_map/reduce_scatter | solution.py:88
  263.5 211.6 %reduce-scatter.5.cloned.1.call-start = ((), (), s32[]{:S(2)}) async-start(), calls=%async_computation.4 | async-start | bytes 1572864 | tf_op jit(solution)/shard_map/reduce_scatter | solution.py:94
Sparse Core Ops, SparseCore 0:
  263.7 172.7 reduce-scatter.2
  439.2 7.5 reduce-scatter.4
where the time goes:
time: 485 us; the launch traced here: 484 us
  waiting for transfers between devices  285 us (59%)
  local copies, waits for them, and re-layouts  104 us (21%)
  blocking collectives  32 us (7%)
  other arithmetic  26.8 us (6%)
  between operations  14.9 us (3%)
  matrix products  13.7 us (3%)
  starting transfers between devices  7.82 us (2%)
    reduce_scatter x1, waiting for transfers between devices, local(): lax.psum_scatter(jnp.concatenate([contract(leading, leading), contract(le...  173 us
    all_to_all x1, waiting for transfers between devices, local(): lax.all_to_all(outgoing, ('dp', 'tile'), split_axis=0, concat_axis=0, til...  112 us
    gather x1, local copies, waits for them, and re-layouts, local(): outgoing = jnp.take(coords, frame_index, axis=0)  88.2 us
    psum x1, blocking collectives, local(): lax.psum((jnp.sum(leading, axis=0, dtype=jnp.float32), jnp.sum(lagged, ax...  32 us
  transfers between devices with their start and end apart: 3, of which 2 were waited for; matrix products, arithmetic and copies ran while one was open for 1% of the time, Pallas kernels for 0%

commit v1 on v0

v1 whole, which is shorter than its diff:
```python
import functools

import jax
import jax.numpy as jnp
from jax import lax
from jax.experimental import pallas as pl
from jax.experimental.pallas import tpu as pltpu
from jax.sharding import PartitionSpec as P

LAG = 500
FRAME_TILE = 512
FEATURE_TILE = 256
DEPTH_UNIT = 256
SLOPE = 6.0 * 1.4426950408889634
LEVELS = 32752.0
SLACK = 2e-5
FLOOR = 1e-36
VMEM = 52 * 1024 * 1024


def round_up(value, unit):
    return -(-value // unit) * unit


def contacts_kernel(pairs_count, pairs_ref, coords_ref, features_ref, stats_ref, table_ref, *, home):
    step = pl.program_id(0)
    atoms, feats = table_ref.shape
    tile = features_ref.shape[0]

    @pl.when(step == 0)
    def _():
        atom_ids = lax.broadcasted_iota(jnp.int32, (atoms, feats), 0)
        first_hit = (atom_ids == pairs_ref[0:1, :]).astype(jnp.float32)
        second_hit = (atom_ids == pairs_ref[1:2, :]).astype(jnp.float32)
        table_ref[...] = (first_hit - second_hit).astype(jnp.bfloat16)
        stats_ref[...] = jnp.zeros_like(stats_ref)

    live = pairs_count[0]
    frame = step * tile + lax.broadcasted_iota(jnp.int32, (tile, 1), 0)
    lead_rows = (frame < live).astype(jnp.float32)
    lag_rows = ((frame >= LAG) & (frame < live + LAG)).astype(jnp.float32)
    for start in range(0, feats, FEATURE_TILE):
        columns = slice(start, start + FEATURE_TILE)
        weights = table_ref[:, columns]
        squared = None
        for axis in range(3):
            separation = jnp.dot(coords_ref[axis], weights, preferred_element_type=jnp.float32)
            square = separation * separation
            squared = square if squared is None else squared + square
        squared = jnp.maximum(squared, 1e-30)
        distance = squared * lax.rsqrt(squared)
        value = 1.0 / (1.0 + jnp.exp2(distance * SLOPE - SLOPE))
        value = jnp.where(frame < home, value, 0.0).astype(jnp.bfloat16)
        features_ref[:, columns] = value
        value = value.astype(jnp.float32)
        lead = value * lead_rows
        lag = value * lag_rows
        stats_ref[0:1, columns] += jnp.sum(lead, axis=0, keepdims=True)
        stats_ref[1:2, columns] += jnp.sum(lag, axis=0, keepdims=True)
        stats_ref[2:3, columns] += jnp.sum(lead * value, axis=0, keepdims=True)
        stats_ref[3:4, columns] += jnp.sum(lag * value, axis=0, keepdims=True)

    @pl.when(step == pl.num_programs(0) - 1)
    def _():
        totals = stats_ref[0:2, :]
        squares = stats_ref[2:4, :]
        spread = squares - totals * totals / live.astype(jnp.float32)
        stats_ref[2:4, :] = jnp.maximum(spread, 0.0) + (SLACK * squares + FLOOR)


def contact_features(coords, atom_pairs, live, rows):
    home, atoms = coords.shape[1], coords.shape[2]
    feats = atom_pairs.shape[1]
    return pl.pallas_call(
        functools.partial(contacts_kernel, home=home),
        grid=(rows // FRAME_TILE,),
        in_specs=[
            pl.BlockSpec(memory_space=pltpu.SMEM),
            pl.BlockSpec((2, feats), lambda i: (0, 0)),
            pl.BlockSpec((3, FRAME_TILE, atoms), lambda i: (0, i, 0)),
        ],
        out_specs=[
            pl.BlockSpec((FRAME_TILE, feats), lambda i: (i, 0)),
            pl.BlockSpec((8, feats), lambda i: (0, 0)),
        ],
        out_shape=[
            jax.ShapeDtypeStruct((rows, feats), jnp.bfloat16),
            jax.ShapeDtypeStruct((8, feats), jnp.float32),
        ],
        scratch_shapes=[pltpu.VMEM((atoms, feats), jnp.bfloat16)],
        compiler_params=pltpu.CompilerParams(vmem_limit_bytes=VMEM),
        name="contact_features",
    )(live, atom_pairs, coords)


def gram_kernel(scalars, features_ref, stats_ref, kept_ref, sent_ref, lead_ref, right_ref, *, lagged):
    live, side = scalars[0], scalars[1]
    depth, feats = lead_ref.shape
    half = feats // 2
    frame = lax.broadcasted_iota(jnp.int32, (depth, 1), 0)
    lead_ref[...] = jnp.where(frame < live, features_ref[0:depth, :], 0.0).astype(jnp.bfloat16)
    if lagged:
        right_ref[...] = features_ref[LAG : LAG + depth, :]
    else:
        right_ref = lead_ref
    other = 1 if lagged else 0
    stats = stats_ref[...]
    inverse = lax.rsqrt(stats)
    count = live.astype(jnp.float32)
    left_total = jnp.transpose(stats)[:, 0:1]
    left_inverse = jnp.transpose(inverse)[:, 2:3] * LEVELS
    own = pl.ds(pl.multiple_of(side * half, half), half)
    peer = pl.ds(pl.multiple_of((1 - side) * half, half), half)
    own_total = stats_ref[other : other + 1, own] / count
    peer_total = stats_ref[other : other + 1, peer] / count
    peer_inverse = lax.rsqrt(stats_ref[2 + other : 3 + other, peer])
    for start in range(0, feats, FEATURE_TILE):
        rows = slice(start, start + FEATURE_TILE)
        left = lead_ref[:, rows]
        kept = lax.dot_general(
            left, right_ref[:, own], (((0,), (0,)), ((), ())), preferred_element_type=jnp.float32
        )
        kept_ref[rows, :] = kept - left_total[rows] * own_total
        sent = lax.dot_general(
            left, right_ref[:, peer], (((0,), (0,)), ((), ())), preferred_element_type=jnp.float32
        )
        sent = (sent - left_total[rows] * peer_total) * (left_inverse[rows] * peer_inverse)
        sent_ref[rows, :] = jnp.round(sent).astype(jnp.int32).astype(jnp.int16)


def local_gram(features, stats, scalars, depth, lagged):
    rows, feats = features.shape
    whole = pl.BlockSpec(memory_space=pltpu.VMEM)
    return pl.pallas_call(
        functools.partial(gram_kernel, lagged=lagged),
        in_specs=[pl.BlockSpec(memory_space=pltpu.SMEM), whole, whole],
        out_specs=[whole, whole],
        out_shape=[
            jax.ShapeDtypeStruct((feats, feats // 2), jnp.float32),
            jax.ShapeDtypeStruct((feats, feats // 2), jnp.int16),
        ],
        scratch_shapes=[
            pltpu.VMEM((depth, feats), jnp.bfloat16),
            pltpu.VMEM((depth, feats) if lagged else (16, 128), jnp.bfloat16),
        ],
        compiler_params=pltpu.CompilerParams(vmem_limit_bytes=VMEM),
        name="gram_lag" if lagged else "gram_zero",
    )(scalars, features, stats)


def quantize(values, row_spread, column_spread):
    scale = (lax.rsqrt(row_spread) * LEVELS)[..., None] * lax.rsqrt(column_spread)
    return jnp.round(values * scale).astype(jnp.int16)


def restore(values, row_spread, column_spread):
    scale = (jnp.sqrt(row_spread) * (1.0 / LEVELS))[..., None] * jnp.sqrt(column_spread)
    return values.astype(jnp.float32) * scale


def exclusive(size, distance):
    return [(i, i ^ distance) for i in range(size)]


def local(coords, lengths, atom_pairs):
    members = lengths.shape[0]
    feats = atom_pairs.shape[1]
    half = feats // 2
    dp = lax.axis_size("dp")
    far = dp // 2
    block = feats // dp
    home = coords.shape[0]
    depth = round_up(home - LAG, DEPTH_UNIT)
    rows = round_up(max(home, depth + LAG), FRAME_TILE)
    dp_index = lax.axis_index("dp")
    side = lax.axis_index("tile")
    place = dp_index * 2 + side
    near_index = dp_index % 2
    far_index = dp_index // 2
    live = (lengths - LAG).astype(jnp.int32)
    own_live = lax.dynamic_slice_in_dim(live, place, 1)
    scalars = jnp.concatenate([own_live, side[None].astype(jnp.int32)])

    features, stats = contact_features(
        jnp.transpose(coords, (1, 0, 2)), atom_pairs, own_live, rows
    )
    kept_zero, sent_zero = local_gram(features, stats, scalars, depth, False)
    kept_lag, sent_lag = local_gram(features, stats, scalars, depth, True)

    stats = stats[0:4]
    peer_stats = lax.ppermute(stats, "tile", exclusive(2, 1))
    chip_sums = jnp.concatenate([stats[0:2], peer_stats[0:2]], axis=0)
    chip_spread = stats[2:4] + peer_stats[2:4]
    chip = jnp.concatenate([chip_sums, chip_spread], axis=0)
    near_chip = lax.ppermute(chip, "dp", exclusive(dp, 1))
    pair_spread = chip_spread + near_chip[4:6]
    gathered = jnp.concatenate([chip_sums, near_chip[0:4], pair_spread], axis=0)[None]
    distance = 1
    while distance < far:
        other = lax.ppermute(gathered, "dp", exclusive(dp, 2 * distance))
        gathered = jnp.concatenate([gathered, other], axis=0)
        distance *= 2

    def own_columns(vector):
        return lax.dynamic_slice_in_dim(vector, side * half, half, axis=-1)

    def reduce_over_group(kept, sent, which):
        came = lax.ppermute(sent, "tile", exclusive(2, 1))
        total = kept + restore(came, peer_stats[2], own_columns(peer_stats[2 + which]))
        total = total.reshape(far, 2, block, half)
        row_spread = chip_spread[0].reshape(far, 2, block)
        near_spread = near_chip[4].reshape(far, 2, block)
        to_near = lax.dynamic_index_in_dim(total, 1 - near_index, 1, keepdims=False)
        to_near = quantize(
            to_near,
            lax.dynamic_index_in_dim(row_spread, 1 - near_index, 1, keepdims=False),
            own_columns(chip_spread[which]),
        )
        came = lax.ppermute(to_near, "dp", exclusive(dp, 1))
        total = lax.dynamic_index_in_dim(total, near_index, 1, keepdims=False) + restore(
            came,
            lax.dynamic_index_in_dim(near_spread, near_index, 1, keepdims=False),
            own_columns(near_chip[4 + which]),
        )
        row_spread = pair_spread[0].reshape(far, 2, block)
        result = lax.dynamic_index_in_dim(total, far_index, 0, keepdims=False)
        for step in range(1, far):
            target = far_index ^ step
            to_far = quantize(
                lax.dynamic_index_in_dim(total, target, 0, keepdims=False),
                row_spread[target, near_index],
                own_columns(pair_spread[which]),
            )
            came = lax.ppermute(to_far, "dp", exclusive(dp, 2 * step))
            spread = gathered[step, 8].reshape(dp, block)[dp_index]
            result = result + restore(came, spread, own_columns(gathered[step, 8 + which]))
        return result

    within_zero = reduce_over_group(kept_zero, sent_zero, 0)
    within_lag = reduce_over_group(kept_lag, sent_lag, 1)

    pair_total = jnp.sum(live).astype(jnp.float32)
    order = place ^ jnp.arange(members, dtype=jnp.int32)
    weight = jnp.take(live, order).astype(jnp.float32)
    sums = gathered[:, 0:8].reshape(members, 2, feats)
    shift = sums / weight[:, None, None] - jnp.sum(sums, axis=0) / pair_total
    lead_shift = lax.dynamic_slice_in_dim(shift[:, 0], dp_index * block, block, axis=1)
    lead_shift = lead_shift * weight[:, None]
    columns = own_columns(shift)

    def between(right):
        return lax.dot_general(
            lead_shift, right, (((0,), (0,)), ((), ())), precision=lax.Precision.HIGHEST
        )

    cov_zero = (within_zero + between(columns[:, 0])) / pair_total
    cov_lag = (within_lag + between(columns[:, 1])) / pair_total
    return (cov_zero, cov_lag)


def solution(mesh):
    placed = (P(("groups", "dp", "tile"), None, None), P("groups"), P())
    return jax.shard_map(
        local,
        mesh=mesh,
        in_specs=placed,
        out_specs=(P(("groups", "dp"), "tile"), P(("groups", "dp"), "tile")),
        check_vma=False,
    )
```

time: 485 us -> 113 us (0.23)
  waiting for transfers between devices: 285 us -> 38.5 us
  local copies, waits for them, and re-layouts: 104 us -> 4.83 us
  Pallas kernels: 0 us -> 32.2 us
  blocking collectives: 32 us -> 0 us
  other arithmetic: 26.8 us -> 10.9 us
  starting transfers between devices: 7.82 us -> 22.2 us
  between operations: 14.9 us -> 1.68 us
  matrix products: 13.7 us -> 2.39 us
    reduce_scatter x2 -> x0, waiting for transfers between devices: 173 us -> none  [the longest x1 173 us: local(): lax.psum_scatter(jnp.concatenate([contract(leading, leading), contract(le...]
    all_to_all x1 -> x0, waiting for transfers between devices: 112 us -> none  [local(): lax.all_to_all(outgoing, ('dp', 'tile'), split_axis=0, concat_axis=0, til...]
    gather x4 -> x1, local copies, waits for them, and re-layouts: 92.6 us -> 0.66 us  [local(): weight = jnp.take(live, order).astype(jnp.float32)]
    ppermute x0 -> x14, waiting for transfers between devices: none -> 38.5 us  [the longest x2 22.4 us: reduce_over_group(): came = lax.ppermute(to_near, 'dp', exclusive(dp, 1))]
    pallas_call x0 -> x3, Pallas kernels: none -> 32.2 us  [the longest x2 18 us: local_gram(): pl.pallas_call(functools.partial(gram_kernel, lagged=lagged), in_specs=[p...]
    psum x1 -> x0, blocking collectives: 32 us -> none  [local(): lax.psum((jnp.sum(leading, axis=0, dtype=jnp.float32), jnp.sum(lagged, ax...]
    ppermute x0 -> x14, starting transfers between devices: none -> 22.2 us  [the longest x6 11.6 us: reduce_over_group(): came = lax.ppermute(to_far, 'dp', exclusive(dp, 2 * step))]
    dot_general x6 -> x2, matrix products: 13.7 us -> 2.39 us  [between(): lax.dot_general(lead_shift, right, (((0,), (0,)), ((), ())), precision=la...]
  transfers between devices with their start and end apart: 3 -> 14, of which waited for: 2 -> 7; matrix products, arithmetic and copies ran while one was open for 1% -> 8% of each run, Pallas kernels for 0% -> 8%
where the time goes in v1:
time: 113 us
  waiting for transfers between devices  38.5 us (34%)
  Pallas kernels  32.2 us (28%)
  starting transfers between devices  22.2 us (20%)
  other arithmetic  10.9 us (10%)
  local copies, waits for them, and re-layouts  4.83 us (4%)
  matrix products  2.39 us (2%)
  between operations  1.68 us (1%)
    ppermute x2, waiting for transfers between devices, reduce_over_group(): came = lax.ppermute(to_near, 'dp', exclusive(dp, 1))  22.4 us
    pallas_call x2, Pallas kernels, local_gram(): pl.pallas_call(functools.partial(gram_kernel, lagged=lagged), in_specs=[p...  18 us
    pallas_call x1, Pallas kernels, contact_features(): pl.pallas_call(functools.partial(contacts_kernel, home=home), grid=(rows...  14.2 us
    ppermute x6, starting transfers between devices, reduce_over_group(): came = lax.ppermute(to_far, 'dp', exclusive(dp, 2 * step))  11.6 us
    ppermute x6, waiting for transfers between devices, reduce_over_group(): came = lax.ppermute(to_far, 'dp', exclusive(dp, 2 * step))  10.8 us
    ppermute x2, waiting for transfers between devices, local(): other = lax.ppermute(gathered, 'dp', exclusive(dp, 2 * distance))  5.02 us
    ppermute x2, starting transfers between devices, local(): other = lax.ppermute(gathered, 'dp', exclusive(dp, 2 * distance))  4.89 us
    add x1, other arithmetic, reduce_over_group(): kept + restore(came, peer_stats[2], own_columns(peer_stats[2 + which]))  3.47 us
  transfers between devices with their start and end apart: 14, of which 7 were waited for; matrix products, arithmetic and copies ran while one was open for 8% of the time, Pallas kernels for 8%

profile of v1, /device:TPU:0, one launch (start us, length us, event | category | flops | bytes accessed | tf_op | source)
XLA Modules:
  0.0 112.7 jit_solution(6050534113027758638)
XLA Ops:
  0.6 1.3 %fusion.73 = (s32[]{:T(128)}, s32[16]{0:T(128)S(1)}) fusion(s32[16]{0:T(128)} %param.4), kind=kLoop, calls=%fused_computation.125 | loop fusion | flops 31 | bytes 132 | tf_op jit(solution)/shard_map/reduce_sum | solution.py:242
  1.9 0.6 dynamic_slice.126.pairs_count
  2.5 0.6 pad_add_fusion.scalars
  3.1 0.7 copy-done
  3.8 14.2 %contact_features.1 = (bf16[2560,1024]{1,0:T(8,128)(2,1)}, f32[8,1024]{1,0:T(8,128)S(1)}) custom-call(s32[1]{0:T(128)} %dynamic_slice.126.pairs_count, s32[2,1024]{1,0:T(2,128)S(1)} %copy-done, bf16[3,2516,256]{2,1,0:T(8,128)(2,1)} %bitcast.132), custom_call_target="tpu_custom_call" | custom-call | tf_op jit(solution)/shard_map/contact_features/pallas_call | solution.py:74
  18.0 8.9 %gram_lag.1 = (f32[1024,512]{1,0:T(8,128)}, s16[1024,512]{1,0:T(8,128)(2,1)S(1)}) custom-call(s32[2]{0:T(128)S(1)} %pad_add_fusion.scalars, bf16[2560,1024]{1,0:T(8,128)(2,1)} %get-tuple-element.8.features_ref, f32[8,1024]{1,0:T(8,128)S(1)} %get-tuple-element.9.stats_ref), custom_call_target="tpu_custom_call" | custom-call | tf_op jit(solution)/shard_map/gram_lag/pallas_call | solution.py:134
  27.0 0.4 collective-permute-start.9
  27.4 0.1 collective-permute-start.1
  27.5 9.1 %gram_zero.1 = (f32[1024,512]{1,0:T(8,128)}, s16[1024,512]{1,0:T(8,128)(2,1)S(1)}) custom-call(s32[2]{0:T(128)S(1)} %pad_add_fusion.scalars, bf16[2560,1024]{1,0:T(8,128)(2,1)} %get-tuple-element.8.features_ref, f32[8,1024]{1,0:T(8,128)S(1)} %get-tuple-element.9.stats_ref), custom_call_target="tpu_custom_call" | custom-call | tf_op jit(solution)/shard_map/gram_zero/pallas_call | solution.py:134
  36.6 0.4 collective-permute-start
  36.9 0.7 gather_fusion
  37.6 0.6 fusion.66
  38.8 0.0 collective-permute-done.1
  38.9 2.7 %collective-permute-start.3 = (f32[6,1024]{1,0:T(8,128)S(1)}, f32[6,1024]{1,0:T(8,128)S(1)}, u32[]{:S(2)}, u32[]{:S(2)}) collective-permute-start(f32[6,1024]{1,0:T(8,128)S(1)} %pad_maximum_fusion.3), channel_id=1, source_target_pairs={{0,2},{2,0},{4,6},{6,4},{8,10},{10,8},{12,14},{14,12},{1,3},{3,1},... | collective-permute-start | bytes 73736 | tf_op jit(solution)/shard_map/ppermute | solution.py:195
  41.6 0.6 fusion.35
  42.2 0.6 fusion.38
  42.8 0.6 fusion.37
  43.4 0.2 collective-permute-done.3
  43.7 2.0 %collective-permute-start.5 = (f32[1,10,1024]{2,1,0:T(8,128)S(1)}, f32[1,10,1024]{2,1,0:T(8,128)S(1)}, u32[]{:S(2)}, u32[]{:S(2)}) collective-permute-start(f32[1,10,1024]{2,1,0:T(8,128)S(1)} %maximum_bitcast_fusion), channel_id=1, source_target_pairs={{0,4},{2,6},{4,0},{6,2},{8,12},{10,14},{12,8},{14,10},{1,5},{3,7},... | collective-permute-start | bytes 122888 | tf_op jit(solution)/shard_map/ppermute | solution.py:200
  45.7 0.6 fusion.41
  46.3 0.6 fusion.40
  46.9 0.6 fusion.42
  47.5 0.6 fusion.72
  48.1 0.0 collective-permute-done.5
  48.1 2.9 %collective-permute-start.7 = (f32[2,10,1024]{2,1,0:T(8,128)S(1)}, f32[2,10,1024]{2,1,0:T(8,128)S(1)}, u32[]{:S(2)}, u32[]{:S(2)}) collective-permute-start(f32[2,10,1024]{2,1,0:T(8,128)S(1)} %pad_maximum_fusion.2), channel_id=1, source_target_pairs={{0,8},{2,10},{4,12},{6,14},{8,0},{10,2},{12,4},{14,6},{1,9},{3,11}... | collective-permute-start | bytes 245768 | tf_op jit(solution)/shard_map/ppermute | solution.py:200
  51.1 0.6 fusion.71
  51.7 5.0 %collective-permute-done.7 = f32[2,10,1024]{2,1,0:T(8,128)S(1)} collective-permute-done((f32[2,10,1024]{2,1,0:T(8,128)S(1)}, f32[2,10,1024]{2,1,0:T(8,128)S(1)}, u32[]{:S(2)}, u32[]{:S(2)}) %collective-permute-start.7) | collective-permute-done | bytes 81952 | tf_op jit(solution)/shard_map/ppermute | solution.py:200
  56.7 0.1 reshape.231
  56.8 0.1 reduce_sum.18
  56.8 0.8 divide_subtract_fusion
  57.6 0.0 copy-start.1
  57.7 0.0 collective-permute-done.9
  57.7 0.0 collective-permute-done
  57.7 3.5 %multiply_add_fusion = (f32[1024,512]{1,0:T(8,128)S(1)}, f32[1024,512]{1,0:T(8,128)S(1)}) fusion(f32[1024,512]{1,0:T(8,128)} %get-tuple-element.12, s16[1024,512]{1,0:T(8,128)(2,1)S(1)} %collective-permute-done.9, f32[512]{0:T(512)} %bitcast.147, f32[1024]{0:T(1024)S(1)} %bitcast.133, f32[1024,512]{1,0:T(8,128)} %get-tuple-element.10, f32[512]{0:T(512)} %bitcast.146, ...), kind=kLoop, calls=%fused_computation.1 | loop fusion | flops 4194304 | bytes 10493952 | tf_op jit(solution)/shard_map/add | solution.py:209
  61.2 0.0 slice-start
  61.3 0.7 fusion.1
  61.9 1.3 %collective-permute-start.10 = (s16[4,128,512]{2,1,0:T(8,128)(2,1)S(1)}, s16[4,128,512]{2,1,0:T(8,128)(2,1)S(1)}, u32[]{:S(2)}, u32[]{:S(2)}) collective-permute-start(s16[4,128,512]{2,1,0:T(8,128)(2,1)S(1)} %get-tuple-element.47), channel_id=1, source_target_pairs={{0,2},{2,0},{4,6},{6,4},{8,10},{10,8},{12,14},{14,12},{1,3},{3,1},... | collective-permute-start | bytes 1572872 | tf_op jit(solution)/shard_map/ppermute | solution.py:219
  63.2 0.8 collective-permute-start.2
  64.1 0.0 copy-done.10
  64.1 0.0 slice-done
  64.1 0.1 fusion.34
  64.2 12.6 %collective-permute-done.10 = s16[4,128,512]{2,1,0:T(8,128)(2,1)S(1)} collective-permute-done((s16[4,128,512]{2,1,0:T(8,128)(2,1)S(1)}, s16[4,128,512]{2,1,0:T(8,128)(2,1)S(1)}, u32[]{:S(2)}, u32[]{:S(2)}) %collective-permute-start.10) | collective-permute-done | bytes 524320 | tf_op jit(solution)/shard_map/ppermute | solution.py:219
  76.9 9.8 %collective-permute-done.2 = s16[4,128,512]{2,1,0:T(8,128)(2,1)S(1)} collective-permute-done((s16[4,128,512]{2,1,0:T(8,128)(2,1)S(1)}, s16[4,128,512]{2,1,0:T(8,128)(2,1)S(1)}, u32[]{:S(2)}, u32[]{:S(2)}) %collective-permute-start.2) | collective-permute-done | bytes 524320 | tf_op jit(solution)/shard_map/ppermute | solution.py:219
  86.6 0.0 copy-done.5
  86.7 0.5 bitcast_add_fusion
  87.2 0.0 copy-start.2
  87.2 0.1 copy-done.3
  87.3 0.0 copy-done.11
  87.3 0.3 fusion.19
  87.7 2.6 %collective-permute-start.8 = (s16[128,512]{1,0:T(8,128)(2,1)S(1)}, s16[128,512]{1,0:T(8,128)(2,1)S(1)}, u32[]{:S(2)}, u32[]{:S(2)}) collective-permute-start(s16[128,512]{1,0:T(8,128)(2,1)S(1)} %get-tuple-element.18), channel_id=1, source_target_pairs={{0,12},{2,14},{4,8},{6,10},{8,4},{10,6},{12,0},{14,2},{1,13},{3,15... | collective-permute-start | bytes 393224 | tf_op jit(solution)/shard_map/ppermute | solution.py:234
  90.3 0.0 collective-permute-start.6
  90.3 1.9 %collective-permute-start.4 = (s16[128,512]{1,0:T(8,128)(2,1)S(1)}, s16[128,512]{1,0:T(8,128)(2,1)S(1)}, u32[]{:S(2)}, u32[]{:S(2)}) collective-permute-start(s16[128,512]{1,0:T(8,128)(2,1)S(1)} %get-tuple-element.17), channel_id=1, source_target_pairs={{0,4},{2,6},{4,0},{6,2},{8,12},{10,14},{12,8},{14,10},{1,5},{3,7},... | collective-permute-start | bytes 393224 | tf_op jit(solution)/shard_map/ppermute | solution.py:234
  92.2 0.1 constant_dynamic-slice_fusion.8
  92.3 2.6 %collective-permute-start.13 = (s16[128,512]{1,0:T(8,128)(2,1)S(1)}, s16[128,512]{1,0:T(8,128)(2,1)S(1)}, u32[]{:S(2)}, u32[]{:S(2)}) collective-permute-start(s16[128,512]{1,0:T(8,128)(2,1)S(1)} %get-tuple-element.50), channel_id=1, source_target_pairs={{0,12},{2,14},{4,8},{6,10},{8,4},{10,6},{12,0},{14,2},{1,13},{3,15... | collective-permute-start | bytes 393224 | tf_op jit(solution)/shard_map/ppermute | solution.py:234
  94.9 0.0 collective-permute-start.12
  94.9 1.1 collective-permute-done.8
  96.0 4.6 %collective-permute-start.11 = (s16[128,512]{1,0:T(8,128)(2,1)S(1)}, s16[128,512]{1,0:T(8,128)(2,1)S(1)}, u32[]{:S(2)}, u32[]{:S(2)}) collective-permute-start(s16[128,512]{1,0:T(8,128)(2,1)S(1)} %get-tuple-element.51), channel_id=1, source_target_pairs={{0,4},{2,6},{4,0},{6,2},{8,12},{10,14},{12,8},{14,10},{1,5},{3,7},... | collective-permute-start | bytes 393224 | tf_op jit(solution)/shard_map/ppermute | solution.py:234
  100.6 6.3 %collective-permute-done.6 = s16[128,512]{1,0:T(8,128)(2,1)S(1)} collective-permute-done((s16[128,512]{1,0:T(8,128)(2,1)S(1)}, s16[128,512]{1,0:T(8,128)(2,1)S(1)}, u32[]{:S(2)}, u32[]{:S(2)}) %collective-permute-start.6) | collective-permute-done | bytes 131104 | tf_op jit(solution)/shard_map/ppermute | solution.py:234
  106.9 0.0 collective-permute-done.4
  106.9 1.2 %fusion.23 = f32[128,512]{1,0:T(8,128)} fusion(s16[128,512]{1,0:T(8,128)(2,1)S(1)} %collective-permute-done.8, s16[128,512]{1,0:T(8,128)(2,1)S(1)} %collective-permute-done.6, s16[128,512]{1,0:T(8,128)(2,1)S(1)} %collective-permute-done.4, f32[4,128,512]{2,1,0:T(8,128)S(1)} %get-tuple-element.46, s32[]{:T(128)S(6)} %select_n.130, ...), kind=kOutput, calls=%fused_computation.38 | convolution fusion | flops 13500416 | bytes 966152 | tf_op jit(solution)/shard_map/dot_general | solution.py:252
  108.1 0.0 collective-permute-done.13
  108.1 3.5 %collective-permute-done.12 = s16[128,512]{1,0:T(8,128)(2,1)S(1)} collective-permute-done((s16[128,512]{1,0:T(8,128)(2,1)S(1)}, s16[128,512]{1,0:T(8,128)(2,1)S(1)}, u32[]{:S(2)}, u32[]{:S(2)}) %collective-permute-start.12) | collective-permute-done | bytes 131104 | tf_op jit(solution)/shard_map/ppermute | solution.py:234
  111.5 0.0 collective-permute-done.11
  111.5 1.2 %fusion.13 = f32[128,512]{1,0:T(8,128)} fusion(s16[128,512]{1,0:T(8,128)(2,1)S(1)} %collective-permute-done.13, s16[128,512]{1,0:T(8,128)(2,1)S(1)} %collective-permute-done.12, s16[128,512]{1,0:T(8,128)(2,1)S(1)} %collective-permute-done.11, f32[4,128,512]{2,1,0:T(8,128)S(1)} %get-tuple-element.45, s32[]{:T(128)S(6)} %select_n.130, f32[512]{0:T(512)S(1)} %bitcast.157, ...), kind=kOutput, calls=%fused_computation.24 | convolution fusion | flops 13500416 | bytes 966152 | tf_op jit(solution)/shard_map/dot_general | solution.py:252
  (45 shorter events, 0.3 us)
Async XLA Ops:
  3.1 0.7 copy-start
  27.0 30.7 %collective-permute-start.9 = (s16[1024,512]{1,0:T(8,128)(2,1)S(1)}, s16[1024,512]{1,0:T(8,128)(2,1)S(1)}, u32[]{:S(2)}, u32[]{:S(2)}) collective-permute-start(s16[1024,512]{1,0:T(8,128)(2,1)S(1)} %get-tuple-element.13), channel_id=1, source_target_pairs={{0,1},{1,0},{2,3},{3,2},{4,5},{5,4},{6,7},{7,6},{8,9},{9,8},{10,11... | collective-permute-start | bytes 3145736 | tf_op jit(solution)/shard_map/ppermute | solution.py:208
  27.4 11.4 %collective-permute-start.1 = (f32[4,1024]{1,0:T(4,128)S(1)}, f32[4,1024]{1,0:T(4,128)S(1)}, u32[]{:S(2)}, u32[]{:S(2)}) collective-permute-start(f32[4,1024]{1,0:T(4,128)S(1)} %slice.95), channel_id=1, source_target_pairs={{0,1},{1,0},{2,3},{3,2},{4,5},{5,4},{6,7},{7,6},{8,9},{9,8},{10,11... | collective-permute-start | bytes 49160 | tf_op jit(solution)/shard_map/ppermute | solution.py:191
  36.6 21.1 %collective-permute-start = (s16[1024,512]{1,0:T(8,128)(2,1)S(1)}, s16[1024,512]{1,0:T(8,128)(2,1)}, u32[]{:S(2)}, u32[]{:S(2)}) collective-permute-start(s16[1024,512]{1,0:T(8,128)(2,1)S(1)} %get-tuple-element.11), channel_id=1, source_target_pairs={{0,1},{1,0},{2,3},{3,2},{4,5},{5,4},{6,7},{7,6},{8,9},{9,8},{10,11... | collective-permute-start | bytes 3145736 | tf_op jit(solution)/shard_map/ppermute | solution.py:208
  38.9 4.7 %collective-permute-start.3 = (f32[6,1024]{1,0:T(8,128)S(1)}, f32[6,1024]{1,0:T(8,128)S(1)}, u32[]{:S(2)}, u32[]{:S(2)}) collective-permute-start(f32[6,1024]{1,0:T(8,128)S(1)} %pad_maximum_fusion.3), channel_id=1, source_target_pairs={{0,2},{2,0},{4,6},{6,4},{8,10},{10,8},{12,14},{14,12},{1,3},{3,1},... | collective-permute-start | bytes 73736 | tf_op jit(solution)/shard_map/ppermute | solution.py:195
  43.7 4.4 %collective-permute-start.5 = (f32[1,10,1024]{2,1,0:T(8,128)S(1)}, f32[1,10,1024]{2,1,0:T(8,128)S(1)}, u32[]{:S(2)}, u32[]{:S(2)}) collective-permute-start(f32[1,10,1024]{2,1,0:T(8,128)S(1)} %maximum_bitcast_fusion), channel_id=1, source_target_pairs={{0,4},{2,6},{4,0},{6,2},{8,12},{10,14},{12,8},{14,10},{1,5},{3,7},... | collective-permute-start | bytes 122888 | tf_op jit(solution)/shard_map/ppermute | solution.py:200
  48.1 8.5 %collective-permute-start.7 = (f32[2,10,1024]{2,1,0:T(8,128)S(1)}, f32[2,10,1024]{2,1,0:T(8,128)S(1)}, u32[]{:S(2)}, u32[]{:S(2)}) collective-permute-start(f32[2,10,1024]{2,1,0:T(8,128)S(1)} %pad_maximum_fusion.2), channel_id=1, source_target_pairs={{0,8},{2,10},{4,12},{6,14},{8,0},{10,2},{12,4},{14,6},{1,9},{3,11}... | collective-permute-start | bytes 245768 | tf_op jit(solution)/shard_map/ppermute | solution.py:200
  57.6 3.6 %copy-start.1 = (f32[16,2,1024]{2,1,0:T(2,128)}, f32[16,2,1024]{2,1,0:T(2,128)S(1)}, u32[]{:S(2)}) copy-start(f32[16,2,1024]{2,1,0:T(2,128)S(1)} %divide_subtract_fusion) | copy-start | bytes 393220
  57.7 3.6 %copy-start.6 = (f32[1,512]{1,0:T(1,128)S(1)}, f32[1,512]{1,0:T(1,128)}, u32[]{:S(2)}) copy-start(f32[1,512]{1,0:T(1,128)} %get-tuple-element.56) | copy-start | bytes 6148
  57.7 3.6 %copy-start.7 = (f32[1,512]{1,0:T(1,128)S(1)}, f32[1,512]{1,0:T(1,128)}, u32[]{:S(2)}) copy-start(f32[1,512]{1,0:T(1,128)} %get-tuple-element.57) | copy-start | bytes 6148
  57.7 3.6 %copy-start.9 = (f32[4,1,128]{2,1,0:T(1,128)S(1)}, f32[4,1,128]{2,1,0:T(1,128)}, u32[]{:S(2)}) copy-start(f32[4,1,128]{2,1,0:T(1,128)} %fusion.37) | copy-start | bytes 6148
  61.2 2.9 %copy-start.10 = (f32[16]{0:T(128)S(1)}, f32[16]{0:T(128)}, u32[]{:S(2)}) copy-start(f32[16]{0:T(128)} %fusion.66) | copy-start | bytes 196
  61.2 25.4 %copy-start.4 = (f32[1,512]{1,0:T(1,128)S(1)}, f32[1,512]{1,0:T(1,128)}, u32[]{:S(2)}) copy-start(f32[1,512]{1,0:T(1,128)} %get-tuple-element.58) | copy-start | bytes 6148
  61.2 25.4 %copy-start.5 = (f32[1,512]{1,0:T(1,128)S(1)}, f32[1,512]{1,0:T(1,128)}, u32[]{:S(2)}) copy-start(f32[1,512]{1,0:T(1,128)} %get-tuple-element.59) | copy-start | bytes 6148
  61.2 25.4 %copy-start.8 = (f32[4,1,128]{2,1,0:T(1,128)S(1)}, f32[4,1,128]{2,1,0:T(1,128)}, u32[]{:S(2)}) copy-start(f32[4,1,128]{2,1,0:T(1,128)} %fusion.40) | copy-start | bytes 6148
  61.2 2.9 %slice-start = ((f32[16,2,1024]{2,1,0:T(2,128)}), f32[16,1,1024]{2,1,0:T(1,128)S(1)}, s32[]{:S(2)}) async-start(f32[16,2,1024]{2,1,0:T(2,128)} %copy-done.1), calls=%async_computation | async-start | bytes 131072 | tf_op jit(solution)/shard_map/slice | solution.py:247
  61.9 14.9 %collective-permute-start.10 = (s16[4,128,512]{2,1,0:T(8,128)(2,1)S(1)}, s16[4,128,512]{2,1,0:T(8,128)(2,1)S(1)}, u32[]{:S(2)}, u32[]{:S(2)}) collective-permute-start(s16[4,128,512]{2,1,0:T(8,128)(2,1)S(1)} %get-tuple-element.47), channel_id=1, source_target_pairs={{0,2},{2,0},{4,6},{6,4},{8,10},{10,8},{12,14},{14,12},{1,3},{3,1},... | collective-permute-start | bytes 1572872 | tf_op jit(solution)/shard_map/ppermute | solution.py:219
  63.2 23.4 %collective-permute-start.2 = (s16[4,128,512]{2,1,0:T(8,128)(2,1)S(1)}, s16[4,128,512]{2,1,0:T(8,128)(2,1)S(1)}, u32[]{:S(2)}, u32[]{:S(2)}) collective-permute-start(s16[4,128,512]{2,1,0:T(8,128)(2,1)S(1)} %get-tuple-element.48), channel_id=1, source_target_pairs={{0,2},{2,0},{4,6},{6,4},{8,10},{10,8},{12,14},{14,12},{1,3},{3,1},... | collective-permute-start | bytes 1572872 | tf_op jit(solution)/shard_map/ppermute | solution.py:219
  86.6 0.7 copy-start.3
  86.6 0.7 copy-start.11
  86.7 0.7 copy-start.12
  86.7 0.7 copy-start.13
  87.2 4.9 %copy-start.2 = (f32[16,2,1024]{2,1,0:T(2,128)S(1)}, f32[16,2,1024]{2,1,0:T(2,128)}, u32[]{:S(2)}) copy-start(f32[16,2,1024]{2,1,0:T(2,128)} %copy-done.1) | copy-start | bytes 393220
  87.2 19.7 %copy-start.14 = (f32[128]{0:T(128)S(1)}, f32[128]{0:T(128)}, u32[]{:S(2)}) copy-start(f32[128]{0:T(128)} %fusion.71) | copy-start | bytes 1540
  87.7 8.3 %collective-permute-start.8 = (s16[128,512]{1,0:T(8,128)(2,1)S(1)}, s16[128,512]{1,0:T(8,128)(2,1)S(1)}, u32[]{:S(2)}, u32[]{:S(2)}) collective-permute-start(s16[128,512]{1,0:T(8,128)(2,1)S(1)} %get-tuple-element.18), channel_id=1, source_target_pairs={{0,12},{2,14},{4,8},{6,10},{8,4},{10,6},{12,0},{14,2},{1,13},{3,15... | collective-permute-start | bytes 393224 | tf_op jit(solution)/shard_map/ppermute | solution.py:234
  90.3 16.6 %collective-permute-start.6 = (s16[128,512]{1,0:T(8,128)(2,1)S(1)}, s16[128,512]{1,0:T(8,128)(2,1)S(1)}, u32[]{:S(2)}, u32[]{:S(2)}) collective-permute-start(s16[128,512]{1,0:T(8,128)(2,1)S(1)} %get-tuple-element.19), channel_id=1, source_target_pairs={{0,8},{2,10},{4,12},{6,14},{8,0},{10,2},{12,4},{14,6},{1,9},{3,11}... | collective-permute-start | bytes 393224 | tf_op jit(solution)/shard_map/ppermute | solution.py:234
  90.3 16.6 %collective-permute-start.4 = (s16[128,512]{1,0:T(8,128)(2,1)S(1)}, s16[128,512]{1,0:T(8,128)(2,1)S(1)}, u32[]{:S(2)}, u32[]{:S(2)}) collective-permute-start(s16[128,512]{1,0:T(8,128)(2,1)S(1)} %get-tuple-element.17), channel_id=1, source_target_pairs={{0,4},{2,6},{4,0},{6,2},{8,12},{10,14},{12,8},{14,10},{1,5},{3,7},... | collective-permute-start | bytes 393224 | tf_op jit(solution)/shard_map/ppermute | solution.py:234
  92.3 15.8 %collective-permute-start.13 = (s16[128,512]{1,0:T(8,128)(2,1)S(1)}, s16[128,512]{1,0:T(8,128)(2,1)S(1)}, u32[]{:S(2)}, u32[]{:S(2)}) collective-permute-start(s16[128,512]{1,0:T(8,128)(2,1)S(1)} %get-tuple-element.50), channel_id=1, source_target_pairs={{0,12},{2,14},{4,8},{6,10},{8,4},{10,6},{12,0},{14,2},{1,13},{3,15... | collective-permute-start | bytes 393224 | tf_op jit(solution)/shard_map/ppermute | solution.py:234
  94.9 16.6 %collective-permute-start.12 = (s16[128,512]{1,0:T(8,128)(2,1)S(1)}, s16[128,512]{1,0:T(8,128)(2,1)S(1)}, u32[]{:S(2)}, u32[]{:S(2)}) collective-permute-start(s16[128,512]{1,0:T(8,128)(2,1)S(1)} %get-tuple-element.49), channel_id=1, source_target_pairs={{0,8},{2,10},{4,12},{6,14},{8,0},{10,2},{12,4},{14,6},{1,9},{3,11}... | collective-permute-start | bytes 393224 | tf_op jit(solution)/shard_map/ppermute | solution.py:234
  96.0 15.5 %collective-permute-start.11 = (s16[128,512]{1,0:T(8,128)(2,1)S(1)}, s16[128,512]{1,0:T(8,128)(2,1)S(1)}, u32[]{:S(2)}, u32[]{:S(2)}) collective-permute-start(s16[128,512]{1,0:T(8,128)(2,1)S(1)} %get-tuple-element.51), channel_id=1, source_target_pairs={{0,4},{2,6},{4,0},{6,2},{8,12},{10,14},{12,8},{14,10},{1,5},{3,7},... | collective-permute-start | bytes 393224 | tf_op jit(solution)/shard_map/ppermute | solution.py:234

commit v2 on v0

v2 whole, which is shorter than its diff:
```python
import functools

import jax
import jax.numpy as jnp
from jax import lax
from jax.experimental import pallas as pl
from jax.experimental.pallas import tpu as pltpu
from jax.sharding import PartitionSpec as P

LAG = 500
FRAME_TILE = 512
FEATURE_TILE = 256
DEPTH_UNIT = 256
SLOPE = 6.0 * 1.4426950408889634
LEVELS = 32752.0
SLACK = 2e-5
FLOOR = 1e-36
VMEM = 24 * 1024 * 1024
WHOLE = pl.BlockSpec(memory_space=pltpu.VMEM)
SCALARS = pl.BlockSpec(memory_space=pltpu.SMEM)


def round_up(value, unit):
    return -(-value // unit) * unit


def own_place():
    return lax.axis_index("dp") * lax.axis_size("tile") + lax.axis_index("tile")


def params():
    return pltpu.CompilerParams(vmem_limit_bytes=VMEM)


def cost(depth, feats):
    return pl.CostEstimate(flops=depth * feats * feats, bytes_accessed=2 * depth * feats, transcendentals=0)


def shape(dims, dtype=jnp.float32):
    return jax.ShapeDtypeStruct(dims, dtype)


def to_levels(values):
    return jnp.round(values).astype(jnp.int32).astype(jnp.int16)


def from_levels(values):
    return values.astype(jnp.int32).astype(jnp.float32)


def side_columns(half, own):
    side = lax.axis_index("tile")
    return pl.ds(pl.multiple_of((side if own else 1 - side) * half, half), half)


def load_right(features_ref, right_ref, own, lagged):
    depth, half = right_ref.shape
    first = LAG if lagged else 0
    right_ref[...] = features_ref[first : first + depth, side_columns(half, own)]


def gram_rows(features_ref, right_ref, start, live):
    depth = right_ref.shape[0]
    alive = lax.broadcasted_iota(jnp.int32, (depth, 1), 0) < live
    left = jnp.where(alive, features_ref[0:depth, start : start + FEATURE_TILE], 0.0)
    return lax.dot_general(
        left.astype(jnp.bfloat16),
        right_ref[...],
        (((0,), (0,)), ((), ())),
        preferred_element_type=jnp.float32,
    )


def sent_gram(features_ref, stats_ref, sent_ref, right_ref, live, lagged):
    feats, half = sent_ref.shape
    load_right(features_ref, right_ref, False, lagged)
    columns = side_columns(half, False)
    right = 1 if lagged else 0
    left_stats = jnp.transpose(stats_ref[...])
    right_mean = stats_ref[right : right + 1, columns] / live.astype(jnp.float32)
    right_inverse = lax.rsqrt(stats_ref[2:3, columns])
    for start in range(0, feats, FEATURE_TILE):
        rows = slice(start, start + FEATURE_TILE)
        gram = gram_rows(features_ref, right_ref, start, live)
        gram = gram - left_stats[rows, 0:1] * right_mean
        scale = (lax.rsqrt(left_stats[rows, 2:3]) * LEVELS) * right_inverse
        sent_ref[rows, :] = to_levels(gram * scale)


def contacts_kernel(lengths_ref, pairs_ref, coords_ref, features_ref, stats_ref, table_ref):
    step = pl.program_id(0)
    atoms, feats = table_ref.shape
    tile = coords_ref.shape[1]

    @pl.when(step == 0)
    def _():
        atom_ids = lax.broadcasted_iota(jnp.int32, (atoms, feats), 0)
        first_hit = (atom_ids == pairs_ref[0:1, :]).astype(jnp.float32)
        second_hit = (atom_ids == pairs_ref[1:2, :]).astype(jnp.float32)
        table_ref[...] = (first_hit - second_hit).astype(jnp.bfloat16)
        stats_ref[...] = jnp.zeros_like(stats_ref)

    live = lengths_ref[own_place()] - LAG
    frame = step * tile + lax.broadcasted_iota(jnp.int32, (tile, 1), 0)
    used = (frame < live) | ((frame >= LAG) & (frame < live + LAG))
    row = lax.broadcasted_iota(jnp.int32, (8, tile), 0)
    column = step * tile + lax.broadcasted_iota(jnp.int32, (8, tile), 1)
    leads = column < live
    lags = (column >= LAG) & (column < live + LAG)
    masks = ((row == 0) & leads) | ((row == 1) & lags) | ((row == 2) & (leads | lags))
    masks = masks.astype(jnp.float32).astype(jnp.bfloat16)
    target = pl.ds(pl.multiple_of(step * tile, tile), tile)
    for start in range(0, feats, FEATURE_TILE):
        columns = slice(start, start + FEATURE_TILE)
        weights = table_ref[:, columns]
        squared = None
        for axis in range(3):
            separation = jnp.dot(coords_ref[axis], weights, preferred_element_type=jnp.float32)
            square = separation * separation
            squared = square if squared is None else squared + square
        squared = jnp.maximum(squared, 1e-30)
        distance = squared * lax.rsqrt(squared)
        value = pl.reciprocal(1.0 + jnp.exp2(distance * SLOPE - SLOPE), approx=True)
        value = jnp.where(used, value, 0.0).astype(jnp.bfloat16)
        features_ref[target, columns] = value
        stats_ref[:, columns] += jnp.dot(masks, value, preferred_element_type=jnp.float32)
        value = value.astype(jnp.float32)
        stats_ref[3:4, columns] += jnp.sum(value * value, axis=0, keepdims=True)

    @pl.when(step == pl.num_programs(0) - 1)
    def _():
        count = live + jnp.minimum(live, LAG)
        total = stats_ref[2:3, :]
        squares = stats_ref[3:4, :]
        spread = squares - total * total / count.astype(jnp.float32)
        stats_ref[2:3, :] = jnp.maximum(spread, 0.0) + (SLACK * squares + FLOOR)


def contacts_call(coords, lengths, atom_pairs, rows):
    atoms = coords.shape[2]
    feats = atom_pairs.shape[1]
    return pl.pallas_call(
        contacts_kernel,
        grid=(rows // FRAME_TILE,),
        in_specs=[
            SCALARS,
            pl.BlockSpec((2, feats), lambda i: (0, 0)),
            pl.BlockSpec((3, FRAME_TILE, atoms), lambda i: (0, i, 0)),
        ],
        out_specs=[WHOLE, WHOLE],
        out_shape=[shape((rows, feats), jnp.bfloat16), shape((8, feats))],
        scratch_shapes=[pltpu.VMEM((atoms, feats), jnp.bfloat16)],
        compiler_params=params(),
        name="contacts",
    )(lengths, atom_pairs, coords)


def sent_lag_kernel(lengths_ref, features_ref, stats_ref, sent_ref, right_ref):
    live = lengths_ref[own_place()] - LAG
    sent_gram(features_ref, stats_ref, sent_ref, right_ref, live, True)


def sent_zero_kernel(lengths_ref, features_ref, stats_ref, peer_ref, sent_ref, chip_ref, right_ref):
    live = lengths_ref[own_place()] - LAG
    chip_ref[0:2, :] = stats_ref[0:2, :]
    chip_ref[2:4, :] = peer_ref[0:2, :]
    chip_ref[4:8, :] = jnp.broadcast_to(stats_ref[2:3, :] + peer_ref[2:3, :], (4, stats_ref.shape[1]))
    sent_gram(features_ref, stats_ref, sent_ref, right_ref, live, False)


def sent_call(lengths, features, stats, peer, depth):
    feats = features.shape[1]
    sent = shape((feats, feats // 2), jnp.int16)
    operands = [lengths, features, stats] + ([] if peer is None else [peer])
    return pl.pallas_call(
        sent_lag_kernel if peer is None else sent_zero_kernel,
        in_specs=[SCALARS] + [WHOLE] * (len(operands) - 1),
        out_specs=WHOLE if peer is None else [WHOLE, WHOLE],
        out_shape=sent if peer is None else [sent, shape((8, feats))],
        scratch_shapes=[pltpu.VMEM((depth, feats // 2), jnp.bfloat16)],
        compiler_params=params(),
        cost_estimate=cost(depth, feats),
        name="sent_lag" if peer is None else "sent_zero",
    )(*operands)


def near_kernel(lengths_ref, features_ref, stats_ref, peer_ref, came_ref, *refs, lagged, block):
    if lagged:
        keep_ref, sent_ref, right_ref = refs
    else:
        chip_ref, near_ref, _, keep_ref, sent_ref, pair_ref, right_ref = refs
        pair_ref[0, 0:4, :] = chip_ref[0:4, :]
        pair_ref[0, 4:8, :] = near_ref[0:4, :]
        pair_ref[0, 8:16, :] = jnp.broadcast_to(chip_ref[4:5, :] + near_ref[4:5, :], (8, chip_ref.shape[1]))
    live = lengths_ref[own_place()] - LAG
    near = lax.axis_index("dp") % 2
    feats, half = came_ref.shape
    load_right(features_ref, right_ref, True, lagged)
    columns = side_columns(half, True)
    right = 1 if lagged else 0
    chip_spread = stats_ref[2:3, :] + peer_ref[2:3, :]
    left = jnp.concatenate([stats_ref[0:1, :], peer_ref[2:3, :], chip_spread, chip_spread], axis=0)
    left = jnp.transpose(jnp.concatenate([left, left], axis=0))
    right_mean = stats_ref[right : right + 1, columns] / live.astype(jnp.float32)
    came_right = jnp.sqrt(peer_ref[2:3, columns])
    sent_right = lax.rsqrt(stats_ref[2:3, columns] + peer_ref[2:3, columns])
    for start in range(0, feats, FEATURE_TILE):
        rows = slice(start, start + FEATURE_TILE)
        gram = gram_rows(features_ref, right_ref, start, live)
        gram = gram - left[rows, 0:1] * right_mean
        scale = (jnp.sqrt(left[rows, 1:2]) * (1.0 / LEVELS)) * came_right
        gram = gram + from_levels(came_ref[rows, :]) * scale
        spread = left[rows, 2:3]
        for first in range(0, FEATURE_TILE, 2 * block):
            even, odd = slice(first, first + block), slice(first + block, first + 2 * block)
            place = (start + first) // 2
            target = slice(place, place + block)
            keep_ref[target, :] = jnp.where(near == 0, gram[even], gram[odd])
            other = jnp.where(near == 0, gram[odd], gram[even])
            other_spread = jnp.where(near == 0, spread[odd], spread[even])
            scale = (lax.rsqrt(other_spread) * LEVELS) * sent_right
            sent_ref[target, :] = to_levels(other * scale)


def near_call(lengths, features, stats, peer, came, after, depth, block, lagged):
    feats, half = came.shape
    outs = [shape((half, half)), shape((half, half), jnp.int16)]
    specs = [SCALARS] + [WHOLE] * 4
    if not lagged:
        outs.append(shape((1, 16, feats)))
        specs += [WHOLE, WHOLE, pl.BlockSpec(memory_space=pl.ANY)]
    return pl.pallas_call(
        functools.partial(near_kernel, lagged=lagged, block=block),
        in_specs=specs,
        out_specs=[WHOLE] * len(outs),
        out_shape=outs,
        scratch_shapes=[pltpu.VMEM((depth, half), jnp.bfloat16)],
        compiler_params=params(),
        cost_estimate=cost(depth, feats),
        name="kept_lag" if lagged else "kept_zero",
    )(lengths, features, stats, peer, came, *after)


def far_kernel(keep_ref, came_ref, chip_ref, near_ref, *refs, block):
    kept_ref, sent_refs = refs[0], refs[1:-2]
    total_ref, level_ref = refs[-2], refs[-1]
    place = lax.axis_index("dp")
    near, far = place % 2, place // 2
    half = came_ref.shape[0]
    feats = chip_ref.shape[1]
    columns = side_columns(half, True)
    pair = chip_ref[4:5, :] + near_ref[4:5, :]
    left = jnp.concatenate([near_ref[4:5, :], pair] * 4, axis=0)
    left = jnp.transpose(left)
    came_right = jnp.sqrt(near_ref[4:5, columns])
    sent_right = lax.rsqrt(chip_ref[4:5, columns] + near_ref[4:5, columns])
    for index in range(half // block):
        rows = slice(index * block, (index + 1) * block)
        even = left[2 * index * block : (2 * index + 1) * block]
        odd = left[(2 * index + 1) * block : (2 * index + 2) * block]
        mine = jnp.where(near == 0, even, odd)
        scale = (jnp.sqrt(mine[:, 0:1]) * (1.0 / LEVELS)) * came_right
        total = keep_ref[rows, :] + from_levels(came_ref[rows, :]) * scale
        total_ref[index] = total
        scale = (lax.rsqrt(mine[:, 1:2]) * LEVELS) * sent_right
        level_ref[index] = to_levels(total * scale)
    kept_ref[...] = total_ref[far]
    for step, sent_ref in enumerate(sent_refs):
        sent_ref[...] = level_ref[far ^ (step + 1)]


def far_call(keep, came, chip, near, block, name):
    half = came.shape[0]
    far = half // block
    return pl.pallas_call(
        functools.partial(far_kernel, block=block),
        in_specs=[WHOLE] * 4,
        out_specs=[WHOLE] * far,
        out_shape=[shape((block, half))] + [shape((block, half), jnp.int16)] * (far - 1),
        scratch_shapes=[
            pltpu.VMEM((far, block, half), jnp.float32),
            pltpu.VMEM((far, block, half), jnp.int16),
        ],
        compiler_params=params(),
        name=name,
    )(keep, came, chip, near)


def gathered_total(kept_ref, came_refs, left_ref, stats_ref, columns):
    total = kept_ref[...]
    width = stats_ref.shape[1]
    for index, came_ref in enumerate(came_refs):
        spread = width * (index + 1) + 8
        scale = jnp.sqrt(left_ref[:, spread : spread + 1]) * (1.0 / LEVELS)
        scale = scale * jnp.sqrt(stats_ref[index + 1, 8:9, columns])
        total = total + from_levels(came_ref[...]) * scale
    return total


def finish_lag_kernel(lengths_ref, left_ref, stats_ref, kept_ref, *refs):
    came_refs, out_ref, zero_ref = refs[:-2], refs[-2], refs[-1]
    groups, width = stats_ref.shape[0:2]
    members = 4 * groups
    columns = side_columns(kept_ref.shape[1], True)
    place = own_place()
    pair_total = lax.fori_loop(0, members, lambda i, t: t + lengths_ref[i] - LAG, 0)
    pair_total = pair_total.astype(jnp.float32)
    lead_mean = lead_row = lag_row = 0.0
    for group in range(groups):
        for member in range(4):
            first = 2 * member
            lead_mean += left_ref[:, width * group + first : width * group + first + 1]
            lead_row += stats_ref[group, first : first + 1, columns]
            lag_row += stats_ref[group, first + 1 : first + 2, columns]
    lead_mean, lead_row, lag_row = (v / pair_total for v in (lead_mean, lead_row, lag_row))
    lag = gathered_total(kept_ref, came_refs, left_ref, stats_ref, columns)
    zero = jnp.zeros_like(lag)
    for group in range(groups):
        for member in range(4):
            first = 2 * member
            weight = (lengths_ref[place ^ (4 * group + member)] - LAG).astype(jnp.float32)
            lead = left_ref[:, width * group + first : width * group + first + 1]
            lead = lead - lead_mean * weight
            zero = zero + lead * (stats_ref[group, first : first + 1, columns] / weight - lead_row)
            lag = lag + lead * (stats_ref[group, first + 1 : first + 2, columns] / weight - lag_row)
    out_ref[...] = lag / pair_total
    zero_ref[...] = zero


def finish_lag(lengths, left, stats, kept, came):
    return pl.pallas_call(
        finish_lag_kernel,
        in_specs=[SCALARS] + [WHOLE] * (3 + len(came)),
        out_specs=[WHOLE, WHOLE],
        out_shape=[shape(kept.shape), shape(kept.shape)],
        compiler_params=params(),
        name="finish_lag",
    )(lengths, left, stats, kept, *came)


def finish_zero_kernel(lengths_ref, left_ref, stats_ref, between_ref, kept_ref, *refs):
    came_refs, out_ref = refs[:-1], refs[-1]
    members = 4 * stats_ref.shape[0]
    columns = side_columns(kept_ref.shape[1], True)
    pair_total = lax.fori_loop(0, members, lambda i, t: t + lengths_ref[i] - LAG, 0)
    zero = gathered_total(kept_ref, came_refs, left_ref, stats_ref, columns)
    out_ref[...] = (zero + between_ref[...]) / pair_total.astype(jnp.float32)


def finish_zero(lengths, left, stats, between, kept, came):
    return pl.pallas_call(
        finish_zero_kernel,
        in_specs=[SCALARS] + [WHOLE] * (4 + len(came)),
        out_specs=WHOLE,
        out_shape=shape(kept.shape),
        compiler_params=params(),
        name="finish_zero",
    )(lengths, left, stats, between, kept, *came)


def exclusive(size, distance):
    return [(i, i ^ distance) for i in range(size)]


def local(coords, lengths, atom_pairs):
    feats = atom_pairs.shape[1]
    dp = lax.axis_size("dp")
    far = dp // 2
    block = feats // dp
    home = coords.shape[0]
    depth = round_up(home - LAG, DEPTH_UNIT)
    rows = round_up(max(home, depth + LAG), FRAME_TILE)

    def swap(array, axis, distance):
        return lax.ppermute(array, axis, exclusive(lax.axis_size(axis), distance))

    coords = pltpu.with_memory_space_constraint(jnp.transpose(coords, (1, 0, 2)), pltpu.HBM)
    features, stats = contacts_call(coords, lengths, atom_pairs, rows)
    peer = swap(stats, "tile", 1)
    sent_lag = sent_call(lengths, features, stats, None, depth)
    came_lag = swap(sent_lag, "tile", 1)
    sent_zero, chip = sent_call(lengths, features, stats, peer, depth)
    near = swap(chip, "dp", 1)
    came_zero = swap(sent_zero, "tile", 1)
    keep_lag, sent_lag = near_call(
        lengths, features, stats, peer, came_lag, [], depth, block, True
    )
    came_lag = swap(sent_lag, "dp", 1)
    keep_zero, sent_zero, gathered = near_call(
        lengths, features, stats, peer, came_zero, [chip, near, sent_lag], depth, block, False
    )
    came_zero = swap(sent_zero, "dp", 1)

    distance = 1
    while distance < far:
        other = swap(gathered, "dp", 2 * distance)
        gathered = jnp.concatenate([gathered, other], axis=0)
        distance *= 2
    left = lax.dynamic_slice_in_dim(
        gathered.reshape(-1, feats), lax.axis_index("dp") * block, block, axis=1
    ).T

    kept_lag, *sent_lag = far_call(keep_lag, came_lag, chip, near, block, "far_lag")
    came_lag = [swap(s, "dp", 2 * (i + 1)) for i, s in enumerate(sent_lag)]
    kept_zero, *sent_zero = far_call(keep_zero, came_zero, chip, near, block, "far_zero")
    came_zero = [swap(s, "dp", 2 * (i + 1)) for i, s in enumerate(sent_zero)]
    cov_lag, between = finish_lag(lengths, left, gathered, kept_lag, came_lag)
    cov_zero = finish_zero(lengths, left, gathered, between, kept_zero, came_zero)
    return (cov_zero, cov_lag)


def solution(mesh):
    placed = (P(("groups", "dp", "tile"), None, None), P("groups"), P())
    return jax.shard_map(
        local,
        mesh=mesh,
        in_specs=placed,
        out_specs=(P(("groups", "dp"), "tile"), P(("groups", "dp"), "tile")),
        check_vma=False,
    )
```

time: 485 us -> 74.8 us (0.15)
  waiting for transfers between devices: 285 us -> 15.2 us
  local copies, waits for them, and re-layouts: 104 us -> 3.27 us
  Pallas kernels: 0 us -> 36.5 us
  blocking collectives: 32 us -> 0 us
  other arithmetic: 26.8 us -> 0.01 us
  between operations: 14.9 us -> 0.75 us
  matrix products: 13.7 us -> 0 us
  starting transfers between devices: 7.82 us -> 18.8 us
    reduce_scatter x2 -> x0, waiting for transfers between devices: 173 us -> none  [the longest x1 173 us: local(): lax.psum_scatter(jnp.concatenate([contract(leading, leading), contract(le...]
    all_to_all x1 -> x0, waiting for transfers between devices: 112 us -> none  [local(): lax.all_to_all(outgoing, ('dp', 'tile'), split_axis=0, concat_axis=0, til...]
    gather x4 -> x0, local copies, waits for them, and re-layouts: 92.6 us -> none  [the longest x1 88.2 us: local(): outgoing = jnp.take(coords, frame_index, axis=0)]
    pallas_call x0 -> x9, Pallas kernels: none -> 36.5 us  [the longest x1 14.4 us: contacts_call(): pl.pallas_call(contacts_kernel, grid=(rows // FRAME_TILE,), in_specs=[SCA...]
    psum x1 -> x0, blocking collectives: 32 us -> none  [local(): lax.psum((jnp.sum(leading, axis=0, dtype=jnp.float32), jnp.sum(lagged, ax...]
    ppermute x0 -> x14, starting transfers between devices: none -> 18.8 us  [swap(): return lax.ppermute(array, axis, exclusive(lax.axis_size(axis), distance))]
    ppermute x0 -> x14, waiting for transfers between devices: none -> 15.2 us  [swap(): return lax.ppermute(array, axis, exclusive(lax.axis_size(axis), distance))]
    dot_general x6 -> x0, matrix products: 13.7 us -> none  [the longest x2 9.43 us: contract(): lax.dot_general(left_rows, right_rows, (((0,), (0,)), ((), ())), preferre...]
  transfers between devices with their start and end apart: 3 -> 14, of which waited for: 2 -> 4; matrix products, arithmetic and copies ran while one was open for 1% -> 1% of each run, Pallas kernels for 0% -> 28%
where the time goes in v2:
time: 74.8 us; the launch traced here: 74.5 us
  Pallas kernels  36.5 us (49%)
  starting transfers between devices  18.8 us (25%)
  waiting for transfers between devices  15.2 us (20%)
  local copies, waits for them, and re-layouts  3.27 us (4%)
  between operations  0.75 us (1%)
    ppermute x14, starting transfers between devices, swap(): return lax.ppermute(array, axis, exclusive(lax.axis_size(axis), distance))  18.8 us
    ppermute x14, waiting for transfers between devices, swap(): return lax.ppermute(array, axis, exclusive(lax.axis_size(axis), distance))  15.2 us
    pallas_call x1, Pallas kernels, contacts_call(): pl.pallas_call(contacts_kernel, grid=(rows // FRAME_TILE,), in_specs=[SCA...  14.4 us
    pallas_call x2, Pallas kernels, near_call(): pl.pallas_call(functools.partial(near_kernel, lagged=lagged, block=block)...  8.73 us
    pallas_call x2, Pallas kernels, sent_call(): pl.pallas_call(sent_lag_kernel if peer is None else sent_zero_kernel, in_...  6.68 us
    pallas_call x1, Pallas kernels, finish_lag(): pl.pallas_call(finish_lag_kernel, in_specs=[SCALARS] + [WHOLE] * (3 + len...  3.3 us
    unnamed x15, local copies, waits for them, and re-layouts  3.24 us
    pallas_call x2, Pallas kernels, far_call(): pl.pallas_call(functools.partial(far_kernel, block=block), in_specs=[WHOL...  1.89 us
  transfers between devices with their start and end apart: 14, of which 4 were waited for; matrix products, arithmetic and copies ran while one was open for 1% of the time, Pallas kernels for 28%

profile of v2, /device:TPU:0, one launch (start us, length us, event | category | flops | bytes accessed | tf_op | source)
XLA Modules:
  0.0 74.5 jit_solution(15566215055861727209)
XLA Ops:
  0.6 0.0 copy-start.2
  0.6 0.7 copy-done.2
  1.3 0.0 copy-start.3
  1.3 0.7 copy-done.3
  2.0 14.4 %contacts.1 = (bf16[2560,1024]{1,0:T(8,128)(2,1)S(1)}, f32[8,1024]{1,0:T(8,128)S(1)}) custom-call(s32[16]{0:T(128)S(1)} %copy-done.3, s32[2,1024]{1,0:T(2,128)S(1)} %copy-done.2, bf16[3,2516,256]{2,1,0:T(8,128)(2,1)} %bitcast.6), custom_call_target="tpu_custom_call" | custom-call | tf_op jit(solution)/shard_map/contacts/pallas_call | solution.py:142
  16.3 0.5 collective-permute-start
  16.9 3.5 %sent_lag.1 = s16[1024,512]{1,0:T(8,128)(2,1)S(1)} custom-call(s32[16]{0:T(128)S(1)} %copy-done.3, bf16[2560,1024]{1,0:T(8,128)(2,1)S(1)} %get-tuple-element.21.features_ref, f32[8,1024]{1,0:T(8,128)S(1)} %get-tuple-element.22.stats_ref), custom_call_target="tpu_custom_call" | custom-call | flops 2147483648 | bytes 4194304 | tf_op jit(solution)/shard_map/sent_lag/pallas_call | solution.py:175
  20.3 0.1 collective-permute-start.3
  20.4 0.0 collective-permute-done.peer_ref
  20.4 3.2 %sent_zero.1 = (s16[1024,512]{1,0:T(8,128)(2,1)S(1)}, f32[8,1024]{1,0:T(8,128)S(1)}) custom-call(s32[16]{0:T(128)S(1)} %copy-done.3, bf16[2560,1024]{1,0:T(8,128)(2,1)S(1)} %get-tuple-element.21.features_ref, f32[8,1024]{1,0:T(8,128)S(1)} %get-tuple-element.22.stats_ref, f32[8,1024]{1,0:T(8,128)S(1)} %collective-permute-done.peer_ref), custom_call_target="tpu_custom_call" | custom-call | flops 2147483648 | bytes 4194304 | tf_op jit(solution)/shard_map/sent_zero/pallas_call | solution.py:175
  23.7 0.5 collective-permute-start.1
  24.2 2.6 %collective-permute-start.2 = (f32[8,1024]{1,0:T(8,128)S(1)}, f32[8,1024]{1,0:T(8,128)S(1)}, u32[]{:S(2)}, u32[]{:S(2)}) collective-permute-start(f32[8,1024]{1,0:T(8,128)S(1)} %get-tuple-element.24.refs_0_.chip_ref), channel_id=1, source_target_pairs={{0,2},{2,0},{4,6},{6,4},{8,10},{10,8},{12,14},{14,12},{1,3},{3,1},... | collective-permute-start | bytes 98312 | tf_op jit(solution)/shard_map/ppermute | solution.py:375
  26.8 0.0 collective-permute-done.3.came_ref
  26.8 4.5 %kept_lag.1 = (f32[512,512]{1,0:T(8,128)S(1)}, s16[512,512]{1,0:T(8,128)(2,1)}) custom-call(s32[16]{0:T(128)S(1)} %copy-done.3, bf16[2560,1024]{1,0:T(8,128)(2,1)S(1)} %get-tuple-element.21.features_ref, f32[8,1024]{1,0:T(8,128)S(1)} %get-tuple-element.22.stats_ref, f32[8,1024]{1,0:T(8,128)S(1)} %collective-permute-done.peer_ref, ...), custom_call_target="tpu_custom_call" | custom-call | flops 2147483648 | bytes 4194304 | tf_op jit(solution)/shard_map/kept_lag/pallas_call | solution.py:232
  31.3 0.0 copy-start.4
  31.3 0.0 collective-permute-start.6
  31.3 0.0 collective-permute-done.2.refs_1_.near_ref
  31.3 0.0 collective-permute-done.1.came_ref
  31.3 4.3 %kept_zero.1 = (f32[512,512]{1,0:T(8,128)S(1)}, s16[512,512]{1,0:T(8,128)(2,1)}, f32[1,16,1024]{2,1,0:T(8,128)S(1)}) custom-call(s32[16]{0:T(128)S(1)} %copy-done.3, bf16[2560,1024]{1,0:T(8,128)(2,1)S(1)} %get-tuple-element.21.features_ref, f32[8,1024]{1,0:T(8,128)S(1)} %get-tuple-element.22.stats_ref, f32[8,1024]{1,0:T(8,128)S(1)} %collective-permute-done.peer_ref, ...), custom_call_target="tpu_custom_call" | custom-call | flops 2147483648 | bytes 4194304 | tf_op jit(solution)/shard_map/kept_zero/pallas_call | solution.py:232
  35.6 2.0 %collective-permute-start.10 = (s16[512,512]{1,0:T(8,128)(2,1)}, s16[512,512]{1,0:T(8,128)(2,1)S(1)}, u32[]{:S(2)}, u32[]{:S(2)}) collective-permute-start(s16[512,512]{1,0:T(8,128)(2,1)} %get-tuple-element.34), channel_id=1, source_target_pairs={{0,2},{2,0},{4,6},{6,4},{8,10},{10,8},{12,14},{14,12},{1,3},{3,1},... | collective-permute-start | bytes 1572872 | tf_op jit(solution)/shard_map/ppermute | solution.py:375
  37.6 1.6 %collective-permute-start.4 = (f32[1,16,1024]{2,1,0:T(8,128)S(1)}, f32[1,16,1024]{2,1,0:T(8,128)S(1)}, u32[]{:S(2)}, u32[]{:S(2)}) collective-permute-start(f32[1,16,1024]{2,1,0:T(8,128)S(1)} %get-tuple-element.26), channel_id=1, source_target_pairs={{0,4},{2,6},{4,0},{6,2},{8,12},{10,14},{12,8},{14,10},{1,5},{3,7},... | collective-permute-start | bytes 196616 | tf_op jit(solution)/shard_map/ppermute | solution.py:375
  39.1 2.7 %collective-permute-done.4 = f32[1,16,1024]{2,1,0:T(8,128)S(1)} collective-permute-done((f32[1,16,1024]{2,1,0:T(8,128)S(1)}, f32[1,16,1024]{2,1,0:T(8,128)S(1)}, u32[]{:S(2)}, u32[]{:S(2)}) %collective-permute-start.4) | collective-permute-done | bytes 65568 | tf_op jit(solution)/shard_map/ppermute | solution.py:375
  41.8 0.0 copy-start.5
  41.8 2.7 %collective-permute-start.5 = (f32[2,16,1024]{2,1,0:T(8,128)S(1)}, f32[2,16,1024]{2,1,0:T(8,128)S(1)}, u32[]{:S(2)}, u32[]{:S(2)}) collective-permute-start(f32[2,16,1024]{2,1,0:T(8,128)S(1)} %pad_maximum_fusion), channel_id=1, source_target_pairs={{0,8},{2,10},{4,12},{6,14},{8,0},{10,2},{12,4},{14,6},{1,9},{3,11}... | collective-permute-start | bytes 393224 | tf_op jit(solution)/shard_map/ppermute | solution.py:375
  44.5 1.8 %collective-permute-done.6.came_ref = s16[512,512]{1,0:T(8,128)(2,1)S(1)} collective-permute-done((s16[512,512]{1,0:T(8,128)(2,1)}, s16[512,512]{1,0:T(8,128)(2,1)S(1)}, u32[]{:S(2)}, u32[]{:S(2)}) %collective-permute-start.6) | collective-permute-done | bytes 524320 | tf_op jit(solution)/shard_map/ppermute | solution.py:375
  46.3 0.0 copy-done.5
  46.3 1.3 %far_lag.1 = (f32[128,512]{1,0:T(8,128)S(1)}, s16[128,512]{1,0:T(8,128)(2,1)S(1)}, s16[128,512]{1,0:T(8,128)(2,1)}, s16[128,512]{1,0:T(8,128)(2,1)}) custom-call(f32[512,512]{1,0:T(8,128)S(1)} %get-tuple-element.27.keep_ref, s16[512,512]{1,0:T(8,128)(2,1)S(1)} %collective-permute-done.6.came_ref, f32[8,1024]{1,0:T(8,128)S(1)} %get-tuple-element.24.refs_0_.chip_ref, ...), custom_call_target="tpu_custom_call" | custom-call | tf_op jit(solution)/shard_map/far_lag/pallas_call | solution.py:275
  47.6 0.0 copy-start
  47.6 1.6 %collective-permute-start.7 = (s16[128,512]{1,0:T(8,128)(2,1)S(1)}, s16[128,512]{1,0:T(8,128)(2,1)S(1)}, u32[]{:S(2)}, u32[]{:S(2)}) collective-permute-start(s16[128,512]{1,0:T(8,128)(2,1)S(1)} %get-tuple-element.29), channel_id=1, source_target_pairs={{0,4},{2,6},{4,0},{6,2},{8,12},{10,14},{12,8},{14,10},{1,5},{3,7},... | collective-permute-start | bytes 393224 | tf_op jit(solution)/shard_map/ppermute | solution.py:375
  49.1 0.8 %constant_dynamic-update-slice_fusion.1 = f32[4,16,1024]{2,1,0:T(8,128)S(1)} fusion(f32[4,16,1024]{2,1,0:T(8,128)S(1)} %constant_dynamic-update-slice_fusion.2, f32[1,16,1024]{2,1,0:T(8,128)} %copy-done.5), kind=kLoop, calls=%fused_computation.2 | loop fusion | bytes 131072
  50.0 2.6 %collective-permute-start.8 = (s16[128,512]{1,0:T(8,128)(2,1)}, s16[128,512]{1,0:T(8,128)(2,1)S(1)}, u32[]{:S(2)}, u32[]{:S(2)}) collective-permute-start(s16[128,512]{1,0:T(8,128)(2,1)} %get-tuple-element.30), channel_id=1, source_target_pairs={{0,8},{2,10},{4,12},{6,14},{8,0},{10,2},{12,4},{14,6},{1,9},{3,11}... | collective-permute-start | bytes 393224 | tf_op jit(solution)/shard_map/ppermute | solution.py:375
  52.6 0.2 collective-permute-start.9
  52.8 3.9 %collective-permute-done.10.came_ref = s16[512,512]{1,0:T(8,128)(2,1)S(1)} collective-permute-done((s16[512,512]{1,0:T(8,128)(2,1)}, s16[512,512]{1,0:T(8,128)(2,1)S(1)}, u32[]{:S(2)}, u32[]{:S(2)}) %collective-permute-start.10) | collective-permute-done | bytes 524320 | tf_op jit(solution)/shard_map/ppermute | solution.py:375
  56.7 0.6 far_zero.1
  57.3 1.6 %collective-permute-start.11 = (s16[128,512]{1,0:T(8,128)(2,1)S(1)}, s16[128,512]{1,0:T(8,128)(2,1)S(1)}, u32[]{:S(2)}, u32[]{:S(2)}) collective-permute-start(s16[128,512]{1,0:T(8,128)(2,1)S(1)} %get-tuple-element.36), channel_id=1, source_target_pairs={{0,4},{2,6},{4,0},{6,2},{8,12},{10,14},{12,8},{14,10},{1,5},{3,7},... | collective-permute-start | bytes 393224 | tf_op jit(solution)/shard_map/ppermute | solution.py:375
  59.0 0.0 collective-permute-done.5
  59.0 2.6 %collective-permute-start.12 = (s16[128,512]{1,0:T(8,128)(2,1)S(1)}, s16[128,512]{1,0:T(8,128)(2,1)S(1)}, u32[]{:S(2)}, u32[]{:S(2)}) collective-permute-start(s16[128,512]{1,0:T(8,128)(2,1)S(1)} %get-tuple-element.37), channel_id=1, source_target_pairs={{0,8},{2,10},{4,12},{6,14},{8,0},{10,2},{12,4},{14,6},{1,9},{3,11}... | collective-permute-start | bytes 393224 | tf_op jit(solution)/shard_map/ppermute | solution.py:375
  61.6 0.0 collective-permute-done.7.refs_0_
  61.6 0.2 collective-permute-start.13
  61.8 0.0 copy-done
  61.8 0.1 copy.6
  61.9 0.0 collective-permute-done.8.refs_1_
  61.9 0.0 collective-permute-done.9.refs_2_
  62.0 0.0 copy-done.4
  62.0 0.0 copy-start.1
  62.0 0.9 %copy-done.1 = f32[128,512]{1,0:T(8,128)S(1)} copy-done((f32[128,512]{1,0:T(8,128)S(1)}, f32[128,512]{1,0:T(8,128)}, u32[]{:S(2)}) %copy-start.1) | copy-done | bytes 262168
  62.9 3.3 %finish_lag.1 = (f32[128,512]{1,0:T(8,128)}, f32[128,512]{1,0:T(8,128)S(1)}) custom-call(s32[16]{0:T(128)S(1)} %copy-done.4, f32[128,64]{1,0:T(8,128)S(1)} %bitcast.4, f32[4,16,1024]{2,1,0:T(8,128)S(1)} %constant_dynamic-update-slice_fusion.stats_ref, f32[128,512]{1,0:T(8,128)S(1)} %copy-done.1, s16[128,512]{1,0:T(8,128)(2,1)S(1)} %collective-permute-done.7.refs_0_, ...), custom_call_target="tpu_custom_call" | custom-call | tf_op jit(solution)/shard_map/finish_lag/pallas_call | solution.py:331
  66.2 0.0 collective-permute-done.11.refs_0_
  66.2 6.8 %collective-permute-done.12.refs_1_ = s16[128,512]{1,0:T(8,128)(2,1)S(1)} collective-permute-done((s16[128,512]{1,0:T(8,128)(2,1)S(1)}, s16[128,512]{1,0:T(8,128)(2,1)S(1)}, u32[]{:S(2)}, u32[]{:S(2)}) %collective-permute-start.12) | collective-permute-done | bytes 131104 | tf_op jit(solution)/shard_map/ppermute | solution.py:375
  73.0 0.0 collective-permute-done.13.refs_2_
  73.0 1.5 %finish_zero.1 = f32[128,512]{1,0:T(8,128)} custom-call(s32[16]{0:T(128)S(1)} %copy-done.4, f32[128,64]{1,0:T(8,128)S(1)} %bitcast.5, f32[4,16,1024]{2,1,0:T(8,128)S(1)} %constant_dynamic-update-slice_fusion.stats_ref, f32[128,512]{1,0:T(8,128)S(1)} %get-tuple-element.32.between_ref, f32[128,512]{1,0:T(8,128)S(1)} %get-tuple-element.35.kept_ref, ...), custom_call_target="tpu_custom_call" | custom-call | tf_op jit(solution)/shard_map/finish_zero/pallas_call | solution.py:351
  (4 shorter events, 0.0 us)
Async XLA Ops:
  0.6 0.7 copy-start.2
  1.3 0.7 copy-start.3
  16.3 4.1 %collective-permute-start = (f32[8,1024]{1,0:T(8,128)S(1)}, f32[8,1024]{1,0:T(8,128)S(1)}, u32[]{:S(2)}, u32[]{:S(2)}) collective-permute-start(f32[8,1024]{1,0:T(8,128)S(1)} %get-tuple-element.22.stats_ref), channel_id=1, source_target_pairs={{0,1},{1,0},{2,3},{3,2},{4,5},{5,4},{6,7},{7,6},{8,9},{9,8},{10,11... | collective-permute-start | bytes 98312 | tf_op jit(solution)/shard_map/ppermute | solution.py:375
  20.3 6.5 %collective-permute-start.3 = (s16[1024,512]{1,0:T(8,128)(2,1)S(1)}, s16[1024,512]{1,0:T(8,128)(2,1)S(1)}, u32[]{:S(2)}, u32[]{:S(2)}) collective-permute-start(s16[1024,512]{1,0:T(8,128)(2,1)S(1)} %sent_lag.1), channel_id=1, source_target_pairs={{0,1},{1,0},{2,3},{3,2},{4,5},{5,4},{6,7},{7,6},{8,9},{9,8},{10,11... | collective-permute-start | bytes 3145736 | tf_op jit(solution)/shard_map/ppermute | solution.py:375
  23.7 7.6 %collective-permute-start.1 = (s16[1024,512]{1,0:T(8,128)(2,1)S(1)}, s16[1024,512]{1,0:T(8,128)(2,1)S(1)}, u32[]{:S(2)}, u32[]{:S(2)}) collective-permute-start(s16[1024,512]{1,0:T(8,128)(2,1)S(1)} %get-tuple-element.23), channel_id=1, source_target_pairs={{0,1},{1,0},{2,3},{3,2},{4,5},{5,4},{6,7},{7,6},{8,9},{9,8},{10,11... | collective-permute-start | bytes 3145736 | tf_op jit(solution)/shard_map/ppermute | solution.py:375
  24.2 7.1 %collective-permute-start.2 = (f32[8,1024]{1,0:T(8,128)S(1)}, f32[8,1024]{1,0:T(8,128)S(1)}, u32[]{:S(2)}, u32[]{:S(2)}) collective-permute-start(f32[8,1024]{1,0:T(8,128)S(1)} %get-tuple-element.24.refs_0_.chip_ref), channel_id=1, source_target_pairs={{0,2},{2,0},{4,6},{6,4},{8,10},{10,8},{12,14},{14,12},{1,3},{3,1},... | collective-permute-start | bytes 98312 | tf_op jit(solution)/shard_map/ppermute | solution.py:375
  31.3 30.7 %copy-start.4 = (s32[16]{0:T(128)S(1)}, s32[16]{0:T(128)}, u32[]{:S(2)}) copy-start(s32[16]{0:T(128)} %lengths_ref.13) | copy-start | bytes 196
  31.3 15.0 %collective-permute-start.6 = (s16[512,512]{1,0:T(8,128)(2,1)}, s16[512,512]{1,0:T(8,128)(2,1)S(1)}, u32[]{:S(2)}, u32[]{:S(2)}) collective-permute-start(s16[512,512]{1,0:T(8,128)(2,1)} %get-tuple-element.25.refs_2_), channel_id=1, source_target_pairs={{0,2},{2,0},{4,6},{6,4},{8,10},{10,8},{12,14},{14,12},{1,3},{3,1},... | collective-permute-start | bytes 1572872 | tf_op jit(solution)/shard_map/ppermute | solution.py:375
  35.6 21.2 %collective-permute-start.10 = (s16[512,512]{1,0:T(8,128)(2,1)}, s16[512,512]{1,0:T(8,128)(2,1)S(1)}, u32[]{:S(2)}, u32[]{:S(2)}) collective-permute-start(s16[512,512]{1,0:T(8,128)(2,1)} %get-tuple-element.34), channel_id=1, source_target_pairs={{0,2},{2,0},{4,6},{6,4},{8,10},{10,8},{12,14},{14,12},{1,3},{3,1},... | collective-permute-start | bytes 1572872 | tf_op jit(solution)/shard_map/ppermute | solution.py:375
  37.6 4.3 %collective-permute-start.4 = (f32[1,16,1024]{2,1,0:T(8,128)S(1)}, f32[1,16,1024]{2,1,0:T(8,128)S(1)}, u32[]{:S(2)}, u32[]{:S(2)}) collective-permute-start(f32[1,16,1024]{2,1,0:T(8,128)S(1)} %get-tuple-element.26), channel_id=1, source_target_pairs={{0,4},{2,6},{4,0},{6,2},{8,12},{10,14},{12,8},{14,10},{1,5},{3,7},... | collective-permute-start | bytes 196616 | tf_op jit(solution)/shard_map/ppermute | solution.py:375
  41.8 4.4 %copy-start.5 = (f32[1,16,1024]{2,1,0:T(8,128)}, f32[1,16,1024]{2,1,0:T(8,128)S(1)}, u32[]{:S(2)}) copy-start(f32[1,16,1024]{2,1,0:T(8,128)S(1)} %collective-permute-done.4) | copy-start | bytes 196612
  41.8 17.1 %collective-permute-start.5 = (f32[2,16,1024]{2,1,0:T(8,128)S(1)}, f32[2,16,1024]{2,1,0:T(8,128)S(1)}, u32[]{:S(2)}, u32[]{:S(2)}) collective-permute-start(f32[2,16,1024]{2,1,0:T(8,128)S(1)} %pad_maximum_fusion), channel_id=1, source_target_pairs={{0,8},{2,10},{4,12},{6,14},{8,0},{10,2},{12,4},{14,6},{1,9},{3,11}... | collective-permute-start | bytes 393224 | tf_op jit(solution)/shard_map/ppermute | solution.py:375
  47.6 14.3 %copy-start = (f32[128,512]{1,0:T(8,128)}, f32[128,512]{1,0:T(8,128)S(1)}, u32[]{:S(2)}) copy-start(f32[128,512]{1,0:T(8,128)S(1)} %get-tuple-element.28.kept_ref) | copy-start | bytes 786436
  47.6 14.0 %collective-permute-start.7 = (s16[128,512]{1,0:T(8,128)(2,1)S(1)}, s16[128,512]{1,0:T(8,128)(2,1)S(1)}, u32[]{:S(2)}, u32[]{:S(2)}) collective-permute-start(s16[128,512]{1,0:T(8,128)(2,1)S(1)} %get-tuple-element.29), channel_id=1, source_target_pairs={{0,4},{2,6},{4,0},{6,2},{8,12},{10,14},{12,8},{14,10},{1,5},{3,7},... | collective-permute-start | bytes 393224 | tf_op jit(solution)/shard_map/ppermute | solution.py:375
  50.0 12.0 %collective-permute-start.8 = (s16[128,512]{1,0:T(8,128)(2,1)}, s16[128,512]{1,0:T(8,128)(2,1)S(1)}, u32[]{:S(2)}, u32[]{:S(2)}) collective-permute-start(s16[128,512]{1,0:T(8,128)(2,1)} %get-tuple-element.30), channel_id=1, source_target_pairs={{0,8},{2,10},{4,12},{6,14},{8,0},{10,2},{12,4},{14,6},{1,9},{3,11}... | collective-permute-start | bytes 393224 | tf_op jit(solution)/shard_map/ppermute | solution.py:375
  52.6 9.4 %collective-permute-start.9 = (s16[128,512]{1,0:T(8,128)(2,1)}, s16[128,512]{1,0:T(8,128)(2,1)S(1)}, u32[]{:S(2)}, u32[]{:S(2)}) collective-permute-start(s16[128,512]{1,0:T(8,128)(2,1)} %get-tuple-element.31), channel_id=1, source_target_pairs={{0,12},{2,14},{4,8},{6,10},{8,4},{10,6},{12,0},{14,2},{1,13},{3,15... | collective-permute-start | bytes 393224 | tf_op jit(solution)/shard_map/ppermute | solution.py:375
  57.3 8.9 %collective-permute-start.11 = (s16[128,512]{1,0:T(8,128)(2,1)S(1)}, s16[128,512]{1,0:T(8,128)(2,1)S(1)}, u32[]{:S(2)}, u32[]{:S(2)}) collective-permute-start(s16[128,512]{1,0:T(8,128)(2,1)S(1)} %get-tuple-element.36), channel_id=1, source_target_pairs={{0,4},{2,6},{4,0},{6,2},{8,12},{10,14},{12,8},{14,10},{1,5},{3,7},... | collective-permute-start | bytes 393224 | tf_op jit(solution)/shard_map/ppermute | solution.py:375
  59.0 14.0 %collective-permute-start.12 = (s16[128,512]{1,0:T(8,128)(2,1)S(1)}, s16[128,512]{1,0:T(8,128)(2,1)S(1)}, u32[]{:S(2)}, u32[]{:S(2)}) collective-permute-start(s16[128,512]{1,0:T(8,128)(2,1)S(1)} %get-tuple-element.37), channel_id=1, source_target_pairs={{0,8},{2,10},{4,12},{6,14},{8,0},{10,2},{12,4},{14,6},{1,9},{3,11}... | collective-permute-start | bytes 393224 | tf_op jit(solution)/shard_map/ppermute | solution.py:375
  61.6 11.4 %collective-permute-start.13 = (s16[128,512]{1,0:T(8,128)(2,1)S(1)}, s16[128,512]{1,0:T(8,128)(2,1)S(1)}, u32[]{:S(2)}, u32[]{:S(2)}) collective-permute-start(s16[128,512]{1,0:T(8,128)(2,1)S(1)} %get-tuple-element.38), channel_id=1, source_target_pairs={{0,12},{2,14},{4,8},{6,10},{8,4},{10,6},{12,0},{14,2},{1,13},{3,15... | collective-permute-start | bytes 393224 | tf_op jit(solution)/shard_map/ppermute | solution.py:375
  62.0 1.0 %copy-start.1 = (f32[128,512]{1,0:T(8,128)S(1)}, f32[128,512]{1,0:T(8,128)}, u32[]{:S(2)}) copy-start(f32[128,512]{1,0:T(8,128)} %copy-done) | copy-start | bytes 786436

commit v3 on v2

v3 whole, which is shorter than its diff:
```python
import functools

import jax
import jax.numpy as jnp
from jax import lax
from jax.experimental import pallas as pl
from jax.experimental.pallas import tpu as pltpu
from jax.sharding import PartitionSpec as P

LAG = 500
FRAME_TILE = 512
FEATURE_TILE = 256
DEPTH_UNIT = 256
SLOPE = 6.0 * 1.4426950408889634
LEVELS = 32752.0
SLACK = 2e-5
FLOOR = 1e-36
LONG = 1 << 31
VMEM = 12 * 1024 * 1024
WHOLE = pl.BlockSpec(memory_space=pltpu.VMEM)
SCALARS = pl.BlockSpec(memory_space=pltpu.SMEM)


def round_up(value, unit):
    return -(-value // unit) * unit


def own_place():
    return lax.axis_index("dp") * lax.axis_size("tile") + lax.axis_index("tile")


def params():
    return pltpu.CompilerParams(vmem_limit_bytes=VMEM)


def shape(dims, dtype=jnp.float32):
    return jax.ShapeDtypeStruct(dims, dtype)


def to_levels(values):
    return jnp.round(values).astype(jnp.int32).astype(jnp.int16)


def from_levels(values):
    return values.astype(jnp.int32).astype(jnp.float32)


def side_columns(half, own):
    side = lax.axis_index("tile")
    return pl.ds(pl.multiple_of((side if own else 1 - side) * half, half), half)


def load_right(features_ref, right_ref, own, lagged):
    depth, half = right_ref.shape
    first = LAG if lagged else 0
    right_ref[...] = features_ref[first : first + depth, side_columns(half, own)]


def gram_rows(features_ref, right_ref, start, live):
    depth = right_ref.shape[0]
    alive = lax.broadcasted_iota(jnp.int32, (depth, 1), 0) < live
    left = jnp.where(alive, features_ref[0:depth, start : start + FEATURE_TILE], 0.0)
    return lax.dot_general(
        left.astype(jnp.bfloat16),
        right_ref[...],
        (((0,), (0,)), ((), ())),
        preferred_element_type=jnp.float32,
    )


def contacts_kernel(lengths_ref, pairs_ref, coords_ref, features_ref, stats_ref, table_ref):
    step = pl.program_id(0)
    atoms, feats = table_ref.shape
    tile = coords_ref.shape[1]

    @pl.when(step == 0)
    def _():
        atom_ids = lax.broadcasted_iota(jnp.int32, (atoms, feats), 0)
        first_hit = (atom_ids == pairs_ref[0:1, :]).astype(jnp.float32)
        second_hit = (atom_ids == pairs_ref[1:2, :]).astype(jnp.float32)
        table_ref[...] = (first_hit - second_hit).astype(jnp.bfloat16)
        stats_ref[...] = jnp.zeros_like(stats_ref)

    live = lengths_ref[own_place()] - LAG
    frame = step * tile + lax.broadcasted_iota(jnp.int32, (tile, 1), 0)
    used = (frame < live) | ((frame >= LAG) & (frame < live + LAG))
    leads = (step * tile + tile <= live).astype(jnp.float32)
    target = pl.ds(pl.multiple_of(step * tile, tile), tile)
    for start in range(0, feats, FEATURE_TILE):
        columns = slice(start, start + FEATURE_TILE)
        weights = table_ref[:, columns]
        squared = None
        for axis in range(3):
            separation = jnp.dot(coords_ref[axis], weights, preferred_element_type=jnp.float32)
            square = separation * separation
            squared = square if squared is None else squared + square
        squared = jnp.maximum(squared, 1e-30)
        distance = squared * lax.rsqrt(squared)
        value = pl.reciprocal(1.0 + jnp.exp2(distance * SLOPE - SLOPE), approx=True)
        value = jnp.where(used, value, 0.0).astype(jnp.bfloat16)
        features_ref[target, columns] = value
        value = value.astype(jnp.float32)
        total = jnp.sum(value, axis=0, keepdims=True)
        stats_ref[0:1, columns] += total * leads
        stats_ref[2:3, columns] += total
        stats_ref[3:4, columns] += jnp.sum(value * value, axis=0, keepdims=True)

    @pl.when((step * tile < live) & (step * tile + tile > live))
    def _():
        value = jnp.where(frame < live, features_ref[target, :], 0.0).astype(jnp.float32)
        stats_ref[0:1, :] += jnp.sum(value, axis=0, keepdims=True)

    @pl.when(step == 0)
    def _():
        value = features_ref[0:LAG, :].astype(jnp.float32)
        stats_ref[1:2, :] = -jnp.sum(value, axis=0, keepdims=True)

    @pl.when(step == pl.num_programs(0) - 1)
    def _():
        count = live + jnp.minimum(live, LAG)
        total = stats_ref[2:3, :]
        squares = stats_ref[3:4, :]
        stats_ref[1:2, :] += total
        spread = squares - total * total / count.astype(jnp.float32)
        stats_ref[2:3, :] = jnp.maximum(spread, 0.0) + (SLACK * squares + FLOOR)


def contacts_call(coords, lengths, atom_pairs, rows):
    atoms = coords.shape[2]
    feats = atom_pairs.shape[1]
    return pl.pallas_call(
        contacts_kernel,
        grid=(rows // FRAME_TILE,),
        in_specs=[
            SCALARS,
            pl.BlockSpec((2, feats), lambda i: (0, 0)),
            pl.BlockSpec((3, FRAME_TILE, atoms), lambda i: (0, i, 0)),
        ],
        out_specs=[WHOLE, WHOLE],
        out_shape=[shape((rows, feats), jnp.bfloat16), shape((8, feats))],
        scratch_shapes=[pltpu.VMEM((atoms, feats), jnp.bfloat16)],
        compiler_params=params(),
        name="contacts",
    )(lengths, atom_pairs, coords)


def gram_half(features_ref, stats_ref, out_refs, right_ref, live, kept, lagged):
    part, half = out_refs[0].shape
    feats = 2 * half
    load_right(features_ref, right_ref, kept, lagged)
    columns = side_columns(half, kept)
    right = 1 if lagged else 0
    left_stats = jnp.transpose(stats_ref[...])
    right_mean = stats_ref[right : right + 1, columns] / live.astype(jnp.float32)
    right_inverse = lax.rsqrt(stats_ref[2:3, columns])
    for start in range(0, feats, FEATURE_TILE):
        rows = slice(start, start + FEATURE_TILE)
        gram = gram_rows(features_ref, right_ref, start, live)
        gram = gram - left_stats[rows, 0:1] * right_mean
        if not kept:
            scale = (lax.rsqrt(left_stats[rows, 2:3]) * LEVELS) * right_inverse
            gram = to_levels(gram * scale)
        first = start % part
        out_refs[start // part][first : first + FEATURE_TILE, :] = gram


def sent_lag_kernel(lengths_ref, features_ref, stats_ref, sent_ref, right_ref):
    live = lengths_ref[own_place()] - LAG
    gram_half(features_ref, stats_ref, [sent_ref], right_ref, live, False, True)


def kept_lag_kernel(lengths_ref, features_ref, stats_ref, _, kept_ref, right_ref):
    live = lengths_ref[own_place()] - LAG
    gram_half(features_ref, stats_ref, [kept_ref], right_ref, live, True, True)


def sent_zero_kernel(lengths_ref, features_ref, stats_ref, peer_ref, sent_ref, chip_ref, right_ref):
    live = lengths_ref[own_place()] - LAG
    feats = stats_ref.shape[1]
    chip_ref[0:2, :] = stats_ref[0:2, :]
    chip_ref[2:4, :] = peer_ref[0:2, :]
    chip_ref[4:8, :] = jnp.broadcast_to(stats_ref[2:3, :] + peer_ref[2:3, :], (4, feats))
    gram_half(features_ref, stats_ref, [sent_ref], right_ref, live, False, False)


def kept_zero_kernel(
    lengths_ref, features_ref, stats_ref, chip_ref, near_ref, _, kept_ref, pair_ref, right_ref
):
    live = lengths_ref[own_place()] - LAG
    feats = stats_ref.shape[1]
    pair_ref[0:4, :] = chip_ref[0:4, :]
    pair_ref[4:8, :] = near_ref[0:4, :]
    pair_ref[8:16, :] = jnp.broadcast_to(chip_ref[4:5, :] + near_ref[4:5, :], (8, feats))
    gram_half(features_ref, stats_ref, [kept_ref], right_ref, live, True, False)


def gram_call(body, operands, after, outs, depth, estimate):
    feats = operands[1].shape[1]
    return pl.pallas_call(
        body,
        in_specs=[SCALARS]
        + [WHOLE] * (len(operands) - 1)
        + [pl.BlockSpec(memory_space=pl.ANY)] * len(after),
        out_specs=[WHOLE] * len(outs),
        out_shape=outs,
        scratch_shapes=[pltpu.VMEM((depth, feats // 2), jnp.bfloat16)],
        compiler_params=params(),
        cost_estimate=pl.CostEstimate(flops=estimate, bytes_accessed=estimate // 1024, transcendentals=0),
        name=body.__name__.removesuffix("_kernel"),
    )(*operands, *after)


def near_kernel(kept_ref, stats_ref, peer_ref, *refs, block):
    came_refs, keep_ref, sent_ref = refs[:-2], refs[-2], refs[-1]
    near = lax.axis_index("dp") % 2
    part = came_refs[0].shape[0]
    feats, half = kept_ref.shape
    columns = side_columns(half, True)
    chip_spread = stats_ref[2:3, :] + peer_ref[2:3, :]
    left = jnp.concatenate([peer_ref[2:3, :], chip_spread] * 4, axis=0)
    left = jnp.transpose(left)
    came_right = jnp.sqrt(peer_ref[2:3, columns])
    sent_right = lax.rsqrt(stats_ref[2:3, columns] + peer_ref[2:3, columns])
    for start in range(0, feats, 2 * block):
        totals = []
        for rows in (slice(start, start + block), slice(start + block, start + 2 * block)):
            scale = (jnp.sqrt(left[rows, 0:1]) * (1.0 / LEVELS)) * came_right
            first = rows.start % part
            came = came_refs[rows.start // part][first : first + block, :]
            totals.append(kept_ref[rows, :] + from_levels(came) * scale)
        target = slice(start // 2, start // 2 + block)
        keep_ref[target, :] = jnp.where(near == 0, totals[0], totals[1])
        other = jnp.where(near == 0, totals[1], totals[0])
        even = left[start : start + block, 1:2]
        odd = left[start + block : start + 2 * block, 1:2]
        scale = (lax.rsqrt(jnp.where(near == 0, odd, even)) * LEVELS) * sent_right
        sent_ref[target, :] = to_levels(other * scale)


def near_call(kept, came, stats, peer, block, name):
    half = kept.shape[1]
    return pl.pallas_call(
        functools.partial(near_kernel, block=block),
        in_specs=[WHOLE] * (3 + len(came)),
        out_specs=[WHOLE, WHOLE],
        out_shape=[shape((half, half)), shape((half, half), jnp.int16)],
        compiler_params=params(),
        name=name,
    )(kept, stats, peer, *came)


def far_kernel(keep_ref, came_ref, chip_ref, near_ref, *refs, block):
    kept_ref, sent_refs = refs[0], refs[1:-2]
    total_ref, level_ref = refs[-2], refs[-1]
    place = lax.axis_index("dp")
    near, far = place % 2, place // 2
    half = came_ref.shape[0]
    feats = chip_ref.shape[1]
    columns = side_columns(half, True)
    pair = chip_ref[4:5, :] + near_ref[4:5, :]
    left = jnp.concatenate([near_ref[4:5, :], pair] * 4, axis=0)
    left = jnp.transpose(left)
    came_right = jnp.sqrt(near_ref[4:5, columns])
    sent_right = lax.rsqrt(chip_ref[4:5, columns] + near_ref[4:5, columns])
    for index in range(half // block):
        rows = slice(index * block, (index + 1) * block)
        even = left[2 * index * block : (2 * index + 1) * block]
        odd = left[(2 * index + 1) * block : (2 * index + 2) * block]
        mine = jnp.where(near == 0, even, odd)
        scale = (jnp.sqrt(mine[:, 0:1]) * (1.0 / LEVELS)) * came_right
        total = keep_ref[rows, :] + from_levels(came_ref[rows, :]) * scale
        total_ref[index] = total
        scale = (lax.rsqrt(mine[:, 1:2]) * LEVELS) * sent_right
        level_ref[index] = to_levels(total * scale)
    kept_ref[...] = total_ref[far]
    for step, sent_ref in enumerate(sent_refs):
        sent_ref[...] = level_ref[far ^ (step + 1)]


def far_call(keep, came, chip, near, block, name):
    half = came.shape[0]
    far = half // block
    return pl.pallas_call(
        functools.partial(far_kernel, block=block),
        in_specs=[WHOLE] * 4,
        out_specs=[WHOLE] * far,
        out_shape=[shape((block, half))] + [shape((block, half), jnp.int16)] * (far - 1),
        scratch_shapes=[
            pltpu.VMEM((far, block, half), jnp.float32),
            pltpu.VMEM((far, block, half), jnp.int16),
        ],
        compiler_params=params(),
        name=name,
    )(keep, came, chip, near)


def gathered_total(kept_ref, came_refs, left_ref, stats_refs, columns):
    total = kept_ref[...]
    for index, came_ref in enumerate(came_refs):
        spread = left_ref[:, 16 * index + 24 : 16 * index + 25]
        scale = jnp.sqrt(spread) * (1.0 / LEVELS)
        scale = scale * jnp.sqrt(stats_refs[index + 1][8:9, columns])
        total = total + from_levels(came_ref[...]) * scale
    return total


def pairs_of(lengths_ref, members):
    total = lax.fori_loop(0, members, lambda i, t: t + lengths_ref[i] - LAG, 0)
    return total.astype(jnp.float32)


def finish_lag_kernel(lengths_ref, left_ref, kept_ref, *refs):
    groups = len(refs) // 2
    stats_refs, came_refs, out_ref, zero_ref = refs[:groups], refs[groups:-2], refs[-2], refs[-1]
    columns = side_columns(kept_ref.shape[1], True)
    place = own_place()
    pair_total = pairs_of(lengths_ref, 4 * groups)
    members = [(group, member) for group in range(groups) for member in range(4)]
    lead_mean = lead_row = lag_row = 0.0
    for group, member in members:
        column = 16 * group + 2 * member
        lead_mean += left_ref[:, column : column + 1]
        lead_row += stats_refs[group][2 * member : 2 * member + 1, columns]
        lag_row += stats_refs[group][2 * member + 1 : 2 * member + 2, columns]
    lead_mean, lead_row, lag_row = (v / pair_total for v in (lead_mean, lead_row, lag_row))
    lag = gathered_total(kept_ref, came_refs, left_ref, stats_refs, columns)
    zero = jnp.zeros_like(lag)
    for group, member in members:
        weight = (lengths_ref[place ^ (4 * group + member)] - LAG).astype(jnp.float32)
        column = 16 * group + 2 * member
        lead = left_ref[:, column : column + 1] - lead_mean * weight
        leads = stats_refs[group][2 * member : 2 * member + 1, columns]
        lags = stats_refs[group][2 * member + 1 : 2 * member + 2, columns]
        zero = zero + lead * (leads / weight - lead_row)
        lag = lag + lead * (lags / weight - lag_row)
    out_ref[...] = lag / pair_total
    zero_ref[...] = zero


def finish_lag(lengths, left, stats, kept, came):
    return pl.pallas_call(
        finish_lag_kernel,
        in_specs=[SCALARS] + [WHOLE] * (2 + len(stats) + len(came)),
        out_specs=[WHOLE, WHOLE],
        out_shape=[shape(kept.shape), shape(kept.shape)],
        compiler_params=params(),
        name="finish_lag",
    )(lengths, left, kept, *stats, *came)


def finish_zero_kernel(lengths_ref, left_ref, between_ref, kept_ref, *refs):
    groups = len(refs) // 2
    stats_refs, came_refs, out_ref = refs[:groups], refs[groups:-1], refs[-1]
    columns = side_columns(kept_ref.shape[1], True)
    zero = gathered_total(kept_ref, came_refs, left_ref, stats_refs, columns)
    out_ref[...] = (zero + between_ref[...]) / pairs_of(lengths_ref, 4 * groups)


def finish_zero(lengths, left, stats, between, kept, came):
    return pl.pallas_call(
        finish_zero_kernel,
        in_specs=[SCALARS] + [WHOLE] * (3 + len(stats) + len(came)),
        out_specs=WHOLE,
        out_shape=shape(kept.shape),
        compiler_params=params(),
        name="finish_zero",
    )(lengths, left, between, kept, *stats, *came)


def exclusive(size, distance):
    return [(i, i ^ distance) for i in range(size)]


def local(coords, lengths, atom_pairs):
    feats = atom_pairs.shape[1]
    dp = lax.axis_size("dp")
    far = dp // 2
    block = feats // dp
    home = coords.shape[0]
    depth = round_up(home - LAG, DEPTH_UNIT)
    rows = round_up(max(home, depth + LAG), FRAME_TILE)

    def swap(array, axis, distance):
        return lax.ppermute(array, axis, exclusive(lax.axis_size(axis), distance))

    coords = pltpu.with_memory_space_constraint(jnp.transpose(coords, (1, 0, 2)), pltpu.HBM)
    features, stats = contacts_call(coords, lengths, atom_pairs, rows)
    common = [lengths, features, stats]
    half = feats // 2
    kept_shape, sent_shape = shape((feats, half)), shape((feats, half), jnp.int16)
    peer = swap(stats, "tile", 1)
    (sent_lag,) = gram_call(sent_lag_kernel, common, [], [sent_shape], depth, LONG)
    came_lag = swap(sent_lag, "tile", 1)
    sent_zero, chip = gram_call(
        sent_zero_kernel, common + [peer], [], [sent_shape, shape((8, feats))], depth, LONG
    )
    near = swap(chip, "dp", 1)
    came_zero = swap(sent_zero, "tile", 1)
    (kept_lag,) = gram_call(kept_lag_kernel, common, [sent_zero], [kept_shape], depth, LONG)
    keep_lag, sent_lag = near_call(kept_lag, [came_lag], stats, peer, block, "near_lag")
    came_lag = swap(sent_lag, "dp", 1)
    kept_zero, pair = gram_call(
        kept_zero_kernel,
        common + [chip, near],
        [sent_lag],
        [kept_shape, shape((16, feats))],
        depth,
        LONG,
    )
    keep_zero, sent_zero = near_call(kept_zero, [came_zero], stats, peer, block, "near_zero")
    came_zero = swap(sent_zero, "dp", 1)

    gathered = [pair] + [swap(pair, "dp", 2 * step) for step in range(1, far)]
    first = lax.axis_index("dp") * block
    left = [lax.dynamic_slice_in_dim(part, first, block, axis=1) for part in gathered]
    left = jnp.concatenate(left, axis=0).T

    kept_lag, *sent_lag = far_call(keep_lag, came_lag, chip, near, block, "far_lag")
    came_lag = [swap(s, "dp", 2 * (i + 1)) for i, s in enumerate(sent_lag)]
    kept_zero, *sent_zero = far_call(keep_zero, came_zero, chip, near, block, "far_zero")
    came_zero = [swap(s, "dp", 2 * (i + 1)) for i, s in enumerate(sent_zero)]
    cov_lag, between = finish_lag(lengths, left, gathered, kept_lag, came_lag)
    cov_zero = finish_zero(lengths, left, gathered, between, kept_zero, came_zero)
    return (cov_zero, cov_lag)


def solution(mesh):
    placed = (P(("groups", "dp", "tile"), None, None), P("groups"), P())
    return jax.shard_map(
        local,
        mesh=mesh,
        in_specs=placed,
        out_specs=(P(("groups", "dp"), "tile"), P(("groups", "dp"), "tile")),
        check_vma=False,
    )
```

time: 74.8 us -> 71.1 us (0.951)
  Pallas kernels: 36.5 us -> 34.6 us
  waiting for transfers between devices: 15.2 us -> 14 us
  local copies, waits for them, and re-layouts: 3.27 us -> 2.41 us
    pallas_call x1, Pallas kernels: 14.4 us -> 11.4 us  [contacts_call(): pl.pallas_call(contacts_kernel, grid=(rows // FRAME_TILE,), in_specs=[SCA...]
    ppermute x14 -> x15, waiting for transfers between devices: 15.2 us -> 14 us  [swap(): return lax.ppermute(array, axis, exclusive(lax.axis_size(axis), distance))]
    pallas_call x6 -> x8, Pallas kernels: 20.2 us -> 21.4 us  [the longest x4 13.2 us: gram_call(): pl.pallas_call(body, in_specs=[SCALARS] + [WHOLE] * (len(operands) - 1) +...]
    unnamed x15 -> x10, local copies, waits for them, and re-layouts: 3.24 us -> 2.3 us
    ppermute x14 -> x15, starting transfers between devices: 18.8 us -> 19.1 us  [swap(): return lax.ppermute(array, axis, exclusive(lax.axis_size(axis), distance))]
  transfers between devices with their start and end apart: 14 -> 15, of which waited for: 4 -> 3; matrix products, arithmetic and copies ran while one was open for 1% -> 0% of each run, Pallas kernels for 28% -> 31%
where the time goes in v3:
time: 71.1 us; the launch traced here: 70.9 us
  Pallas kernels  34.6 us (49%)
  starting transfers between devices  19.1 us (27%)
  waiting for transfers between devices  14 us (20%)
  local copies, waits for them, and re-layouts  2.41 us (3%)
  between operations  0.78 us (1%)
    ppermute x15, starting transfers between devices, swap(): return lax.ppermute(array, axis, exclusive(lax.axis_size(axis), distance))  19.1 us
    ppermute x15, waiting for transfers between devices, swap(): return lax.ppermute(array, axis, exclusive(lax.axis_size(axis), distance))  14 us
    pallas_call x4, Pallas kernels, gram_call(): pl.pallas_call(body, in_specs=[SCALARS] + [WHOLE] * (len(operands) - 1) +...  13.2 us
    pallas_call x1, Pallas kernels, contacts_call(): pl.pallas_call(contacts_kernel, grid=(rows // FRAME_TILE,), in_specs=[SCA...  11.4 us
    pallas_call x2, Pallas kernels, near_call(): pl.pallas_call(functools.partial(near_kernel, block=block), in_specs=[WHO...  3.35 us
    pallas_call x1, Pallas kernels, finish_lag(): pl.pallas_call(finish_lag_kernel, in_specs=[SCALARS] + [WHOLE] * (2 + len...  3.28 us
    unnamed x10, local copies, waits for them, and re-layouts  2.3 us
    pallas_call x2, Pallas kernels, far_call(): pl.pallas_call(functools.partial(far_kernel, block=block), in_specs=[WHOL...  1.84 us
  transfers between devices with their start and end apart: 15, of which 3 were waited for; matrix products, arithmetic and copies ran while one was open for 0% of the time, Pallas kernels for 31%

profile of v3, /device:TPU:0, one launch (start us, length us, event | category | flops | bytes accessed | tf_op | source)
XLA Modules:
  0.0 70.9 jit_solution(1476005298353418950)
XLA Ops:
  0.6 0.0 copy-start.2
  0.6 0.6 copy-done.2
  1.3 0.0 copy-start.4
  1.3 0.7 copy-done.4
  2.0 11.4 %contacts.1 = (bf16[2560,1024]{1,0:T(8,128)(2,1)S(1)}, f32[8,1024]{1,0:T(8,128)S(1)}) custom-call(s32[16]{0:T(128)S(1)} %copy-done.2, s32[2,1024]{1,0:T(2,128)S(1)} %copy-done.4, bf16[3,2516,256]{2,1,0:T(8,128)(2,1)} %bitcast.3), custom_call_target="tpu_custom_call" | custom-call | tf_op jit(solution)/shard_map/contacts/pallas_call | solution.py:131
  13.4 0.5 collective-permute-start
  13.9 3.5 %sent_lag.1 = s16[1024,512]{1,0:T(8,128)(2,1)S(1)} custom-call(s32[16]{0:T(128)S(1)} %copy-done.2, bf16[2560,1024]{1,0:T(8,128)(2,1)S(1)} %get-tuple-element.22.features_ref, f32[8,1024]{1,0:T(8,128)S(1)} %get-tuple-element.23.stats_ref), custom_call_target="tpu_custom_call" | custom-call | flops 2147483648 | bytes 2097152 | tf_op jit(solution)/shard_map/sent_lag/pallas_call | solution.py:199
  17.4 0.1 collective-permute-start.2
  17.5 0.0 collective-permute-done.peer_ref
  17.5 3.2 %sent_zero.1 = (s16[1024,512]{1,0:T(8,128)(2,1)S(1)}, f32[8,1024]{1,0:T(8,128)S(1)}) custom-call(s32[16]{0:T(128)S(1)} %copy-done.2, bf16[2560,1024]{1,0:T(8,128)(2,1)S(1)} %get-tuple-element.22.features_ref, f32[8,1024]{1,0:T(8,128)S(1)} %get-tuple-element.23.stats_ref, f32[8,1024]{1,0:T(8,128)S(1)} %collective-permute-done.peer_ref), custom_call_target="tpu_custom_call" | custom-call | flops 2147483648 | bytes 2097152 | tf_op jit(solution)/shard_map/sent_zero/pallas_call | solution.py:199
  20.7 0.5 collective-permute-start.10
  21.3 2.6 %collective-permute-start.1 = (f32[8,1024]{1,0:T(8,128)S(1)}, f32[8,1024]{1,0:T(8,128)S(1)}, u32[]{:S(2)}, u32[]{:S(2)}) collective-permute-start(f32[8,1024]{1,0:T(8,128)S(1)} %get-tuple-element.24.chip_ref), channel_id=1, source_target_pairs={{0,2},{2,0},{4,6},{6,4},{8,10},{10,8},{12,14},{14,12},{1,3},{3,1},... | collective-permute-start | bytes 98312 | tf_op jit(solution)/shard_map/ppermute | solution.py:384
  23.8 3.4 %kept_lag.1.kept_ref = f32[1024,512]{1,0:T(8,128)S(1)} custom-call(s32[16]{0:T(128)S(1)} %copy-done.2, bf16[2560,1024]{1,0:T(8,128)(2,1)S(1)} %get-tuple-element.22.features_ref, f32[8,1024]{1,0:T(8,128)S(1)} %get-tuple-element.23.stats_ref, s16[1024,512]{1,0:T(8,128)(2,1)S(1)} %get-tuple-element.25._), custom_call_target="tpu_custom_call" | custom-call | flops 2147483648 | bytes 2097152 | tf_op jit(solution)/shard_map/kept_lag/pallas_call | solution.py:199
  27.2 0.0 collective-permute-done.2.refs_0_
  27.2 1.7 %near_lag.1 = (f32[512,512]{1,0:T(8,128)S(1)}, s16[512,512]{1,0:T(8,128)(2,1)}) custom-call(f32[1024,512]{1,0:T(8,128)S(1)} %kept_lag.1.kept_ref, f32[8,1024]{1,0:T(8,128)S(1)} %get-tuple-element.23.stats_ref, f32[8,1024]{1,0:T(8,128)S(1)} %collective-permute-done.peer_ref, s16[1024,512]{1,0:T(8,128)(2,1)S(1)} %collective-permute-done.2.refs_0_), custom_call_target="tpu_custom_call" | custom-call | tf_op jit(solution)/shard_map/near_lag/pallas_call | solution.py:242
  28.9 0.0 collective-permute-start.6
  28.9 0.0 collective-permute-done.1.near_ref
  28.9 3.1 %kept_zero.1 = (f32[1024,512]{1,0:T(8,128)S(1)}, f32[16,1024]{1,0:T(8,128)S(1)}) custom-call(s32[16]{0:T(128)S(1)} %copy-done.2, bf16[2560,1024]{1,0:T(8,128)(2,1)S(1)} %get-tuple-element.22.features_ref, f32[8,1024]{1,0:T(8,128)S(1)} %get-tuple-element.23.stats_ref, f32[8,1024]{1,0:T(8,128)S(1)} %get-tuple-element.24.chip_ref, ...), custom_call_target="tpu_custom_call" | custom-call | flops 2147483648 | bytes 2097152 | tf_op jit(solution)/shard_map/kept_zero/pallas_call | solution.py:199
  32.1 0.0 copy-start.3
  32.1 0.0 collective-permute-done.10.refs_0_
  32.1 1.7 %near_zero.1 = (f32[512,512]{1,0:T(8,128)S(1)}, s16[512,512]{1,0:T(8,128)(2,1)}) custom-call(f32[1024,512]{1,0:T(8,128)S(1)} %get-tuple-element.34.kept_ref, f32[8,1024]{1,0:T(8,128)S(1)} %get-tuple-element.23.stats_ref, f32[8,1024]{1,0:T(8,128)S(1)} %collective-permute-done.peer_ref, s16[1024,512]{1,0:T(8,128)(2,1)S(1)} %collective-permute-done.10.refs_0_), custom_call_target="tpu_custom_call" | custom-call | tf_op jit(solution)/shard_map/near_zero/pallas_call | solution.py:242
  33.8 2.0 %collective-permute-start.11 = (s16[512,512]{1,0:T(8,128)(2,1)}, s16[512,512]{1,0:T(8,128)(2,1)S(1)}, u32[]{:S(2)}, u32[]{:S(2)}) collective-permute-start(s16[512,512]{1,0:T(8,128)(2,1)} %get-tuple-element.36), channel_id=1, source_target_pairs={{0,2},{2,0},{4,6},{6,4},{8,10},{10,8},{12,14},{14,12},{1,3},{3,1},... | collective-permute-start | bytes 1572872 | tf_op jit(solution)/shard_map/ppermute | solution.py:384
  35.8 2.6 %collective-permute-start.4 = (f32[16,1024]{1,0:T(8,128)S(1)}, f32[16,1024]{1,0:T(8,128)S(1)}, u32[]{:S(2)}, u32[]{:S(2)}) collective-permute-start(f32[16,1024]{1,0:T(8,128)S(1)} %get-tuple-element.27.refs_0_), channel_id=1, source_target_pairs={{0,8},{2,10},{4,12},{6,14},{8,0},{10,2},{12,4},{14,6},{1,9},{3,11}... | collective-permute-start | bytes 196616 | tf_op jit(solution)/shard_map/ppermute | solution.py:384
  38.4 1.6 %collective-permute-start.3 = (f32[16,1024]{1,0:T(8,128)S(1)}, f32[16,1024]{1,0:T(8,128)S(1)}, u32[]{:S(2)}, u32[]{:S(2)}) collective-permute-start(f32[16,1024]{1,0:T(8,128)S(1)} %get-tuple-element.27.refs_0_), channel_id=1, source_target_pairs={{0,4},{2,6},{4,0},{6,2},{8,12},{10,14},{12,8},{14,10},{1,5},{3,7},... | collective-permute-start | bytes 196616 | tf_op jit(solution)/shard_map/ppermute | solution.py:384
  40.0 0.2 collective-permute-start.5
  40.2 3.7 %collective-permute-done.6.came_ref = s16[512,512]{1,0:T(8,128)(2,1)S(1)} collective-permute-done((s16[512,512]{1,0:T(8,128)(2,1)}, s16[512,512]{1,0:T(8,128)(2,1)S(1)}, u32[]{:S(2)}, u32[]{:S(2)}) %collective-permute-start.6) | collective-permute-done | bytes 524320 | tf_op jit(solution)/shard_map/ppermute | solution.py:384
  43.9 1.3 %far_lag.1 = (f32[128,512]{1,0:T(8,128)S(1)}, s16[128,512]{1,0:T(8,128)(2,1)S(1)}, s16[128,512]{1,0:T(8,128)(2,1)}, s16[128,512]{1,0:T(8,128)(2,1)}) custom-call(f32[512,512]{1,0:T(8,128)S(1)} %get-tuple-element.28.keep_ref, s16[512,512]{1,0:T(8,128)(2,1)S(1)} %collective-permute-done.6.came_ref, f32[8,1024]{1,0:T(8,128)S(1)} %get-tuple-element.24.chip_ref, ...), custom_call_target="tpu_custom_call" | custom-call | tf_op jit(solution)/shard_map/far_lag/pallas_call | solution.py:283
  45.2 0.0 copy-start
  45.2 1.6 %collective-permute-start.7 = (s16[128,512]{1,0:T(8,128)(2,1)S(1)}, s16[128,512]{1,0:T(8,128)(2,1)S(1)}, u32[]{:S(2)}, u32[]{:S(2)}) collective-permute-start(s16[128,512]{1,0:T(8,128)(2,1)S(1)} %get-tuple-element.30), channel_id=1, source_target_pairs={{0,4},{2,6},{4,0},{6,2},{8,12},{10,14},{12,8},{14,10},{1,5},{3,7},... | collective-permute-start | bytes 393224 | tf_op jit(solution)/shard_map/ppermute | solution.py:384
  46.7 0.0 collective-permute-done.4.refs_2_
  46.8 0.0 collective-permute-done.3.refs_1_
  46.8 2.7 %collective-permute-start.8 = (s16[128,512]{1,0:T(8,128)(2,1)}, s16[128,512]{1,0:T(8,128)(2,1)S(1)}, u32[]{:S(2)}, u32[]{:S(2)}) collective-permute-start(s16[128,512]{1,0:T(8,128)(2,1)} %get-tuple-element.31), channel_id=1, source_target_pairs={{0,8},{2,10},{4,12},{6,14},{8,0},{10,2},{12,4},{14,6},{1,9},{3,11}... | collective-permute-start | bytes 393224 | tf_op jit(solution)/shard_map/ppermute | solution.py:384
  49.4 0.2 collective-permute-start.9
  49.7 4.7 %collective-permute-done.11.came_ref = s16[512,512]{1,0:T(8,128)(2,1)S(1)} collective-permute-done((s16[512,512]{1,0:T(8,128)(2,1)}, s16[512,512]{1,0:T(8,128)(2,1)S(1)}, u32[]{:S(2)}, u32[]{:S(2)}) %collective-permute-start.11) | collective-permute-done | bytes 524320 | tf_op jit(solution)/shard_map/ppermute | solution.py:384
  54.4 0.6 far_zero.1
  54.9 1.6 %collective-permute-start.12 = (s16[128,512]{1,0:T(8,128)(2,1)S(1)}, s16[128,512]{1,0:T(8,128)(2,1)S(1)}, u32[]{:S(2)}, u32[]{:S(2)}) collective-permute-start(s16[128,512]{1,0:T(8,128)(2,1)S(1)} %get-tuple-element.38), channel_id=1, source_target_pairs={{0,4},{2,6},{4,0},{6,2},{8,12},{10,14},{12,8},{14,10},{1,5},{3,7},... | collective-permute-start | bytes 393224 | tf_op jit(solution)/shard_map/ppermute | solution.py:384
  56.6 0.0 collective-permute-done.5.refs_3_
  56.6 2.6 %collective-permute-start.13 = (s16[128,512]{1,0:T(8,128)(2,1)S(1)}, s16[128,512]{1,0:T(8,128)(2,1)S(1)}, u32[]{:S(2)}, u32[]{:S(2)}) collective-permute-start(s16[128,512]{1,0:T(8,128)(2,1)S(1)} %get-tuple-element.39), channel_id=1, source_target_pairs={{0,8},{2,10},{4,12},{6,14},{8,0},{10,2},{12,4},{14,6},{1,9},{3,11}... | collective-permute-start | bytes 393224 | tf_op jit(solution)/shard_map/ppermute | solution.py:384
  59.2 0.0 collective-permute-done.7.refs_4_
  59.2 0.2 collective-permute-start.14
  59.4 0.0 copy-done
  59.4 0.1 copy.6.left_ref
  59.5 0.0 collective-permute-done.8.refs_5_
  59.5 0.0 collective-permute-done.9.refs_6_
  59.5 0.0 copy-done.3
  59.5 0.0 copy-start.1
  59.5 0.9 %copy-done.1 = f32[128,512]{1,0:T(8,128)S(1)} copy-done((f32[128,512]{1,0:T(8,128)S(1)}, f32[128,512]{1,0:T(8,128)}, u32[]{:S(2)}) %copy-start.1) | copy-done | bytes 262168
  60.5 3.3 %finish_lag.1 = (f32[128,512]{1,0:T(8,128)}, f32[128,512]{1,0:T(8,128)S(1)}) custom-call(s32[16]{0:T(128)S(1)} %copy-done.3, f32[128,64]{1,0:T(8,128)S(1)} %copy.6.left_ref, f32[128,512]{1,0:T(8,128)S(1)} %copy-done.1, f32[16,1024]{1,0:T(8,128)S(1)} %get-tuple-element.27.refs_0_, f32[16,1024]{1,0:T(8,128)S(1)} %collective-permute-done.3.refs_1_, ...), custom_call_target="tpu_custom_call" | custom-call | tf_op jit(solution)/shard_map/finish_lag/pallas_call | solution.py:341
  63.8 0.0 collective-permute-done.12.refs_4_
  63.8 5.6 %collective-permute-done.13.refs_5_ = s16[128,512]{1,0:T(8,128)(2,1)S(1)} collective-permute-done((s16[128,512]{1,0:T(8,128)(2,1)S(1)}, s16[128,512]{1,0:T(8,128)(2,1)S(1)}, u32[]{:S(2)}, u32[]{:S(2)}) %collective-permute-start.13) | collective-permute-done | bytes 131104 | tf_op jit(solution)/shard_map/ppermute | solution.py:384
  69.3 0.0 collective-permute-done.14.refs_6_
  69.3 1.5 %finish_zero.1 = f32[128,512]{1,0:T(8,128)} custom-call(s32[16]{0:T(128)S(1)} %copy-done.3, f32[128,64]{1,0:T(8,128)S(1)} %copy.6.left_ref, f32[128,512]{1,0:T(8,128)S(1)} %get-tuple-element.33.between_ref, f32[128,512]{1,0:T(8,128)S(1)} %get-tuple-element.37.kept_ref, f32[16,1024]{1,0:T(8,128)S(1)} %get-tuple-element.27.refs_0_, ...), custom_call_target="tpu_custom_call" | custom-call | tf_op jit(solution)/shard_map/finish_zero/pallas_call | solution.py:360
  (5 shorter events, 0.0 us)
Async XLA Ops:
  0.6 0.7 copy-start.2
  1.3 0.7 copy-start.4
  13.4 4.1 %collective-permute-start = (f32[8,1024]{1,0:T(8,128)S(1)}, f32[8,1024]{1,0:T(8,128)S(1)}, u32[]{:S(2)}, u32[]{:S(2)}) collective-permute-start(f32[8,1024]{1,0:T(8,128)S(1)} %get-tuple-element.23.stats_ref), channel_id=1, source_target_pairs={{0,1},{1,0},{2,3},{3,2},{4,5},{5,4},{6,7},{7,6},{8,9},{9,8},{10,11... | collective-permute-start | bytes 98312 | tf_op jit(solution)/shard_map/ppermute | solution.py:384
  17.4 9.9 %collective-permute-start.2 = (s16[1024,512]{1,0:T(8,128)(2,1)S(1)}, s16[1024,512]{1,0:T(8,128)(2,1)S(1)}, u32[]{:S(2)}, u32[]{:S(2)}) collective-permute-start(s16[1024,512]{1,0:T(8,128)(2,1)S(1)} %sent_lag.1), channel_id=1, source_target_pairs={{0,1},{1,0},{2,3},{3,2},{4,5},{5,4},{6,7},{7,6},{8,9},{9,8},{10,11... | collective-permute-start | bytes 3145736 | tf_op jit(solution)/shard_map/ppermute | solution.py:384
  20.7 11.4 %collective-permute-start.10 = (s16[1024,512]{1,0:T(8,128)(2,1)S(1)}, s16[1024,512]{1,0:T(8,128)(2,1)S(1)}, u32[]{:S(2)}, u32[]{:S(2)}) collective-permute-start(s16[1024,512]{1,0:T(8,128)(2,1)S(1)} %get-tuple-element.25._), channel_id=1, source_target_pairs={{0,1},{1,0},{2,3},{3,2},{4,5},{5,4},{6,7},{7,6},{8,9},{9,8},{10,11... | collective-permute-start | bytes 3145736 | tf_op jit(solution)/shard_map/ppermute | solution.py:384
  21.3 7.7 %collective-permute-start.1 = (f32[8,1024]{1,0:T(8,128)S(1)}, f32[8,1024]{1,0:T(8,128)S(1)}, u32[]{:S(2)}, u32[]{:S(2)}) collective-permute-start(f32[8,1024]{1,0:T(8,128)S(1)} %get-tuple-element.24.chip_ref), channel_id=1, source_target_pairs={{0,2},{2,0},{4,6},{6,4},{8,10},{10,8},{12,14},{14,12},{1,3},{3,1},... | collective-permute-start | bytes 98312 | tf_op jit(solution)/shard_map/ppermute | solution.py:384
  28.9 15.0 %collective-permute-start.6 = (s16[512,512]{1,0:T(8,128)(2,1)}, s16[512,512]{1,0:T(8,128)(2,1)S(1)}, u32[]{:S(2)}, u32[]{:S(2)}) collective-permute-start(s16[512,512]{1,0:T(8,128)(2,1)} %get-tuple-element.26._), channel_id=1, source_target_pairs={{0,2},{2,0},{4,6},{6,4},{8,10},{10,8},{12,14},{14,12},{1,3},{3,1},... | collective-permute-start | bytes 1572872 | tf_op jit(solution)/shard_map/ppermute | solution.py:384
  32.1 27.4 %copy-start.3 = (s32[16]{0:T(128)S(1)}, s32[16]{0:T(128)}, u32[]{:S(2)}) copy-start(s32[16]{0:T(128)} %lengths_ref.13) | copy-start | bytes 196
  33.8 20.6 %collective-permute-start.11 = (s16[512,512]{1,0:T(8,128)(2,1)}, s16[512,512]{1,0:T(8,128)(2,1)S(1)}, u32[]{:S(2)}, u32[]{:S(2)}) collective-permute-start(s16[512,512]{1,0:T(8,128)(2,1)} %get-tuple-element.36), channel_id=1, source_target_pairs={{0,2},{2,0},{4,6},{6,4},{8,10},{10,8},{12,14},{14,12},{1,3},{3,1},... | collective-permute-start | bytes 1572872 | tf_op jit(solution)/shard_map/ppermute | solution.py:384
  35.8 11.0 %collective-permute-start.4 = (f32[16,1024]{1,0:T(8,128)S(1)}, f32[16,1024]{1,0:T(8,128)S(1)}, u32[]{:S(2)}, u32[]{:S(2)}) collective-permute-start(f32[16,1024]{1,0:T(8,128)S(1)} %get-tuple-element.27.refs_0_), channel_id=1, source_target_pairs={{0,8},{2,10},{4,12},{6,14},{8,0},{10,2},{12,4},{14,6},{1,9},{3,11}... | collective-permute-start | bytes 196616 | tf_op jit(solution)/shard_map/ppermute | solution.py:384
  38.4 8.4 %collective-permute-start.3 = (f32[16,1024]{1,0:T(8,128)S(1)}, f32[16,1024]{1,0:T(8,128)S(1)}, u32[]{:S(2)}, u32[]{:S(2)}) collective-permute-start(f32[16,1024]{1,0:T(8,128)S(1)} %get-tuple-element.27.refs_0_), channel_id=1, source_target_pairs={{0,4},{2,6},{4,0},{6,2},{8,12},{10,14},{12,8},{14,10},{1,5},{3,7},... | collective-permute-start | bytes 196616 | tf_op jit(solution)/shard_map/ppermute | solution.py:384
  40.0 16.6 %collective-permute-start.5 = (f32[16,1024]{1,0:T(8,128)S(1)}, f32[16,1024]{1,0:T(8,128)S(1)}, u32[]{:S(2)}, u32[]{:S(2)}) collective-permute-start(f32[16,1024]{1,0:T(8,128)S(1)} %get-tuple-element.27.refs_0_), channel_id=1, source_target_pairs={{0,12},{2,14},{4,8},{6,10},{8,4},{10,6},{12,0},{14,2},{1,13},{3,15... | collective-permute-start | bytes 196616 | tf_op jit(solution)/shard_map/ppermute | solution.py:384
  45.2 14.2 %copy-start = (f32[128,512]{1,0:T(8,128)}, f32[128,512]{1,0:T(8,128)S(1)}, u32[]{:S(2)}) copy-start(f32[128,512]{1,0:T(8,128)S(1)} %get-tuple-element.29.kept_ref) | copy-start | bytes 786436
  45.2 14.0 %collective-permute-start.7 = (s16[128,512]{1,0:T(8,128)(2,1)S(1)}, s16[128,512]{1,0:T(8,128)(2,1)S(1)}, u32[]{:S(2)}, u32[]{:S(2)}) collective-permute-start(s16[128,512]{1,0:T(8,128)(2,1)S(1)} %get-tuple-element.30), channel_id=1, source_target_pairs={{0,4},{2,6},{4,0},{6,2},{8,12},{10,14},{12,8},{14,10},{1,5},{3,7},... | collective-permute-start | bytes 393224 | tf_op jit(solution)/shard_map/ppermute | solution.py:384
  46.8 12.7 %collective-permute-start.8 = (s16[128,512]{1,0:T(8,128)(2,1)}, s16[128,512]{1,0:T(8,128)(2,1)S(1)}, u32[]{:S(2)}, u32[]{:S(2)}) collective-permute-start(s16[128,512]{1,0:T(8,128)(2,1)} %get-tuple-element.31), channel_id=1, source_target_pairs={{0,8},{2,10},{4,12},{6,14},{8,0},{10,2},{12,4},{14,6},{1,9},{3,11}... | collective-permute-start | bytes 393224 | tf_op jit(solution)/shard_map/ppermute | solution.py:384
  49.4 10.1 %collective-permute-start.9 = (s16[128,512]{1,0:T(8,128)(2,1)}, s16[128,512]{1,0:T(8,128)(2,1)S(1)}, u32[]{:S(2)}, u32[]{:S(2)}) collective-permute-start(s16[128,512]{1,0:T(8,128)(2,1)} %get-tuple-element.32), channel_id=1, source_target_pairs={{0,12},{2,14},{4,8},{6,10},{8,4},{10,6},{12,0},{14,2},{1,13},{3,15... | collective-permute-start | bytes 393224 | tf_op jit(solution)/shard_map/ppermute | solution.py:384
  54.9 8.8 %collective-permute-start.12 = (s16[128,512]{1,0:T(8,128)(2,1)S(1)}, s16[128,512]{1,0:T(8,128)(2,1)S(1)}, u32[]{:S(2)}, u32[]{:S(2)}) collective-permute-start(s16[128,512]{1,0:T(8,128)(2,1)S(1)} %get-tuple-element.38), channel_id=1, source_target_pairs={{0,4},{2,6},{4,0},{6,2},{8,12},{10,14},{12,8},{14,10},{1,5},{3,7},... | collective-permute-start | bytes 393224 | tf_op jit(solution)/shard_map/ppermute | solution.py:384
  56.6 12.7 %collective-permute-start.13 = (s16[128,512]{1,0:T(8,128)(2,1)S(1)}, s16[128,512]{1,0:T(8,128)(2,1)S(1)}, u32[]{:S(2)}, u32[]{:S(2)}) collective-permute-start(s16[128,512]{1,0:T(8,128)(2,1)S(1)} %get-tuple-element.39), channel_id=1, source_target_pairs={{0,8},{2,10},{4,12},{6,14},{8,0},{10,2},{12,4},{14,6},{1,9},{3,11}... | collective-permute-start | bytes 393224 | tf_op jit(solution)/shard_map/ppermute | solution.py:384
  59.2 10.2 %collective-permute-start.14 = (s16[128,512]{1,0:T(8,128)(2,1)S(1)}, s16[128,512]{1,0:T(8,128)(2,1)S(1)}, u32[]{:S(2)}, u32[]{:S(2)}) collective-permute-start(s16[128,512]{1,0:T(8,128)(2,1)S(1)} %get-tuple-element.40), channel_id=1, source_target_pairs={{0,12},{2,14},{4,8},{6,10},{8,4},{10,6},{12,0},{14,2},{1,13},{3,15... | collective-permute-start | bytes 393224 | tf_op jit(solution)/shard_map/ppermute | solution.py:384
  59.5 1.0 %copy-start.1 = (f32[128,512]{1,0:T(8,128)S(1)}, f32[128,512]{1,0:T(8,128)}, u32[]{:S(2)}) copy-start(f32[128,512]{1,0:T(8,128)} %copy-done) | copy-start | bytes 786436

commit v4 on v3

v4 whole, which is shorter than its diff:
```python
import functools

import jax
import jax.numpy as jnp
from jax import lax
from jax.experimental import pallas as pl
from jax.experimental.pallas import tpu as pltpu
from jax.sharding import PartitionSpec as P

LAG = 500
FRAME_TILE = 512
FEATURE_TILE = 256
DEPTH_UNIT = 256
SLOPE = 6.0 * 1.4426950408889634
LEVELS = 32752.0
SLACK = 2e-5
FLOOR = 1e-36
PART = 32000.0
INVERSE_LOG_TWO = 1.4426950408889634
TAIL = 16
LONG = 1 << 34
SHORT = 1 << 20
SPLIT = 4
VMEM = 12 * 1024 * 1024
WHOLE = pl.BlockSpec(memory_space=pltpu.VMEM)
SCALARS = pl.BlockSpec(memory_space=pltpu.SMEM)


def round_up(value, unit):
    return -(-value // unit) * unit


def own_place():
    return lax.axis_index("dp") * lax.axis_size("tile") + lax.axis_index("tile")


def params():
    return pltpu.CompilerParams(vmem_limit_bytes=VMEM)


def shape(dims, dtype=jnp.float32):
    return jax.ShapeDtypeStruct(dims, dtype)


def to_levels(ratio):
    root = lax.rsqrt(jnp.maximum(jnp.abs(ratio), 1e-30)) * LEVELS
    return jnp.round(ratio * root).astype(jnp.int32).astype(jnp.int16)


def parts_of(block):
    return block.astype(jnp.int32).astype(jnp.float32)


def from_levels(block):
    level = parts_of(block)
    return level * jnp.abs(level)


def encode(vectors):
    half = vectors[0].shape[1] // 2
    rows, exponents = [], []
    for vector in vectors:
        top = jnp.maximum(jnp.max(vector, axis=1, keepdims=True), 1e-37)
        exponent = jnp.ceil(jnp.log(top) * INVERSE_LOG_TWO) + 1.0
        units = vector * (jnp.exp2(-exponent) * PART)
        high = jnp.floor(units)
        low = jnp.floor((units - high) * PART)
        rows += [high[:, :half], high[:, half:], low[:, :half], low[:, half:]]
        exponents.append(jnp.broadcast_to(exponent, (1, half)))
    rows = rows + exponents + exponents[:1]
    return jnp.concatenate(rows, axis=0).astype(jnp.int32).astype(jnp.int16)


def decode(block):
    parts = parts_of(block)
    vectors = []
    for index in range(3):
        first = 4 * index
        high = jnp.concatenate([parts[first : first + 1], parts[first + 1 : first + 2]], axis=1)
        low = jnp.concatenate([parts[first + 2 : first + 3], parts[first + 3 : first + 4]], axis=1)
        scale = jnp.exp2(parts[12 + index : 13 + index, 0:1]) * (1.0 / PART)
        vectors.append((high + low * (1.0 / PART)) * scale)
    return vectors


def live_of(lengths_ref, distances):
    place = own_place()
    total = 0
    for distance in distances:
        total = total + lengths_ref[place ^ distance] - LAG
    return total.astype(jnp.float32)


def pool(info_ref, sums, spread, count, other_block, other_count):
    lead, lag, deviation = decode(other_block)
    weight = count * other_count / (count + other_count)
    lead_step = sums[0] / count - lead / other_count
    lag_step = sums[1] / count - lag / other_count
    spread = spread + deviation * deviation + weight * (lead_step * lead_step + lag_step * lag_step)
    rows = [deviation, lead_step, lag_step, spread, sums[0] + lead, sums[1] + lag]
    info_ref[...] = jnp.concatenate(rows + rows[:2], axis=0)


def pooled_code(info_ref):
    return encode([info_ref[4:5, :], info_ref[5:6, :], jnp.sqrt(info_ref[3:4, :])])


def side_columns(half, own):
    side = lax.axis_index("tile")
    return pl.ds(pl.multiple_of((side if own else 1 - side) * half, half), half)


def load_right(features_ref, right_ref, own, lagged):
    depth, half = right_ref.shape
    first = LAG if lagged else 0
    right_ref[...] = features_ref[first : first + depth, side_columns(half, own)]


def gram_rows(features_ref, right_ref, start, live):
    depth = right_ref.shape[0]
    alive = lax.broadcasted_iota(jnp.int32, (depth, 1), 0) < live
    left = jnp.where(alive, features_ref[0:depth, start : start + FEATURE_TILE], 0.0)
    return lax.dot_general(
        left.astype(jnp.bfloat16),
        right_ref[...],
        (((0,), (0,)), ((), ())),
        preferred_element_type=jnp.float32,
    )


def contacts_kernel(
    lengths_ref, pairs_ref, coords_ref, features_ref, stats_ref, sent_ref, table_ref, right_ref
):
    step = pl.program_id(0)
    atoms, feats = table_ref.shape
    tile = coords_ref.shape[1]

    @pl.when(step == 0)
    def _():
        atom_ids = lax.broadcasted_iota(jnp.int32, (atoms, feats), 0)
        first_hit = (atom_ids == pairs_ref[0:1, :]).astype(jnp.float32)
        second_hit = (atom_ids == pairs_ref[1:2, :]).astype(jnp.float32)
        table_ref[...] = (first_hit - second_hit).astype(jnp.bfloat16)
        stats_ref[...] = jnp.zeros_like(stats_ref)

    live = lengths_ref[own_place()] - LAG
    frame = step * tile + lax.broadcasted_iota(jnp.int32, (tile, 1), 0)
    used = (frame < live) | ((frame >= LAG) & (frame < live + LAG))
    leads = (step * tile + tile <= live).astype(jnp.float32)
    target = pl.ds(pl.multiple_of(step * tile, tile), tile)
    for start in range(0, feats, FEATURE_TILE):
        columns = slice(start, start + FEATURE_TILE)
        weights = table_ref[:, columns]
        squared = None
        for axis in range(3):
            separation = jnp.dot(coords_ref[axis], weights, preferred_element_type=jnp.float32)
            square = separation * separation
            squared = square if squared is None else squared + square
        squared = jnp.maximum(squared, 1e-30)
        distance = squared * lax.rsqrt(squared)
        value = pl.reciprocal(1.0 + jnp.exp2(distance * SLOPE - SLOPE), approx=True)
        value = jnp.where(used, value, 0.0).astype(jnp.bfloat16)
        features_ref[target, columns] = value
        value = value.astype(jnp.float32)
        total = jnp.sum(value, axis=0, keepdims=True)
        stats_ref[0:1, columns] += total * leads
        stats_ref[2:3, columns] += total
        stats_ref[3:4, columns] += jnp.sum(value * value, axis=0, keepdims=True)

    @pl.when((step * tile < live) & (step * tile + tile > live))
    def _():
        value = jnp.where(frame < live, features_ref[target, :], 0.0).astype(jnp.float32)
        stats_ref[0:1, :] += jnp.sum(value, axis=0, keepdims=True)

    @pl.when(step == 0)
    def _():
        value = features_ref[0:LAG, :].astype(jnp.float32)
        stats_ref[1:2, :] = -jnp.sum(value, axis=0, keepdims=True)

    @pl.when(step == pl.num_programs(0) - 1)
    def _():
        count = live + jnp.minimum(live, LAG)
        total = stats_ref[2:3, :]
        squares = stats_ref[3:4, :]
        stats_ref[1:2, :] += total
        spread = squares - total * total / count.astype(jnp.float32)
        stats_ref[2:3, :] = jnp.maximum(spread, 0.0) + (SLACK * squares + FLOOR)
        gram_half(features_ref, stats_ref, [sent_ref], right_ref, live, False, True)
        sent_ref[feats : feats + TAIL, :] = encode(
            [stats_ref[0:1, :], stats_ref[1:2, :], jnp.sqrt(stats_ref[2:3, :])]
        )


def contacts_call(coords, lengths, atom_pairs, rows, depth):
    atoms = coords.shape[2]
    feats = atom_pairs.shape[1]
    return pl.pallas_call(
        contacts_kernel,
        grid=(rows // FRAME_TILE,),
        in_specs=[
            SCALARS,
            pl.BlockSpec((2, feats), lambda i: (0, 0)),
            pl.BlockSpec((3, FRAME_TILE, atoms), lambda i: (0, i, 0)),
        ],
        out_specs=[WHOLE, WHOLE, WHOLE],
        out_shape=[
            shape((rows, feats), jnp.bfloat16),
            shape((8, feats)),
            shape((feats + TAIL, feats // 2), jnp.int16),
        ],
        scratch_shapes=[
            pltpu.VMEM((atoms, feats), jnp.bfloat16),
            pltpu.VMEM((depth, feats // 2), jnp.bfloat16),
        ],
        compiler_params=params(),
        name="contacts_sent_lag",
    )(lengths, atom_pairs, coords)


def gram_half(features_ref, stats_ref, out_refs, right_ref, live, kept, lagged):
    half = out_refs[0].shape[1]
    feats = 2 * half
    part = feats // len(out_refs)
    load_right(features_ref, right_ref, kept, lagged)
    columns = side_columns(half, kept)
    right = 1 if lagged else 0
    left_stats = jnp.transpose(stats_ref[...])
    right_mean = stats_ref[right : right + 1, columns] / live.astype(jnp.float32)
    right_inverse = lax.rsqrt(stats_ref[2:3, columns])
    for start in range(0, feats, FEATURE_TILE):
        rows = slice(start, start + FEATURE_TILE)
        gram = gram_rows(features_ref, right_ref, start, live)
        gram = gram - left_stats[rows, 0:1] * right_mean
        if not kept:
            scale = lax.rsqrt(left_stats[rows, 2:3]) * right_inverse
            gram = to_levels(gram * scale)
        first = start % part
        out_refs[start // part][first : first + FEATURE_TILE, :] = gram


def kept_lag_kernel(lengths_ref, features_ref, stats_ref, _, kept_ref, right_ref):
    live = lengths_ref[own_place()] - LAG
    gram_half(features_ref, stats_ref, [kept_ref], right_ref, live, True, True)


def zero_kernel(lengths_ref, features_ref, stats_ref, _, *refs):
    sent_refs, kept_ref, right_ref = refs[:-2], refs[-2], refs[-1]
    live = lengths_ref[own_place()] - LAG
    gram_half(features_ref, stats_ref, sent_refs, right_ref, live, False, False)
    gram_half(features_ref, stats_ref, [kept_ref], right_ref, live, True, False)


def gram_call(body, operands, after, outs, depth, estimate):
    feats = operands[1].shape[1]
    return pl.pallas_call(
        body,
        in_specs=[SCALARS]
        + [WHOLE] * (len(operands) - 1)
        + [pl.BlockSpec(memory_space=pl.ANY)] * len(after),
        out_specs=[WHOLE] * len(outs),
        out_shape=outs,
        scratch_shapes=[pltpu.VMEM((depth, feats // 2), jnp.bfloat16)],
        compiler_params=params(),
        cost_estimate=pl.CostEstimate(flops=estimate, bytes_accessed=estimate // 1024, transcendentals=0),
        name=body.__name__.removesuffix("_kernel"),
    )(*operands, *after)


def near_kernel(lengths_ref, kept_ref, info_ref, *refs, lagged, block, parts):
    came_refs, keep_ref, sent_ref = refs[:parts], refs[parts], refs[parts + 1]
    near = lax.axis_index("dp") % 2
    feats, half = kept_ref.shape
    part = feats // parts
    columns = side_columns(half, True)
    count, peer_count = live_of(lengths_ref, [0]), live_of(lengths_ref, [1])
    if lagged:
        stats_ref, info_ref = info_ref, refs[-1]
        sums = (stats_ref[0:1, :], stats_ref[1:2, :])
        tail = came_refs[0][feats : feats + TAIL, :]
        pool(info_ref, sums, stats_ref[2:3, :], count, tail, peer_count)
        sent_ref[half : half + TAIL, :] = pooled_code(info_ref)
    weight = count * peer_count / (count + peer_count)
    left = jnp.transpose(info_ref[...])
    came_right = info_ref[0:1, columns] * (1.0 / LEVELS**2)
    step_right = info_ref[2 if lagged else 1 : 3 if lagged else 2, columns] * weight
    sent_right = lax.rsqrt(info_ref[3:4, columns])
    for start in range(0, feats, 2 * block):
        totals = []
        for rows in (slice(start, start + block), slice(start + block, start + 2 * block)):
            first = rows.start % part
            came = from_levels(came_refs[rows.start // part][first : first + block, :])
            total = kept_ref[rows, :] + came * (left[rows, 0:1] * came_right)
            totals.append(total + left[rows, 1:2] * step_right)
        target = slice(start // 2, start // 2 + block)
        keep_ref[target, :] = jnp.where(near == 0, totals[0], totals[1])
        other = jnp.where(near == 0, totals[1], totals[0])
        even = left[start : start + block, 3:4]
        odd = left[start + block : start + 2 * block, 3:4]
        spread = jnp.where(near == 0, odd, even)
        sent_ref[target, :] = to_levels(other * (lax.rsqrt(spread) * sent_right))


def near_call(lengths, kept, info, came, block, lagged):
    feats, half = kept.shape
    outs = [shape((half, half)), shape((half + (TAIL if lagged else 0), half), jnp.int16)]
    if lagged:
        outs.append(shape((8, feats)))
    return pl.pallas_call(
        functools.partial(near_kernel, lagged=lagged, block=block, parts=len(came)),
        in_specs=[SCALARS] + [WHOLE] * (2 + len(came)),
        out_specs=[WHOLE] * len(outs),
        out_shape=outs,
        compiler_params=params(),
        name="near_lag" if lagged else "near_zero",
    )(lengths, kept, info, *came)


def far_kernel(lengths_ref, keep_ref, came_ref, info_ref, *refs, lagged, block, far):
    kept_ref, sent_refs = refs[0], refs[1:far]
    total_ref, level_ref = refs[-2], refs[-1]
    place = lax.axis_index("dp")
    near, own_far = place % 2, place // 2
    half = keep_ref.shape[0]
    columns = side_columns(half, True)
    count, near_count = live_of(lengths_ref, [0, 1]), live_of(lengths_ref, [2, 3])
    if lagged:
        chip_ref, info_ref = info_ref, refs[far]
        sums = (chip_ref[4:5, :], chip_ref[5:6, :])
        pool(info_ref, sums, chip_ref[3:4, :], count, came_ref[half : half + TAIL, :], near_count)
        code = pooled_code(info_ref)
        for sent_ref in sent_refs:
            sent_ref[block : block + TAIL, :] = code
    weight = count * near_count / (count + near_count)
    left = jnp.transpose(info_ref[...])
    came_right = info_ref[0:1, columns] * (1.0 / LEVELS**2)
    step_right = info_ref[2 if lagged else 1 : 3 if lagged else 2, columns] * weight
    sent_right = lax.rsqrt(info_ref[3:4, columns])
    for index in range(far):
        rows = slice(index * block, (index + 1) * block)
        even = left[2 * index * block : (2 * index + 1) * block]
        odd = left[(2 * index + 1) * block : (2 * index + 2) * block]
        mine = jnp.where(near == 0, even, odd)
        total = keep_ref[rows, :] + from_levels(came_ref[rows, :]) * (mine[:, 0:1] * came_right)
        total = total + mine[:, 1:2] * step_right
        total_ref[index] = total
        level_ref[index] = to_levels(total * (lax.rsqrt(mine[:, 3:4]) * sent_right))
    kept_ref[...] = total_ref[own_far]
    for step, sent_ref in enumerate(sent_refs):
        sent_ref[0:block, :] = level_ref[own_far ^ (step + 1)]


def far_call(lengths, keep, came, info, block, lagged):
    half = keep.shape[0]
    far = half // block
    outs = [shape((block, half))]
    outs += [shape((block + (TAIL if lagged else 0), half), jnp.int16)] * (far - 1)
    if lagged:
        outs.append(shape(info.shape))
    estimate = LONG if lagged else SHORT
    return pl.pallas_call(
        functools.partial(far_kernel, lagged=lagged, block=block, far=far),
        in_specs=[SCALARS] + [WHOLE] * 3,
        out_specs=[WHOLE] * len(outs),
        out_shape=outs,
        scratch_shapes=[
            pltpu.VMEM((far, block, half), jnp.float32),
            pltpu.VMEM((far, block, half), jnp.int16),
        ],
        compiler_params=params(),
        cost_estimate=pl.CostEstimate(flops=estimate, bytes_accessed=estimate // 1024, transcendentals=0),
        name="far_lag" if lagged else "far_zero",
    )(lengths, keep, came, info)


def gathered_total(kept_ref, came_refs, rows_ref, left_ref, columns):
    block, far = kept_ref.shape[0], len(came_refs) + 1
    total = kept_ref[...]
    for index, came_ref in enumerate(came_refs):
        row = 2 * far + index
        right = rows_ref[row : row + 1, columns] * (1.0 / LEVELS**2)
        total = total + from_levels(came_ref[0:block, :]) * (left_ref[:, row : row + 1] * right)
    return total


def pairs_of(lengths_ref, members):
    total = lax.fori_loop(0, members, lambda i, t: t + lengths_ref[i] - LAG, 0)
    return total.astype(jnp.float32)


def finish_lag_kernel(lengths_ref, info_ref, kept_ref, *refs, far):
    came_refs = refs[: far - 1]
    out_ref, zero_ref, rows_ref, left_ref, turned_ref = refs[far - 1 :]
    block, half = kept_ref.shape
    columns = side_columns(half, True)
    found = [decode(came_ref[block : block + TAIL, :]) for came_ref in came_refs]
    rows = [info_ref[4:5, :]] + [f[0] for f in found] + [info_ref[5:6, :]] + [f[1] for f in found]
    rows += [f[2] for f in found]
    rows += [jnp.zeros_like(rows[0])] * (rows_ref.shape[0] - len(rows))
    rows_ref[...] = jnp.concatenate(rows, axis=0)
    turned_ref[...] = jnp.transpose(rows_ref[...])
    first = pl.multiple_of(lax.axis_index("dp") * block, block)
    left_ref[...] = turned_ref[pl.ds(first, block), :]
    pair_total = pairs_of(lengths_ref, lengths_ref.shape[0])
    lead_mean = lead_row = lag_row = 0.0
    for k in range(far):
        lead_mean += left_ref[:, k : k + 1]
        lead_row += rows_ref[k : k + 1, columns]
        lag_row += rows_ref[far + k : far + k + 1, columns]
    lead_mean, lead_row, lag_row = (v / pair_total for v in (lead_mean, lead_row, lag_row))
    lag = gathered_total(kept_ref, came_refs, rows_ref, left_ref, columns)
    zero = jnp.zeros_like(lag)
    for k in range(far):
        weight = live_of(lengths_ref, [4 * k + i for i in range(4)])
        lead = left_ref[:, k : k + 1] - lead_mean * weight
        zero = zero + lead * (rows_ref[k : k + 1, columns] / weight - lead_row)
        lag = lag + lead * (rows_ref[far + k : far + k + 1, columns] / weight - lag_row)
    out_ref[...] = lag / pair_total
    zero_ref[...] = zero


def finish_lag(lengths, info, kept, came):
    block, half = kept.shape
    feats = 2 * half
    far = len(came) + 1
    rows = round_up(3 * far - 1, 8)
    return pl.pallas_call(
        functools.partial(finish_lag_kernel, far=far),
        in_specs=[SCALARS] + [WHOLE] * (2 + len(came)),
        out_specs=[WHOLE] * 4,
        out_shape=[shape(kept.shape), shape(kept.shape), shape((rows, feats)), shape((block, rows))],
        scratch_shapes=[pltpu.VMEM((feats, rows), jnp.float32)],
        compiler_params=params(),
        name="finish_lag",
    )(lengths, info, kept, *came)


def finish_zero_kernel(lengths_ref, rows_ref, left_ref, between_ref, kept_ref, *refs):
    came_refs, out_ref = refs[:-1], refs[-1]
    columns = side_columns(kept_ref.shape[1], True)
    zero = gathered_total(kept_ref, came_refs, rows_ref, left_ref, columns)
    out_ref[...] = (zero + between_ref[...]) / pairs_of(lengths_ref, lengths_ref.shape[0])


def finish_zero(lengths, rows, left, between, kept, came):
    return pl.pallas_call(
        finish_zero_kernel,
        in_specs=[SCALARS] + [WHOLE] * (4 + len(came)),
        out_specs=WHOLE,
        out_shape=shape(kept.shape),
        compiler_params=params(),
        name="finish_zero",
    )(lengths, rows, left, between, kept, *came)


def exclusive(size, distance):
    return [(i, i ^ distance) for i in range(size)]


def local(coords, lengths, atom_pairs):
    feats = atom_pairs.shape[1]
    dp = lax.axis_size("dp")
    far = dp // 2
    block = feats // dp
    home = coords.shape[0]
    depth = round_up(home - LAG, DEPTH_UNIT)
    rows = round_up(max(home, depth + LAG), FRAME_TILE)

    def swap(array, axis, distance):
        return lax.ppermute(array, axis, exclusive(lax.axis_size(axis), distance))

    coords = pltpu.with_memory_space_constraint(jnp.transpose(coords, (1, 0, 2)), pltpu.HBM)
    atom_pairs = pltpu.with_memory_space_constraint(atom_pairs, pltpu.HBM)
    features, stats, sent_lag = contacts_call(coords, lengths, atom_pairs, rows, depth)
    common = [lengths, features, stats]
    half = feats // 2
    kept_shape = shape((feats, half))
    came_lag = swap(sent_lag, "tile", 1)
    (kept_lag,) = gram_call(kept_lag_kernel, common, [sent_lag], [kept_shape], depth, LONG)
    keep_lag, sent_lag, chip = near_call(lengths, kept_lag, stats, [came_lag], block, True)
    came_lag = swap(sent_lag, "dp", 1)
    *sent_zero, kept_zero = gram_call(
        zero_kernel,
        common,
        [sent_lag],
        [shape((feats // SPLIT, half), jnp.int16)] * SPLIT + [kept_shape],
        depth,
        SHORT,
    )
    came_zero = [swap(part, "tile", 1) for part in sent_zero]
    keep_zero, sent_zero = near_call(lengths, kept_zero, chip, came_zero, block, False)
    came_zero = swap(sent_zero, "dp", 1)

    kept_lag, *sent_lag, pair = far_call(lengths, keep_lag, came_lag, chip, block, True)
    came_lag = [swap(s, "dp", 2 * (i + 1)) for i, s in enumerate(sent_lag)]
    kept_zero, *sent_zero = far_call(lengths, keep_zero, came_zero, pair, block, False)
    came_zero = [swap(s, "dp", 2 * (i + 1)) for i, s in enumerate(sent_zero)]
    cov_lag, between, total_rows, total_left = finish_lag(lengths, pair, kept_lag, came_lag)
    cov_zero = finish_zero(lengths, total_rows, total_left, between, kept_zero, came_zero)
    return (cov_zero, cov_lag)


def solution(mesh):
    placed = (P(("groups", "dp", "tile"), None, None), P("groups"), P())
    return jax.shard_map(
        local,
        mesh=mesh,
        in_specs=placed,
        out_specs=(P(("groups", "dp"), "tile"), P(("groups", "dp"), "tile")),
        check_vma=False,
    )
```

time: 71.1 us -> 67.6 us (0.951)
  starting transfers between devices: 19.1 us -> 13.3 us
  waiting for transfers between devices: 14 us -> 18.8 us
  local copies, waits for them, and re-layouts: 2.41 us -> 0.66 us
    ppermute x15 -> x13, starting transfers between devices: 19.1 us -> 13.3 us  [swap(): return lax.ppermute(array, axis, exclusive(lax.axis_size(axis), distance))]
    ppermute x15 -> x13, waiting for transfers between devices: 14 us -> 18.8 us  [swap(): return lax.ppermute(array, axis, exclusive(lax.axis_size(axis), distance))]
    pallas_call x4 -> x2, Pallas kernels: 13.2 us -> 9.22 us  [gram_call(): pl.pallas_call(body, in_specs=[SCALARS] + [WHOLE] * (len(operands) - 1) +...]
    pallas_call x1, Pallas kernels: 11.4 us -> 14.4 us  [contacts_call(): pl.pallas_call(contacts_kernel, grid=(rows // FRAME_TILE,), in_specs=[SCA...]
    unnamed x10 -> x4, local copies, waits for them, and re-layouts: 2.3 us -> 0.66 us
  transfers between devices with their start and end apart: 15 -> 13, of which waited for: 3 -> 8; matrix products, arithmetic and copies ran while one was open for 0% -> 0% of each run, Pallas kernels for 31% -> 24%
where the time goes in v4:
time: 67.6 us; the launch traced here: 67.5 us
  Pallas kernels  34 us (50%)
  waiting for transfers between devices  18.8 us (28%)
  starting transfers between devices  13.3 us (20%)
  between operations  0.72 us (1%)
    ppermute x13, waiting for transfers between devices, swap(): return lax.ppermute(array, axis, exclusive(lax.axis_size(axis), distance))  18.8 us
    pallas_call x1, Pallas kernels, contacts_call(): pl.pallas_call(contacts_kernel, grid=(rows // FRAME_TILE,), in_specs=[SCA...  14.4 us
    ppermute x13, starting transfers between devices, swap(): return lax.ppermute(array, axis, exclusive(lax.axis_size(axis), distance))  13.3 us
    pallas_call x2, Pallas kernels, gram_call(): pl.pallas_call(body, in_specs=[SCALARS] + [WHOLE] * (len(operands) - 1) +...  9.22 us
    pallas_call x2, Pallas kernels, near_call(): pl.pallas_call(functools.partial(near_kernel, lagged=lagged, block=block,...  3.74 us
    pallas_call x2, Pallas kernels, far_call(): pl.pallas_call(functools.partial(far_kernel, lagged=lagged, block=block,...  2.94 us
    pallas_call x1, Pallas kernels, finish_lag(): pl.pallas_call(functools.partial(finish_lag_kernel, far=far), in_specs=[S...  2.18 us
    pallas_call x1, Pallas kernels, finish_zero(): pl.pallas_call(finish_zero_kernel, in_specs=[SCALARS] + [WHOLE] * (4 + le...  1.56 us
  transfers between devices with their start and end apart: 13, of which 8 were waited for; matrix products, arithmetic and copies ran while one was open for 0% of the time, Pallas kernels for 24%

profile of v4, /device:TPU:0, one launch (start us, length us, event | category | flops | bytes accessed | tf_op | source)
XLA Modules:
  0.0 67.5 jit_solution(17684099338210961747)
XLA Ops:
  0.6 0.0 copy-start
  0.6 0.6 copy-done
  1.3 14.4 %contacts_sent_lag.1 = (bf16[2560,1024]{1,0:T(8,128)(2,1)S(1)}, f32[8,1024]{1,0:T(8,128)S(1)}, s16[1040,512]{1,0:T(8,128)(2,1)S(1)}) custom-call(s32[16]{0:T(128)S(1)} %copy-done, s32[2,1024]{1,0:T(2,128)} %pairs_ref.1, bf16[3,2516,256]{2,1,0:T(8,128)(2,1)} %bitcast.1), custom_call_target="tpu_custom_call" | custom-call | tf_op jit(solution)/shard_map/contacts_sent_lag/pallas_call | solution.py:197
  15.7 0.5 collective-permute-start
  16.2 3.4 %kept_lag.1.kept_ref = f32[1024,512]{1,0:T(8,128)S(1)} custom-call(s32[16]{0:T(128)S(1)} %copy-done, bf16[2560,1024]{1,0:T(8,128)(2,1)S(1)} %get-tuple-element.28.features_ref, f32[8,1024]{1,0:T(8,128)S(1)} %get-tuple-element.29.stats_ref.info_ref, s16[1040,512]{1,0:T(8,128)(2,1)S(1)} %get-tuple-element.30._), custom_call_target="tpu_custom_call" | custom-call | flops 17179869184 | bytes 16777216 | tf_op jit(solution)/shard_map/kept_lag/pallas_call | solution.py:255
  19.6 0.0 collective-permute-done.refs_0_
  19.6 1.9 %near_lag.1 = (f32[512,512]{1,0:T(8,128)S(1)}, s16[528,512]{1,0:T(8,128)(2,1)S(1)}, f32[8,1024]{1,0:T(8,128)S(1)}) custom-call(s32[16]{0:T(128)S(1)} %copy-done, f32[1024,512]{1,0:T(8,128)S(1)} %kept_lag.1.kept_ref, f32[8,1024]{1,0:T(8,128)S(1)} %get-tuple-element.29.stats_ref.info_ref, s16[1040,512]{1,0:T(8,128)(2,1)S(1)} %collective-permute-done.refs_0_), custom_call_target="tpu_custom_call" | custom-call | tf_op jit(solution)/shard_map/near_lag/pallas_call | solution.py:308
  21.5 0.0 copy-start.1
  21.5 2.6 %collective-permute-start.1 = (s16[528,512]{1,0:T(8,128)(2,1)S(1)}, s16[528,512]{1,0:T(8,128)(2,1)S(1)}, u32[]{:S(2)}, u32[]{:S(2)}) collective-permute-start(s16[528,512]{1,0:T(8,128)(2,1)S(1)} %get-tuple-element.32._), channel_id=1, source_target_pairs={{0,2},{2,0},{4,6},{6,4},{8,10},{10,8},{12,14},{14,12},{1,3},{3,1},... | collective-permute-start | bytes 1622024 | tf_op jit(solution)/shard_map/ppermute | solution.py:469
  24.1 5.8 %zero.1 = (s16[256,512]{1,0:T(8,128)(2,1)S(1)}, s16[256,512]{1,0:T(8,128)(2,1)S(1)}, s16[256,512]{1,0:T(8,128)(2,1)S(1)}, s16[256,512]{1,0:T(8,128)(2,1)S(1)}, f32[1024,512]{1,0:T(8,128)S(1)}) custom-call(s32[16]{0:T(128)S(1)} %copy-done, bf16[2560,1024]{1,0:T(8,128)(2,1)S(1)} %get-tuple-element.28.features_ref, ...), custom_call_target="tpu_custom_call" | custom-call | flops 1048576 | bytes 1024 | tf_op jit(solution)/shard_map/zero/pallas_call | solution.py:255
  30.0 0.3 collective-permute-start.5
  30.3 0.3 collective-permute-start.6
  30.6 0.2 collective-permute-start.7
  30.8 0.3 collective-permute-start.8
  31.1 0.5 collective-permute-done.5.refs_0_
  31.6 0.4 collective-permute-done.6.refs_1_
  32.0 0.4 collective-permute-done.7.refs_2_
  32.3 0.4 collective-permute-done.8.refs_3_
  32.7 0.0 copy-done.1
  32.7 1.8 %near_zero.1 = (f32[512,512]{1,0:T(8,128)S(1)}, s16[512,512]{1,0:T(8,128)(2,1)S(1)}) custom-call(s32[16]{0:T(128)S(1)} %copy-done.1, f32[1024,512]{1,0:T(8,128)S(1)} %get-tuple-element.42.kept_ref, f32[8,1024]{1,0:T(8,128)S(1)} %get-tuple-element.33.info_ref, s16[256,512]{1,0:T(8,128)(2,1)S(1)} %collective-permute-done.5.refs_0_, ...), custom_call_target="tpu_custom_call" | custom-call | tf_op jit(solution)/shard_map/near_zero/pallas_call | solution.py:308
  34.5 0.2 collective-permute-start.9
  34.7 2.3 %collective-permute-done.1.came_ref = s16[528,512]{1,0:T(8,128)(2,1)S(1)} collective-permute-done((s16[528,512]{1,0:T(8,128)(2,1)S(1)}, s16[528,512]{1,0:T(8,128)(2,1)S(1)}, u32[]{:S(2)}, u32[]{:S(2)}) %collective-permute-start.1) | collective-permute-done | bytes 540704 | tf_op jit(solution)/shard_map/ppermute | solution.py:469
  37.1 1.6 %far_lag.1 = (f32[128,512]{1,0:T(8,128)S(1)}, s16[144,512]{1,0:T(8,128)(2,1)S(1)}, s16[144,512]{1,0:T(8,128)(2,1)S(1)}, s16[144,512]{1,0:T(8,128)(2,1)S(1)}, f32[8,1024]{1,0:T(8,128)S(1)}) custom-call(s32[16]{0:T(128)S(1)} %copy-done.1, f32[512,512]{1,0:T(8,128)S(1)} %get-tuple-element.31.keep_ref, s16[528,512]{1,0:T(8,128)(2,1)S(1)} %collective-permute-done.1.came_ref, ...), custom_call_target="tpu_custom_call" | custom-call | flops 17179869184 | bytes 16777216 | tf_op jit(solution)/shard_map/far_lag/pallas_call | solution.py:360
  38.6 1.9 %collective-permute-start.2 = (s16[144,512]{1,0:T(8,128)(2,1)S(1)}, s16[144,512]{1,0:T(8,128)(2,1)S(1)}, u32[]{:S(2)}, u32[]{:S(2)}) collective-permute-start(s16[144,512]{1,0:T(8,128)(2,1)S(1)} %get-tuple-element.36), channel_id=1, source_target_pairs={{0,4},{2,6},{4,0},{6,2},{8,12},{10,14},{12,8},{14,10},{1,5},{3,7},... | collective-permute-start | bytes 442376 | tf_op jit(solution)/shard_map/ppermute | solution.py:469
  40.5 2.6 %collective-permute-start.3 = (s16[144,512]{1,0:T(8,128)(2,1)S(1)}, s16[144,512]{1,0:T(8,128)(2,1)S(1)}, u32[]{:S(2)}, u32[]{:S(2)}) collective-permute-start(s16[144,512]{1,0:T(8,128)(2,1)S(1)} %get-tuple-element.37), channel_id=1, source_target_pairs={{0,8},{2,10},{4,12},{6,14},{8,0},{10,2},{12,4},{14,6},{1,9},{3,11}... | collective-permute-start | bytes 442376 | tf_op jit(solution)/shard_map/ppermute | solution.py:469
  43.1 0.0 collective-permute-start.4
  43.1 5.6 %collective-permute-done.9.came_ref = s16[512,512]{1,0:T(8,128)(2,1)S(1)} collective-permute-done((s16[512,512]{1,0:T(8,128)(2,1)S(1)}, s16[512,512]{1,0:T(8,128)(2,1)S(1)}, u32[]{:S(2)}, u32[]{:S(2)}) %collective-permute-start.9) | collective-permute-done | bytes 524320 | tf_op jit(solution)/shard_map/ppermute | solution.py:469
  48.6 1.4 %far_zero.1 = (f32[128,512]{1,0:T(8,128)S(1)}, s16[128,512]{1,0:T(8,128)(2,1)S(1)}, s16[128,512]{1,0:T(8,128)(2,1)S(1)}, s16[128,512]{1,0:T(8,128)(2,1)S(1)}) custom-call(s32[16]{0:T(128)S(1)} %copy-done.1, f32[512,512]{1,0:T(8,128)S(1)} %get-tuple-element.47.keep_ref, s16[512,512]{1,0:T(8,128)(2,1)S(1)} %collective-permute-done.9.came_ref, ...), custom_call_target="tpu_custom_call" | custom-call | flops 1048576 | bytes 1024 | tf_op jit(solution)/shard_map/far_zero/pallas_call | solution.py:360
  50.0 1.7 %collective-permute-start.10 = (s16[128,512]{1,0:T(8,128)(2,1)S(1)}, s16[128,512]{1,0:T(8,128)(2,1)S(1)}, u32[]{:S(2)}, u32[]{:S(2)}) collective-permute-start(s16[128,512]{1,0:T(8,128)(2,1)S(1)} %get-tuple-element.50), channel_id=1, source_target_pairs={{0,4},{2,6},{4,0},{6,2},{8,12},{10,14},{12,8},{14,10},{1,5},{3,7},... | collective-permute-start | bytes 393224 | tf_op jit(solution)/shard_map/ppermute | solution.py:469
  51.7 2.6 %collective-permute-start.11 = (s16[128,512]{1,0:T(8,128)(2,1)S(1)}, s16[128,512]{1,0:T(8,128)(2,1)S(1)}, u32[]{:S(2)}, u32[]{:S(2)}) collective-permute-start(s16[128,512]{1,0:T(8,128)(2,1)S(1)} %get-tuple-element.51), channel_id=1, source_target_pairs={{0,8},{2,10},{4,12},{6,14},{8,0},{10,2},{12,4},{14,6},{1,9},{3,11}... | collective-permute-start | bytes 393224 | tf_op jit(solution)/shard_map/ppermute | solution.py:469
  54.3 0.0 collective-permute-done.2.refs_0_
  54.3 0.2 collective-permute-start.12
  54.5 0.0 collective-permute-done.3.refs_1_
  54.5 0.0 collective-permute-done.4.refs_2_
  54.5 2.2 %finish_lag.1 = (f32[128,512]{1,0:T(8,128)}, f32[128,512]{1,0:T(8,128)S(1)}, f32[16,1024]{1,0:T(8,128)S(1)}, f32[128,16]{1,0:T(8,128)S(1)}) custom-call(s32[16]{0:T(128)S(1)} %copy-done.1, f32[8,1024]{1,0:T(8,128)S(1)} %get-tuple-element.34.info_ref, f32[128,512]{1,0:T(8,128)S(1)} %get-tuple-element.35.kept_ref, ...), custom_call_target="tpu_custom_call" | custom-call | tf_op jit(solution)/shard_map/finish_lag/pallas_call | solution.py:426
  56.7 0.7 %collective-permute-done.10.refs_0_ = s16[128,512]{1,0:T(8,128)(2,1)S(1)} collective-permute-done((s16[128,512]{1,0:T(8,128)(2,1)S(1)}, s16[128,512]{1,0:T(8,128)(2,1)S(1)}, u32[]{:S(2)}, u32[]{:S(2)}) %collective-permute-start.10) | collective-permute-done | bytes 131104 | tf_op jit(solution)/shard_map/ppermute | solution.py:469
  57.4 8.6 %collective-permute-done.11.refs_1_ = s16[128,512]{1,0:T(8,128)(2,1)S(1)} collective-permute-done((s16[128,512]{1,0:T(8,128)(2,1)S(1)}, s16[128,512]{1,0:T(8,128)(2,1)S(1)}, u32[]{:S(2)}, u32[]{:S(2)}) %collective-permute-start.11) | collective-permute-done | bytes 131104 | tf_op jit(solution)/shard_map/ppermute | solution.py:469
  65.9 0.0 collective-permute-done.12.refs_2_
  65.9 1.6 %finish_zero.1 = f32[128,512]{1,0:T(8,128)} custom-call(s32[16]{0:T(128)S(1)} %copy-done.1, f32[16,1024]{1,0:T(8,128)S(1)} %get-tuple-element.39.rows_ref, f32[128,16]{1,0:T(8,128)S(1)} %get-tuple-element.40.left_ref, f32[128,512]{1,0:T(8,128)S(1)} %get-tuple-element.41.between_ref, f32[128,512]{1,0:T(8,128)S(1)} %get-tuple-element.49.kept_ref, ...), custom_call_target="tpu_custom_call" | custom-call | tf_op jit(solution)/shard_map/finish_zero/pallas_call | solution.py:445
Async XLA Ops:
  0.6 0.7 copy-start
  15.7 3.9 %collective-permute-start = (s16[1040,512]{1,0:T(8,128)(2,1)S(1)}, s16[1040,512]{1,0:T(8,128)(2,1)S(1)}, u32[]{:S(2)}, u32[]{:S(2)}) collective-permute-start(s16[1040,512]{1,0:T(8,128)(2,1)S(1)} %get-tuple-element.30._), channel_id=1, source_target_pairs={{0,1},{1,0},{2,3},{3,2},{4,5},{5,4},{6,7},{7,6},{8,9},{9,8},{10,11... | collective-permute-start | bytes 3194888 | tf_op jit(solution)/shard_map/ppermute | solution.py:469
  21.5 11.2 %copy-start.1 = (s32[16]{0:T(128)S(1)}, s32[16]{0:T(128)}, u32[]{:S(2)}) copy-start(s32[16]{0:T(128)} %lengths_ref.17) | copy-start | bytes 196
  21.5 15.5 %collective-permute-start.1 = (s16[528,512]{1,0:T(8,128)(2,1)S(1)}, s16[528,512]{1,0:T(8,128)(2,1)S(1)}, u32[]{:S(2)}, u32[]{:S(2)}) collective-permute-start(s16[528,512]{1,0:T(8,128)(2,1)S(1)} %get-tuple-element.32._), channel_id=1, source_target_pairs={{0,2},{2,0},{4,6},{6,4},{8,10},{10,8},{12,14},{14,12},{1,3},{3,1},... | collective-permute-start | bytes 1622024 | tf_op jit(solution)/shard_map/ppermute | solution.py:469
  30.0 1.6 %collective-permute-start.5 = (s16[256,512]{1,0:T(8,128)(2,1)S(1)}, s16[256,512]{1,0:T(8,128)(2,1)S(1)}, u32[]{:S(2)}, u32[]{:S(2)}) collective-permute-start(s16[256,512]{1,0:T(8,128)(2,1)S(1)} %get-tuple-element.43), channel_id=1, source_target_pairs={{0,1},{1,0},{2,3},{3,2},{4,5},{5,4},{6,7},{7,6},{8,9},{9,8},{10,11... | collective-permute-start | bytes 786440 | tf_op jit(solution)/shard_map/ppermute | solution.py:469
  30.3 1.7 %collective-permute-start.6 = (s16[256,512]{1,0:T(8,128)(2,1)S(1)}, s16[256,512]{1,0:T(8,128)(2,1)S(1)}, u32[]{:S(2)}, u32[]{:S(2)}) collective-permute-start(s16[256,512]{1,0:T(8,128)(2,1)S(1)} %get-tuple-element.44), channel_id=1, source_target_pairs={{0,1},{1,0},{2,3},{3,2},{4,5},{5,4},{6,7},{7,6},{8,9},{9,8},{10,11... | collective-permute-start | bytes 786440 | tf_op jit(solution)/shard_map/ppermute | solution.py:469
  30.6 1.8 %collective-permute-start.7 = (s16[256,512]{1,0:T(8,128)(2,1)S(1)}, s16[256,512]{1,0:T(8,128)(2,1)S(1)}, u32[]{:S(2)}, u32[]{:S(2)}) collective-permute-start(s16[256,512]{1,0:T(8,128)(2,1)S(1)} %get-tuple-element.45), channel_id=1, source_target_pairs={{0,1},{1,0},{2,3},{3,2},{4,5},{5,4},{6,7},{7,6},{8,9},{9,8},{10,11... | collective-permute-start | bytes 786440 | tf_op jit(solution)/shard_map/ppermute | solution.py:469
  30.8 1.9 %collective-permute-start.8 = (s16[256,512]{1,0:T(8,128)(2,1)S(1)}, s16[256,512]{1,0:T(8,128)(2,1)S(1)}, u32[]{:S(2)}, u32[]{:S(2)}) collective-permute-start(s16[256,512]{1,0:T(8,128)(2,1)S(1)} %get-tuple-element.46), channel_id=1, source_target_pairs={{0,1},{1,0},{2,3},{3,2},{4,5},{5,4},{6,7},{7,6},{8,9},{9,8},{10,11... | collective-permute-start | bytes 786440 | tf_op jit(solution)/shard_map/ppermute | solution.py:469
  34.5 14.1 %collective-permute-start.9 = (s16[512,512]{1,0:T(8,128)(2,1)S(1)}, s16[512,512]{1,0:T(8,128)(2,1)S(1)}, u32[]{:S(2)}, u32[]{:S(2)}) collective-permute-start(s16[512,512]{1,0:T(8,128)(2,1)S(1)} %get-tuple-element.48), channel_id=1, source_target_pairs={{0,2},{2,0},{4,6},{6,4},{8,10},{10,8},{12,14},{14,12},{1,3},{3,1},... | collective-permute-start | bytes 1572872 | tf_op jit(solution)/shard_map/ppermute | solution.py:469
  38.6 15.7 %collective-permute-start.2 = (s16[144,512]{1,0:T(8,128)(2,1)S(1)}, s16[144,512]{1,0:T(8,128)(2,1)S(1)}, u32[]{:S(2)}, u32[]{:S(2)}) collective-permute-start(s16[144,512]{1,0:T(8,128)(2,1)S(1)} %get-tuple-element.36), channel_id=1, source_target_pairs={{0,4},{2,6},{4,0},{6,2},{8,12},{10,14},{12,8},{14,10},{1,5},{3,7},... | collective-permute-start | bytes 442376 | tf_op jit(solution)/shard_map/ppermute | solution.py:469
  40.5 14.0 %collective-permute-start.3 = (s16[144,512]{1,0:T(8,128)(2,1)S(1)}, s16[144,512]{1,0:T(8,128)(2,1)S(1)}, u32[]{:S(2)}, u32[]{:S(2)}) collective-permute-start(s16[144,512]{1,0:T(8,128)(2,1)S(1)} %get-tuple-element.37), channel_id=1, source_target_pairs={{0,8},{2,10},{4,12},{6,14},{8,0},{10,2},{12,4},{14,6},{1,9},{3,11}... | collective-permute-start | bytes 442376 | tf_op jit(solution)/shard_map/ppermute | solution.py:469
  43.1 11.4 %collective-permute-start.4 = (s16[144,512]{1,0:T(8,128)(2,1)S(1)}, s16[144,512]{1,0:T(8,128)(2,1)S(1)}, u32[]{:S(2)}, u32[]{:S(2)}) collective-permute-start(s16[144,512]{1,0:T(8,128)(2,1)S(1)} %get-tuple-element.38), channel_id=1, source_target_pairs={{0,12},{2,14},{4,8},{6,10},{8,4},{10,6},{12,0},{14,2},{1,13},{3,15... | collective-permute-start | bytes 442376 | tf_op jit(solution)/shard_map/ppermute | solution.py:469
  50.0 7.3 %collective-permute-start.10 = (s16[128,512]{1,0:T(8,128)(2,1)S(1)}, s16[128,512]{1,0:T(8,128)(2,1)S(1)}, u32[]{:S(2)}, u32[]{:S(2)}) collective-permute-start(s16[128,512]{1,0:T(8,128)(2,1)S(1)} %get-tuple-element.50), channel_id=1, source_target_pairs={{0,4},{2,6},{4,0},{6,2},{8,12},{10,14},{12,8},{14,10},{1,5},{3,7},... | collective-permute-start | bytes 393224 | tf_op jit(solution)/shard_map/ppermute | solution.py:469
  51.7 14.3 %collective-permute-start.11 = (s16[128,512]{1,0:T(8,128)(2,1)S(1)}, s16[128,512]{1,0:T(8,128)(2,1)S(1)}, u32[]{:S(2)}, u32[]{:S(2)}) collective-permute-start(s16[128,512]{1,0:T(8,128)(2,1)S(1)} %get-tuple-element.51), channel_id=1, source_target_pairs={{0,8},{2,10},{4,12},{6,14},{8,0},{10,2},{12,4},{14,6},{1,9},{3,11}... | collective-permute-start | bytes 393224 | tf_op jit(solution)/shard_map/ppermute | solution.py:469
  54.3 11.7 %collective-permute-start.12 = (s16[128,512]{1,0:T(8,128)(2,1)S(1)}, s16[128,512]{1,0:T(8,128)(2,1)S(1)}, u32[]{:S(2)}, u32[]{:S(2)}) collective-permute-start(s16[128,512]{1,0:T(8,128)(2,1)S(1)} %get-tuple-element.52), channel_id=1, source_target_pairs={{0,12},{2,14},{4,8},{6,10},{8,4},{10,6},{12,0},{14,2},{1,13},{3,15... | collective-permute-start | bytes 393224 | tf_op jit(solution)/shard_map/ppermute | solution.py:469

commit v5 on v4

--- a/solution.py
+++ b/solution.py
@@ -18,6 +18,7 @@
 PART = 32000.0
 INVERSE_LOG_TWO = 1.4426950408889634
 TAIL = 16
+LANES = 128
 LONG = 1 << 34
 SHORT = 1 << 20
 SPLIT = 4
@@ -83,12 +84,21 @@
     return vectors
 
 
-def live_of(lengths_ref, distances):
+def count_pairs(lengths_ref, counts_ref):
     place = own_place()
+    lane = lax.broadcasted_iota(jnp.int32, (1, counts_ref.shape[1]), 1)
+    counts = jnp.zeros(lane.shape, jnp.float32)
     total = 0
-    for distance in distances:
-        total = total + lengths_ref[place ^ distance] - LAG
-    return total.astype(jnp.float32)
+    for distance in range(lengths_ref.shape[0]):
+        live = lengths_ref[place ^ distance] - LAG
+        counts = jnp.where(lane == distance, live.astype(jnp.float32), counts)
+        total = total + live
+    counts_ref[0:1, :] = counts
+    counts_ref[1:8, :] = jnp.broadcast_to(total.astype(jnp.float32), (7, counts_ref.shape[1]))
+
+
+def live_of(counts_ref, distances):
+    return sum(counts_ref[0:1, d : d + 1] for d in distances)
 
 
 def pool(info_ref, sums, spread, count, other_block, other_count):
@@ -118,7 +128,7 @@
 
 def gram_rows(features_ref, right_ref, start, live):
     depth = right_ref.shape[0]
-    alive = lax.broadcasted_iota(jnp.int32, (depth, 1), 0) < live
+    alive = lax.broadcasted_iota(jnp.int32, (depth, 1), 0).astype(jnp.float32) < live
     left = jnp.where(alive, features_ref[0:depth, start : start + FEATURE_TILE], 0.0)
     return lax.dot_general(
         left.astype(jnp.bfloat16),
@@ -129,7 +139,7 @@
 
 
 def contacts_kernel(
-    lengths_ref, pairs_ref, coords_ref, features_ref, stats_ref, sent_ref, table_ref, right_ref
+    lengths_ref, pairs_ref, coords_ref, features_ref, stats_ref, sent_ref, counts_ref, table_ref, right_ref
 ):
     step = pl.program_id(0)
     atoms, feats = table_ref.shape
@@ -142,6 +152,7 @@
         second_hit = (atom_ids == pairs_ref[1:2, :]).astype(jnp.float32)
         table_ref[...] = (first_hit - second_hit).astype(jnp.bfloat16)
         stats_ref[...] = jnp.zeros_like(stats_ref)
+        count_pairs(lengths_ref, counts_ref)
 
     live = lengths_ref[own_place()] - LAG
     frame = step * tile + lax.broadcasted_iota(jnp.int32, (tile, 1), 0)
@@ -185,7 +196,7 @@
         stats_ref[1:2, :] += total
         spread = squares - total * total / count.astype(jnp.float32)
         stats_ref[2:3, :] = jnp.maximum(spread, 0.0) + (SLACK * squares + FLOOR)
-        gram_half(features_ref, stats_ref, [sent_ref], right_ref, live, False, True)
+        gram_half(counts_ref, features_ref, stats_ref, [sent_ref], right_ref, False, True)
         sent_ref[feats : feats + TAIL, :] = encode(
             [stats_ref[0:1, :], stats_ref[1:2, :], jnp.sqrt(stats_ref[2:3, :])]
         )
@@ -202,11 +213,12 @@
             pl.BlockSpec((2, feats), lambda i: (0, 0)),
             pl.BlockSpec((3, FRAME_TILE, atoms), lambda i: (0, i, 0)),
         ],
-        out_specs=[WHOLE, WHOLE, WHOLE],
+        out_specs=[WHOLE] * 4,
         out_shape=[
             shape((rows, feats), jnp.bfloat16),
             shape((8, feats)),
             shape((feats + TAIL, feats // 2), jnp.int16),
+            shape((8, LANES)),
         ],
         scratch_shapes=[
             pltpu.VMEM((atoms, feats), jnp.bfloat16),
@@ -217,7 +229,7 @@
     )(lengths, atom_pairs, coords)
 
 
-def gram_half(features_ref, stats_ref, out_refs, right_ref, live, kept, lagged):
+def gram_half(counts_ref, features_ref, stats_ref, out_refs, right_ref, kept, lagged):
     half = out_refs[0].shape[1]
     feats = 2 * half
     part = feats // len(out_refs)
@@ -225,7 +237,8 @@
     columns = side_columns(half, kept)
     right = 1 if lagged else 0
     left_stats = jnp.transpose(stats_ref[...])
-    right_mean = stats_ref[right : right + 1, columns] / live.astype(jnp.float32)
+    live = live_of(counts_ref, [0])
+    right_mean = stats_ref[right : right + 1, columns] / live
     right_inverse = lax.rsqrt(stats_ref[2:3, columns])
     for start in range(0, feats, FEATURE_TILE):
         rows = slice(start, start + FEATURE_TILE)
@@ -238,24 +251,21 @@
         out_refs[start // part][first : first + FEATURE_TILE, :] = gram
 
 
-def kept_lag_kernel(lengths_ref, features_ref, stats_ref, _, kept_ref, right_ref):
-    live = lengths_ref[own_place()] - LAG
-    gram_half(features_ref, stats_ref, [kept_ref], right_ref, live, True, True)
-
-
-def zero_kernel(lengths_ref, features_ref, stats_ref, _, *refs):
+def kept_lag_kernel(counts_ref, features_ref, stats_ref, _, kept_ref, right_ref):
+    gram_half(counts_ref, features_ref, stats_ref, [kept_ref], right_ref, True, True)
+
+
+def zero_kernel(counts_ref, features_ref, stats_ref, _, *refs):
     sent_refs, kept_ref, right_ref = refs[:-2], refs[-2], refs[-1]
-    live = lengths_ref[own_place()] - LAG
-    gram_half(features_ref, stats_ref, sent_refs, right_ref, live, False, False)
-    gram_half(features_ref, stats_ref, [kept_ref], right_ref, live, True, False)
+    gram_half(counts_ref, features_ref, stats_ref, sent_refs, right_ref, False, False)
+    gram_half(counts_ref, features_ref, stats_ref, [kept_ref], right_ref, True, False)
 
 
 def gram_call(body, operands, after, outs, depth, estimate):
     feats = operands[1].shape[1]
     return pl.pallas_call(
         body,
-        in_specs=[SCALARS]
-        + [WHOLE] * (len(operands) - 1)
+        in_specs=[WHOLE] * len(operands)
         + [pl.BlockSpec(memory_space=pl.ANY)] * len(after),
         out_specs=[WHOLE] * len(outs),
         out_shape=outs,
@@ -266,13 +276,13 @@
     )(*operands, *after)
 
 
-def near_kernel(lengths_ref, kept_ref, info_ref, *refs, lagged, block, parts):
+def near_kernel(counts_ref, kept_ref, info_ref, *refs, lagged, block, parts):
     came_refs, keep_ref, sent_ref = refs[:parts], refs[parts], refs[parts + 1]
     near = lax.axis_index("dp") % 2
     feats, half = kept_ref.shape
     part = feats // parts
     columns = side_columns(half, True)
-    count, peer_count = live_of(lengths_ref, [0]), live_of(lengths_ref, [1])
+    count, peer_count = live_of(counts_ref, [0]), live_of(counts_ref, [1])
     if lagged:
         stats_ref, info_ref = info_ref, refs[-1]
         sums = (stats_ref[0:1, :], stats_ref[1:2, :])
@@ -300,29 +310,29 @@
         sent_ref[target, :] = to_levels(other * (lax.rsqrt(spread) * sent_right))
 
 
-def near_call(lengths, kept, info, came, block, lagged):
+def near_call(counts, kept, info, came, block, lagged):
     feats, half = kept.shape
     outs = [shape((half, half)), shape((half + (TAIL if lagged else 0), half), jnp.int16)]
     if lagged:
         outs.append(shape((8, feats)))
     return pl.pallas_call(
         functools.partial(near_kernel, lagged=lagged, block=block, parts=len(came)),
-        in_specs=[SCALARS] + [WHOLE] * (2 + len(came)),
+        in_specs=[WHOLE] * (3 + len(came)),
         out_specs=[WHOLE] * len(outs),
         out_shape=outs,
         compiler_params=params(),
         name="near_lag" if lagged else "near_zero",
-    )(lengths, kept, info, *came)
-
-
-def far_kernel(lengths_ref, keep_ref, came_ref, info_ref, *refs, lagged, block, far):
+    )(counts, kept, info, *came)
+
+
+def far_kernel(counts_ref, keep_ref, came_ref, info_ref, *refs, lagged, block, far):
     kept_ref, sent_refs = refs[0], refs[1:far]
     total_ref, level_ref = refs[-2], refs[-1]
     place = lax.axis_index("dp")
     near, own_far = place % 2, place // 2
     half = keep_ref.shape[0]
     columns = side_columns(half, True)
-    count, near_count = live_of(lengths_ref, [0, 1]), live_of(lengths_ref, [2, 3])
+    count, near_count = live_of(counts_ref, [0, 1]), live_of(counts_ref, [2, 3])
     if lagged:
         chip_ref, info_ref = info_ref, refs[far]
         sums = (chip_ref[4:5, :], chip_ref[5:6, :])
@@ -349,7 +359,7 @@
         sent_ref[0:block, :] = level_ref[own_far ^ (step + 1)]
 
 
-def far_call(lengths, keep, came, info, block, lagged):
+def far_call(counts, keep, came, info, block, lagged):
     half = keep.shape[0]
     far = half // block
     outs = [shape((block, half))]
@@ -359,7 +369,7 @@
     estimate = LONG if lagged else SHORT
     return pl.pallas_call(
         functools.partial(far_kernel, lagged=lagged, block=block, far=far),
-        in_specs=[SCALARS] + [WHOLE] * 3,
+        in_specs=[WHOLE] * 4,
         out_specs=[WHOLE] * len(outs),
         out_shape=outs,
         scratch_shapes=[
@@ -369,7 +379,15 @@
         compiler_params=params(),
         cost_estimate=pl.CostEstimate(flops=estimate, bytes_accessed=estimate // 1024, transcendentals=0),
         name="far_lag" if lagged else "far_zero",
-    )(lengths, keep, came, info)
+    )(counts, keep, came, info)
+
+
+def first_last(items):
+    return [*items[1:], *items[:1]]
+
+
+def last_first(items):
+    return [*items[-1:], *items[:-1]]
 
 
 def gathered_total(kept_ref, came_refs, rows_ref, left_ref, columns):
@@ -382,13 +400,8 @@
     return total
 
 
-def pairs_of(lengths_ref, members):
-    total = lax.fori_loop(0, members, lambda i, t: t + lengths_ref[i] - LAG, 0)
-    return total.astype(jnp.float32)
-
-
-def finish_lag_kernel(lengths_ref, info_ref, kept_ref, *refs, far):
-    came_refs = refs[: far - 1]
+def finish_lag_kernel(counts_ref, info_ref, kept_ref, *refs, far):
+    came_refs = last_first(refs[: far - 1])
     out_ref, zero_ref, rows_ref, left_ref, turned_ref = refs[far - 1 :]
     block, half = kept_ref.shape
     columns = side_columns(half, True)
@@ -400,7 +413,7 @@
     turned_ref[...] = jnp.transpose(rows_ref[...])
     first = pl.multiple_of(lax.axis_index("dp") * block, block)
     left_ref[...] = turned_ref[pl.ds(first, block), :]
-    pair_total = pairs_of(lengths_ref, lengths_ref.shape[0])
+    pair_total = counts_ref[1:2, 0:1]
     lead_mean = lead_row = lag_row = 0.0
     for k in range(far):
         lead_mean += left_ref[:, k : k + 1]
@@ -410,7 +423,7 @@
     lag = gathered_total(kept_ref, came_refs, rows_ref, left_ref, columns)
     zero = jnp.zeros_like(lag)
     for k in range(far):
-        weight = live_of(lengths_ref, [4 * k + i for i in range(4)])
+        weight = live_of(counts_ref, [4 * k + i for i in range(4)])
         lead = left_ref[:, k : k + 1] - lead_mean * weight
         zero = zero + lead * (rows_ref[k : k + 1, columns] / weight - lead_row)
         lag = lag + lead * (rows_ref[far + k : far + k + 1, columns] / weight - lag_row)
@@ -418,38 +431,38 @@
     zero_ref[...] = zero
 
 
-def finish_lag(lengths, info, kept, came):
+def finish_lag(counts, info, kept, came):
     block, half = kept.shape
     feats = 2 * half
     far = len(came) + 1
     rows = round_up(3 * far - 1, 8)
     return pl.pallas_call(
         functools.partial(finish_lag_kernel, far=far),
-        in_specs=[SCALARS] + [WHOLE] * (2 + len(came)),
+        in_specs=[WHOLE] * (3 + len(came)),
         out_specs=[WHOLE] * 4,
         out_shape=[shape(kept.shape), shape(kept.shape), shape((rows, feats)), shape((block, rows))],
         scratch_shapes=[pltpu.VMEM((feats, rows), jnp.float32)],
         compiler_params=params(),
         name="finish_lag",
-    )(lengths, info, kept, *came)
-
-
-def finish_zero_kernel(lengths_ref, rows_ref, left_ref, between_ref, kept_ref, *refs):
-    came_refs, out_ref = refs[:-1], refs[-1]
+    )(counts, info, kept, *first_last(came))
+
+
+def finish_zero_kernel(counts_ref, rows_ref, left_ref, between_ref, kept_ref, *refs):
+    came_refs, out_ref = last_first(refs[:-1]), refs[-1]
     columns = side_columns(kept_ref.shape[1], True)
     zero = gathered_total(kept_ref, came_refs, rows_ref, left_ref, columns)
-    out_ref[...] = (zero + between_ref[...]) / pairs_of(lengths_ref, lengths_ref.shape[0])
-
-
-def finish_zero(lengths, rows, left, between, kept, came):
+    out_ref[...] = (zero + between_ref[...]) / counts_ref[1:2, 0:1]
+
+
+def finish_zero(counts, rows, left, between, kept, came):
     return pl.pallas_call(
         finish_zero_kernel,
-        in_specs=[SCALARS] + [WHOLE] * (4 + len(came)),
+        in_specs=[WHOLE] * (5 + len(came)),
         out_specs=WHOLE,
         out_shape=shape(kept.shape),
         compiler_params=params(),
         name="finish_zero",
-    )(lengths, rows, left, between, kept, *came)
+    )(counts, rows, left, between, kept, *first_last(came))
 
 
 def exclusive(size, distance):
@@ -470,13 +483,14 @@
 
     coords = pltpu.with_memory_space_constraint(jnp.transpose(coords, (1, 0, 2)), pltpu.HBM)
     atom_pairs = pltpu.with_memory_space_constraint(atom_pairs, pltpu.HBM)
-    features, stats, sent_lag = contacts_call(coords, lengths, atom_pairs, rows, depth)
-    common = [lengths, features, stats]
+    lengths = pltpu.with_memory_space_constraint(lengths, pltpu.HBM)
+    features, stats, sent_lag, counts = contacts_call(coords, lengths, atom_pairs, rows, depth)
+    common = [counts, features, stats]
     half = feats // 2
     kept_shape = shape((feats, half))
     came_lag = swap(sent_lag, "tile", 1)
     (kept_lag,) = gram_call(kept_lag_kernel, common, [sent_lag], [kept_shape], depth, LONG)
-    keep_lag, sent_lag, chip = near_call(lengths, kept_lag, stats, [came_lag], block, True)
+    keep_lag, sent_lag, chip = near_call(counts, kept_lag, stats, [came_lag], block, True)
     came_lag = swap(sent_lag, "dp", 1)
     *sent_zero, kept_zero = gram_call(
         zero_kernel,
@@ -487,15 +501,15 @@
         SHORT,
     )
     came_zero = [swap(part, "tile", 1) for part in sent_zero]
-    keep_zero, sent_zero = near_call(lengths, kept_zero, chip, came_zero, block, False)
+    keep_zero, sent_zero = near_call(counts, kept_zero, chip, came_zero, block, False)
     came_zero = swap(sent_zero, "dp", 1)
 
-    kept_lag, *sent_lag, pair = far_call(lengths, keep_lag, came_lag, chip, block, True)
+    kept_lag, *sent_lag, pair = far_call(counts, keep_lag, came_lag, chip, block, True)
     came_lag = [swap(s, "dp", 2 * (i + 1)) for i, s in enumerate(sent_lag)]
-    kept_zero, *sent_zero = far_call(lengths, keep_zero, came_zero, pair, block, False)
+    kept_zero, *sent_zero = far_call(counts, keep_zero, came_zero, pair, block, False)
     came_zero = [swap(s, "dp", 2 * (i + 1)) for i, s in enumerate(sent_zero)]
-    cov_lag, between, total_rows, total_left = finish_lag(lengths, pair, kept_lag, came_lag)
-    cov_zero = finish_zero(lengths, total_rows, total_left, between, kept_zero, came_zero)
+    cov_lag, between, total_rows, total_left = finish_lag(counts, pair, kept_lag, came_lag)
+    cov_zero = finish_zero(counts, total_rows, total_left, between, kept_zero, came_zero)
     return (cov_zero, cov_lag)
 
 

time: 67.6 us -> 64.4 us (0.953)
  Pallas kernels: 34 us -> 31 us
    pallas_call x4, Pallas kernels: 13 us -> 11.5 us  [the longest x2 8.74 us: gram_call(): pl.pallas_call(body, in_specs=[WHOLE] * len(operands) + [pl.BlockSpec(mem...]
    pallas_call x2, Pallas kernels: 3.74 us -> 2.71 us  [near_call(): pl.pallas_call(functools.partial(near_kernel, lagged=lagged, block=block,...]
    pallas_call x2, Pallas kernels: 2.94 us -> 2.05 us  [far_call(): pl.pallas_call(functools.partial(far_kernel, lagged=lagged, block=block,...]
  transfers between devices with their start and end apart: 13 -> 13, of which waited for: 8 -> 7; matrix products, arithmetic and copies ran while one was open for 0% -> 0% of each run, Pallas kernels for 24% -> 22%
where the time goes in v5:
time: 64.4 us; the launch traced here: 63.9 us
  Pallas kernels  31 us (48%)
  waiting for transfers between devices  18.7 us (29%)
  starting transfers between devices  13.5 us (21%)
  between operations  0.7 us (1%)
    ppermute x13, waiting for transfers between devices, swap(): return lax.ppermute(array, axis, exclusive(lax.axis_size(axis), distance))  18.7 us
    pallas_call x1, Pallas kernels, contacts_call(): pl.pallas_call(contacts_kernel, grid=(rows // FRAME_TILE,), in_specs=[SCA...  14.7 us
    ppermute x13, starting transfers between devices, swap(): return lax.ppermute(array, axis, exclusive(lax.axis_size(axis), distance))  13.5 us
    pallas_call x2, Pallas kernels, gram_call(): pl.pallas_call(body, in_specs=[WHOLE] * len(operands) + [pl.BlockSpec(mem...  8.74 us
    pallas_call x2, Pallas kernels, near_call(): pl.pallas_call(functools.partial(near_kernel, lagged=lagged, block=block,...  2.71 us
    pallas_call x2, Pallas kernels, far_call(): pl.pallas_call(functools.partial(far_kernel, lagged=lagged, block=block,...  2.05 us
    pallas_call x1, Pallas kernels, finish_lag(): pl.pallas_call(functools.partial(finish_lag_kernel, far=far), in_specs=[W...  1.8 us
  transfers between devices with their start and end apart: 13, of which 7 were waited for; matrix products, arithmetic and copies ran while one was open for 0% of the time, Pallas kernels for 22%

profile of v5, /device:TPU:0, one launch (start us, length us, event | category | flops | bytes accessed | tf_op | source)
XLA Modules:
  0.0 63.9 jit_solution(9717746489135479552)
XLA Ops:
  0.6 14.7 %contacts_sent_lag.1 = (bf16[2560,1024]{1,0:T(8,128)(2,1)S(1)}, f32[8,1024]{1,0:T(8,128)S(1)}, s16[1040,512]{1,0:T(8,128)(2,1)S(1)}, f32[8,128]{1,0:T(8,128)S(1)}) custom-call(s32[16]{0:T(128)} %lengths_ref.1, s32[2,1024]{1,0:T(2,128)} %pairs_ref.1, bf16[3,2516,256]{2,1,0:T(8,128)(2,1)} %bitcast.1), custom_call_target="tpu_custom_call" | custom-call | tf_op jit(solution)/shard_map/contacts_sent_lag/pallas_call | solution.py:208
  15.4 0.5 collective-permute-start
  15.9 3.2 %kept_lag.1.kept_ref = f32[1024,512]{1,0:T(8,128)S(1)} custom-call(f32[8,128]{1,0:T(8,128)S(1)} %get-tuple-element.29.counts_ref, bf16[2560,1024]{1,0:T(8,128)(2,1)S(1)} %get-tuple-element.30.features_ref, f32[8,1024]{1,0:T(8,128)S(1)} %get-tuple-element.31.stats_ref.info_ref, s16[1040,512]{1,0:T(8,128)(2,1)S(1)} %get-tuple-element.32._), custom_call_target="tpu_custom_call" | custom-call | flops 17179869184 | bytes 16777216 | tf_op jit(solution)/shard_map/kept_lag/pallas_call | solution.py:266
  19.1 0.0 collective-permute-done.refs_0_
  19.1 1.5 %near_lag.1 = (f32[512,512]{1,0:T(8,128)S(1)}, s16[528,512]{1,0:T(8,128)(2,1)S(1)}, f32[8,1024]{1,0:T(8,128)S(1)}) custom-call(f32[8,128]{1,0:T(8,128)S(1)} %get-tuple-element.29.counts_ref, f32[1024,512]{1,0:T(8,128)S(1)} %kept_lag.1.kept_ref, f32[8,1024]{1,0:T(8,128)S(1)} %get-tuple-element.31.stats_ref.info_ref, ...), custom_call_target="tpu_custom_call" | custom-call | tf_op jit(solution)/shard_map/near_lag/pallas_call | solution.py:318
  20.5 2.6 %collective-permute-start.1 = (s16[528,512]{1,0:T(8,128)(2,1)S(1)}, s16[528,512]{1,0:T(8,128)(2,1)S(1)}, u32[]{:S(2)}, u32[]{:S(2)}) collective-permute-start(s16[528,512]{1,0:T(8,128)(2,1)S(1)} %get-tuple-element.34._), channel_id=1, source_target_pairs={{0,2},{2,0},{4,6},{6,4},{8,10},{10,8},{12,14},{14,12},{1,3},{3,1},... | collective-permute-start | bytes 1622024 | tf_op jit(solution)/shard_map/ppermute | solution.py:482
  23.1 5.6 %zero.1 = (s16[256,512]{1,0:T(8,128)(2,1)S(1)}, s16[256,512]{1,0:T(8,128)(2,1)S(1)}, s16[256,512]{1,0:T(8,128)(2,1)S(1)}, s16[256,512]{1,0:T(8,128)(2,1)S(1)}, f32[1024,512]{1,0:T(8,128)S(1)}) custom-call(f32[8,128]{1,0:T(8,128)S(1)} %get-tuple-element.29.counts_ref, bf16[2560,1024]{1,0:T(8,128)(2,1)S(1)} %get-tuple-element.30.features_ref, ...), custom_call_target="tpu_custom_call" | custom-call | flops 1048576 | bytes 1024 | tf_op jit(solution)/shard_map/zero/pallas_call | solution.py:266
  28.7 0.3 collective-permute-start.5
  29.0 0.3 collective-permute-start.6
  29.3 0.2 collective-permute-start.7
  29.5 0.3 collective-permute-start.8
  29.8 0.5 collective-permute-done.5.refs_0_
  30.3 0.4 collective-permute-done.6.refs_1_
  30.7 0.4 collective-permute-done.7.refs_2_
  31.1 0.4 collective-permute-done.8.refs_3_
  31.4 1.3 %near_zero.1 = (f32[512,512]{1,0:T(8,128)S(1)}, s16[512,512]{1,0:T(8,128)(2,1)S(1)}) custom-call(f32[8,128]{1,0:T(8,128)S(1)} %get-tuple-element.29.counts_ref, f32[1024,512]{1,0:T(8,128)S(1)} %get-tuple-element.44.kept_ref, f32[8,1024]{1,0:T(8,128)S(1)} %get-tuple-element.35.info_ref, s16[256,512]{1,0:T(8,128)(2,1)S(1)} %collective-permute-done.5.refs_0_, ...), custom_call_target="tpu_custom_call" | custom-call | tf_op jit(solution)/shard_map/near_zero/pallas_call | solution.py:318
  32.7 0.2 collective-permute-start.9
  32.9 3.3 %collective-permute-done.1.came_ref = s16[528,512]{1,0:T(8,128)(2,1)S(1)} collective-permute-done((s16[528,512]{1,0:T(8,128)(2,1)S(1)}, s16[528,512]{1,0:T(8,128)(2,1)S(1)}, u32[]{:S(2)}, u32[]{:S(2)}) %collective-permute-start.1) | collective-permute-done | bytes 540704 | tf_op jit(solution)/shard_map/ppermute | solution.py:482
  36.3 1.1 %far_lag.1 = (f32[128,512]{1,0:T(8,128)S(1)}, s16[144,512]{1,0:T(8,128)(2,1)S(1)}, s16[144,512]{1,0:T(8,128)(2,1)S(1)}, s16[144,512]{1,0:T(8,128)(2,1)S(1)}, f32[8,1024]{1,0:T(8,128)S(1)}) custom-call(f32[8,128]{1,0:T(8,128)S(1)} %get-tuple-element.29.counts_ref, f32[512,512]{1,0:T(8,128)S(1)} %get-tuple-element.33.keep_ref, ...), custom_call_target="tpu_custom_call" | custom-call | flops 17179869184 | bytes 16777216 | tf_op jit(solution)/shard_map/far_lag/pallas_call | solution.py:370
  37.4 3.1 %collective-permute-start.2 = (s16[144,512]{1,0:T(8,128)(2,1)S(1)}, s16[144,512]{1,0:T(8,128)(2,1)S(1)}, u32[]{:S(2)}, u32[]{:S(2)}) collective-permute-start(s16[144,512]{1,0:T(8,128)(2,1)S(1)} %get-tuple-element.38), channel_id=1, source_target_pairs={{0,8},{2,10},{4,12},{6,14},{8,0},{10,2},{12,4},{14,6},{1,9},{3,11}... | collective-permute-start | bytes 442376 | tf_op jit(solution)/shard_map/ppermute | solution.py:482
  40.5 1.4 %collective-permute-start.3 = (s16[144,512]{1,0:T(8,128)(2,1)S(1)}, s16[144,512]{1,0:T(8,128)(2,1)S(1)}, u32[]{:S(2)}, u32[]{:S(2)}) collective-permute-start(s16[144,512]{1,0:T(8,128)(2,1)S(1)} %get-tuple-element.39), channel_id=1, source_target_pairs={{0,12},{2,14},{4,8},{6,10},{8,4},{10,6},{12,0},{14,2},{1,13},{3,15... | collective-permute-start | bytes 442376 | tf_op jit(solution)/shard_map/ppermute | solution.py:482
  41.8 0.2 collective-permute-start.4
  42.0 5.3 %collective-permute-done.9.came_ref = s16[512,512]{1,0:T(8,128)(2,1)S(1)} collective-permute-done((s16[512,512]{1,0:T(8,128)(2,1)S(1)}, s16[512,512]{1,0:T(8,128)(2,1)S(1)}, u32[]{:S(2)}, u32[]{:S(2)}) %collective-permute-start.9) | collective-permute-done | bytes 524320 | tf_op jit(solution)/shard_map/ppermute | solution.py:482
  47.3 0.9 %far_zero.1 = (f32[128,512]{1,0:T(8,128)S(1)}, s16[128,512]{1,0:T(8,128)(2,1)S(1)}, s16[128,512]{1,0:T(8,128)(2,1)S(1)}, s16[128,512]{1,0:T(8,128)(2,1)S(1)}) custom-call(f32[8,128]{1,0:T(8,128)S(1)} %get-tuple-element.29.counts_ref, f32[512,512]{1,0:T(8,128)S(1)} %get-tuple-element.49.keep_ref, s16[512,512]{1,0:T(8,128)(2,1)S(1)} %collective-permute-done.9.came_ref, ...), custom_call_target="tpu_custom_call" | custom-call | flops 1048576 | bytes 1024 | tf_op jit(solution)/shard_map/far_zero/pallas_call | solution.py:370
  48.2 2.9 %collective-permute-start.10 = (s16[128,512]{1,0:T(8,128)(2,1)S(1)}, s16[128,512]{1,0:T(8,128)(2,1)S(1)}, u32[]{:S(2)}, u32[]{:S(2)}) collective-permute-start(s16[128,512]{1,0:T(8,128)(2,1)S(1)} %get-tuple-element.52), channel_id=1, source_target_pairs={{0,8},{2,10},{4,12},{6,14},{8,0},{10,2},{12,4},{14,6},{1,9},{3,11}... | collective-permute-start | bytes 393224 | tf_op jit(solution)/shard_map/ppermute | solution.py:482
  51.1 1.4 %collective-permute-start.11 = (s16[128,512]{1,0:T(8,128)(2,1)S(1)}, s16[128,512]{1,0:T(8,128)(2,1)S(1)}, u32[]{:S(2)}, u32[]{:S(2)}) collective-permute-start(s16[128,512]{1,0:T(8,128)(2,1)S(1)} %get-tuple-element.53), channel_id=1, source_target_pairs={{0,12},{2,14},{4,8},{6,10},{8,4},{10,6},{12,0},{14,2},{1,13},{3,15... | collective-permute-start | bytes 393224 | tf_op jit(solution)/shard_map/ppermute | solution.py:482
  52.5 0.0 collective-permute-done.2.refs_0_
  52.5 0.2 collective-permute-start.12
  52.7 0.0 collective-permute-done.3.refs_1_
  52.7 0.0 collective-permute-done.4.refs_2_
  52.7 1.8 %finish_lag.1 = (f32[128,512]{1,0:T(8,128)}, f32[128,512]{1,0:T(8,128)S(1)}, f32[16,1024]{1,0:T(8,128)S(1)}, f32[128,16]{1,0:T(8,128)S(1)}) custom-call(f32[8,128]{1,0:T(8,128)S(1)} %get-tuple-element.29.counts_ref, f32[8,1024]{1,0:T(8,128)S(1)} %get-tuple-element.36.info_ref, f32[128,512]{1,0:T(8,128)S(1)} %get-tuple-element.37.kept_ref, ...), custom_call_target="tpu_custom_call" | custom-call | tf_op jit(solution)/shard_map/finish_lag/pallas_call | solution.py:439
  54.5 8.4 %collective-permute-done.10.refs_0_ = s16[128,512]{1,0:T(8,128)(2,1)S(1)} collective-permute-done((s16[128,512]{1,0:T(8,128)(2,1)S(1)}, s16[128,512]{1,0:T(8,128)(2,1)S(1)}, u32[]{:S(2)}, u32[]{:S(2)}) %collective-permute-start.10) | collective-permute-done | bytes 131104 | tf_op jit(solution)/shard_map/ppermute | solution.py:482
  62.9 0.0 collective-permute-done.11.refs_1_
  62.9 0.0 collective-permute-done.12.refs_2_
  62.9 0.9 %finish_zero.1 = f32[128,512]{1,0:T(8,128)} custom-call(f32[8,128]{1,0:T(8,128)S(1)} %get-tuple-element.29.counts_ref, f32[16,1024]{1,0:T(8,128)S(1)} %get-tuple-element.41.rows_ref, f32[128,16]{1,0:T(8,128)S(1)} %get-tuple-element.42.left_ref, f32[128,512]{1,0:T(8,128)S(1)} %get-tuple-element.43.between_ref, f32[128,512]{1,0:T(8,128)S(1)} %get-tuple-element.51.kept_ref, ...), custom_call_target="tpu_custom_call" | custom-call | tf_op jit(solution)/shard_map/finish_zero/pallas_call | solution.py:458
Async XLA Ops:
  15.4 3.7 %collective-permute-start = (s16[1040,512]{1,0:T(8,128)(2,1)S(1)}, s16[1040,512]{1,0:T(8,128)(2,1)S(1)}, u32[]{:S(2)}, u32[]{:S(2)}) collective-permute-start(s16[1040,512]{1,0:T(8,128)(2,1)S(1)} %get-tuple-element.32._), channel_id=1, source_target_pairs={{0,1},{1,0},{2,3},{3,2},{4,5},{5,4},{6,7},{7,6},{8,9},{9,8},{10,11... | collective-permute-start | bytes 3194888 | tf_op jit(solution)/shard_map/ppermute | solution.py:482
  20.5 15.7 %collective-permute-start.1 = (s16[528,512]{1,0:T(8,128)(2,1)S(1)}, s16[528,512]{1,0:T(8,128)(2,1)S(1)}, u32[]{:S(2)}, u32[]{:S(2)}) collective-permute-start(s16[528,512]{1,0:T(8,128)(2,1)S(1)} %get-tuple-element.34._), channel_id=1, source_target_pairs={{0,2},{2,0},{4,6},{6,4},{8,10},{10,8},{12,14},{14,12},{1,3},{3,1},... | collective-permute-start | bytes 1622024 | tf_op jit(solution)/shard_map/ppermute | solution.py:482
  28.7 1.6 %collective-permute-start.5 = (s16[256,512]{1,0:T(8,128)(2,1)S(1)}, s16[256,512]{1,0:T(8,128)(2,1)S(1)}, u32[]{:S(2)}, u32[]{:S(2)}) collective-permute-start(s16[256,512]{1,0:T(8,128)(2,1)S(1)} %get-tuple-element.45), channel_id=1, source_target_pairs={{0,1},{1,0},{2,3},{3,2},{4,5},{5,4},{6,7},{7,6},{8,9},{9,8},{10,11... | collective-permute-start | bytes 786440 | tf_op jit(solution)/shard_map/ppermute | solution.py:482
  29.0 1.7 %collective-permute-start.6 = (s16[256,512]{1,0:T(8,128)(2,1)S(1)}, s16[256,512]{1,0:T(8,128)(2,1)S(1)}, u32[]{:S(2)}, u32[]{:S(2)}) collective-permute-start(s16[256,512]{1,0:T(8,128)(2,1)S(1)} %get-tuple-element.46), channel_id=1, source_target_pairs={{0,1},{1,0},{2,3},{3,2},{4,5},{5,4},{6,7},{7,6},{8,9},{9,8},{10,11... | collective-permute-start | bytes 786440 | tf_op jit(solution)/shard_map/ppermute | solution.py:482
  29.3 1.8 %collective-permute-start.7 = (s16[256,512]{1,0:T(8,128)(2,1)S(1)}, s16[256,512]{1,0:T(8,128)(2,1)S(1)}, u32[]{:S(2)}, u32[]{:S(2)}) collective-permute-start(s16[256,512]{1,0:T(8,128)(2,1)S(1)} %get-tuple-element.47), channel_id=1, source_target_pairs={{0,1},{1,0},{2,3},{3,2},{4,5},{5,4},{6,7},{7,6},{8,9},{9,8},{10,11... | collective-permute-start | bytes 786440 | tf_op jit(solution)/shard_map/ppermute | solution.py:482
  29.5 1.9 %collective-permute-start.8 = (s16[256,512]{1,0:T(8,128)(2,1)S(1)}, s16[256,512]{1,0:T(8,128)(2,1)S(1)}, u32[]{:S(2)}, u32[]{:S(2)}) collective-permute-start(s16[256,512]{1,0:T(8,128)(2,1)S(1)} %get-tuple-element.48), channel_id=1, source_target_pairs={{0,1},{1,0},{2,3},{3,2},{4,5},{5,4},{6,7},{7,6},{8,9},{9,8},{10,11... | collective-permute-start | bytes 786440 | tf_op jit(solution)/shard_map/ppermute | solution.py:482
  32.7 14.6 %collective-permute-start.9 = (s16[512,512]{1,0:T(8,128)(2,1)S(1)}, s16[512,512]{1,0:T(8,128)(2,1)S(1)}, u32[]{:S(2)}, u32[]{:S(2)}) collective-permute-start(s16[512,512]{1,0:T(8,128)(2,1)S(1)} %get-tuple-element.50), channel_id=1, source_target_pairs={{0,2},{2,0},{4,6},{6,4},{8,10},{10,8},{12,14},{14,12},{1,3},{3,1},... | collective-permute-start | bytes 1572872 | tf_op jit(solution)/shard_map/ppermute | solution.py:482
  37.4 15.1 %collective-permute-start.2 = (s16[144,512]{1,0:T(8,128)(2,1)S(1)}, s16[144,512]{1,0:T(8,128)(2,1)S(1)}, u32[]{:S(2)}, u32[]{:S(2)}) collective-permute-start(s16[144,512]{1,0:T(8,128)(2,1)S(1)} %get-tuple-element.38), channel_id=1, source_target_pairs={{0,8},{2,10},{4,12},{6,14},{8,0},{10,2},{12,4},{14,6},{1,9},{3,11}... | collective-permute-start | bytes 442376 | tf_op jit(solution)/shard_map/ppermute | solution.py:482
  40.5 12.2 %collective-permute-start.3 = (s16[144,512]{1,0:T(8,128)(2,1)S(1)}, s16[144,512]{1,0:T(8,128)(2,1)S(1)}, u32[]{:S(2)}, u32[]{:S(2)}) collective-permute-start(s16[144,512]{1,0:T(8,128)(2,1)S(1)} %get-tuple-element.39), channel_id=1, source_target_pairs={{0,12},{2,14},{4,8},{6,10},{8,4},{10,6},{12,0},{14,2},{1,13},{3,15... | collective-permute-start | bytes 442376 | tf_op jit(solution)/shard_map/ppermute | solution.py:482
  41.8 10.9 %collective-permute-start.4 = (s16[144,512]{1,0:T(8,128)(2,1)S(1)}, s16[144,512]{1,0:T(8,128)(2,1)S(1)}, u32[]{:S(2)}, u32[]{:S(2)}) collective-permute-start(s16[144,512]{1,0:T(8,128)(2,1)S(1)} %get-tuple-element.40), channel_id=1, source_target_pairs={{0,4},{2,6},{4,0},{6,2},{8,12},{10,14},{12,8},{14,10},{1,5},{3,7},... | collective-permute-start | bytes 442376 | tf_op jit(solution)/shard_map/ppermute | solution.py:482
  48.2 14.7 %collective-permute-start.10 = (s16[128,512]{1,0:T(8,128)(2,1)S(1)}, s16[128,512]{1,0:T(8,128)(2,1)S(1)}, u32[]{:S(2)}, u32[]{:S(2)}) collective-permute-start(s16[128,512]{1,0:T(8,128)(2,1)S(1)} %get-tuple-element.52), channel_id=1, source_target_pairs={{0,8},{2,10},{4,12},{6,14},{8,0},{10,2},{12,4},{14,6},{1,9},{3,11}... | collective-permute-start | bytes 393224 | tf_op jit(solution)/shard_map/ppermute | solution.py:482
  51.1 11.8 %collective-permute-start.11 = (s16[128,512]{1,0:T(8,128)(2,1)S(1)}, s16[128,512]{1,0:T(8,128)(2,1)S(1)}, u32[]{:S(2)}, u32[]{:S(2)}) collective-permute-start(s16[128,512]{1,0:T(8,128)(2,1)S(1)} %get-tuple-element.53), channel_id=1, source_target_pairs={{0,12},{2,14},{4,8},{6,10},{8,4},{10,6},{12,0},{14,2},{1,13},{3,15... | collective-permute-start | bytes 393224 | tf_op jit(solution)/shard_map/ppermute | solution.py:482
  52.5 10.5 %collective-permute-start.12 = (s16[128,512]{1,0:T(8,128)(2,1)S(1)}, s16[128,512]{1,0:T(8,128)(2,1)S(1)}, u32[]{:S(2)}, u32[]{:S(2)}) collective-permute-start(s16[128,512]{1,0:T(8,128)(2,1)S(1)} %get-tuple-element.54), channel_id=1, source_target_pairs={{0,4},{2,6},{4,0},{6,2},{8,12},{10,14},{12,8},{14,10},{1,5},{3,7},... | collective-permute-start | bytes 393224 | tf_op jit(solution)/shard_map/ppermute | solution.py:482

commit v6 on v5

--- a/solution.py
+++ b/solution.py
@@ -251,13 +251,101 @@
         out_refs[start // part][first : first + FEATURE_TILE, :] = gram
 
 
-def kept_lag_kernel(counts_ref, features_ref, stats_ref, _, kept_ref, right_ref):
-    gram_half(counts_ref, features_ref, stats_ref, [kept_ref], right_ref, True, True)
-
-
-def zero_kernel(counts_ref, features_ref, stats_ref, _, *refs):
-    sent_refs, kept_ref, right_ref = refs[:-2], refs[-2], refs[-1]
-    gram_half(counts_ref, features_ref, stats_ref, sent_refs, right_ref, False, False)
+def chosen(own, even, odd):
+    near = lax.axis_index("dp") % 2
+    return jnp.where(near == 0, even, odd) if own else jnp.where(near == 0, odd, even)
+
+
+def chosen_block(own, ref, index, block):
+    first = 2 * index * block
+    return chosen(own, ref[first : first + block, :], ref[first + block : first + 2 * block, :])
+
+
+def kept_part(counts_ref, features_ref, stats_ref, right_ref, kept_ref, own, block):
+    depth, half = right_ref.shape
+    columns = side_columns(half, True)
+    live = live_of(counts_ref, [0])
+    left_total = jnp.transpose(stats_ref[...])[:, 0:1]
+    right_mean = stats_ref[1:2, columns] / live
+    alive = lax.broadcasted_iota(jnp.int32, (depth, 1), 0).astype(jnp.float32) < live
+    for start in range(0, half, FEATURE_TILE):
+        left, totals = [], []
+        for first in range(2 * start, 2 * (start + FEATURE_TILE), 2 * block):
+            even, odd = slice(first, first + block), slice(first + block, first + 2 * block)
+            left.append(chosen(own, features_ref[0:depth, even], features_ref[0:depth, odd]))
+            totals.append(chosen(own, left_total[even], left_total[odd]))
+        left = jnp.where(alive, jnp.concatenate(left, axis=1), 0.0).astype(jnp.bfloat16)
+        gram = lax.dot_general(
+            left, right_ref[...], (((0,), (0,)), ((), ())), preferred_element_type=jnp.float32
+        )
+        total = jnp.concatenate(totals, axis=0)
+        kept_ref[start : start + FEATURE_TILE, :] = gram - total * right_mean
+
+
+def other_lag_kernel(counts_ref, features_ref, stats_ref, _, kept_ref, right_ref, *, block):
+    load_right(features_ref, right_ref, True, True)
+    kept_part(counts_ref, features_ref, stats_ref, right_ref, kept_ref, False, block)
+
+
+def own_lag_kernel(counts_ref, features_ref, stats_ref, right_ref, _, kept_ref, *, block):
+    kept_part(counts_ref, features_ref, stats_ref, right_ref, kept_ref, True, block)
+
+
+def part_call(body, operands, after, outs, block, estimate, name):
+    return pl.pallas_call(
+        functools.partial(body, block=block),
+        in_specs=[WHOLE] * len(operands) + [pl.BlockSpec(memory_space=pl.ANY)] * len(after),
+        out_specs=[WHOLE] * len(outs),
+        out_shape=outs,
+        compiler_params=params(),
+        cost_estimate=pl.CostEstimate(flops=estimate, bytes_accessed=estimate // 1024, transcendentals=0),
+        name=name,
+    )(*operands, *after)
+
+
+def near_other_kernel(counts_ref, kept_ref, stats_ref, came_ref, sent_ref, info_ref, *, block):
+    half = kept_ref.shape[0]
+    feats = 2 * half
+    columns = side_columns(half, True)
+    count, peer_count = live_of(counts_ref, [0]), live_of(counts_ref, [1])
+    sums = (stats_ref[0:1, :], stats_ref[1:2, :])
+    pool(info_ref, sums, stats_ref[2:3, :], count, came_ref[feats : feats + TAIL, :], peer_count)
+    sent_ref[half : half + TAIL, :] = pooled_code(info_ref)
+    weight = count * peer_count / (count + peer_count)
+    left = jnp.transpose(info_ref[...])
+    came_right = info_ref[0:1, columns] * (1.0 / LEVELS**2)
+    step_right = info_ref[2:3, columns] * weight
+    sent_right = lax.rsqrt(info_ref[3:4, columns])
+    for index in range(half // block):
+        rows = slice(index * block, (index + 1) * block)
+        mine = chosen_block(False, left, index, block)
+        came = from_levels(chosen_block(False, came_ref, index, block))
+        total = kept_ref[rows, :] + came * (mine[:, 0:1] * came_right) + mine[:, 1:2] * step_right
+        sent_ref[rows, :] = to_levels(total * (lax.rsqrt(mine[:, 3:4]) * sent_right))
+
+
+def near_own_kernel(counts_ref, kept_ref, info_ref, came_ref, keep_ref, *, block):
+    half = kept_ref.shape[0]
+    columns = side_columns(half, True)
+    count, peer_count = live_of(counts_ref, [0]), live_of(counts_ref, [1])
+    weight = count * peer_count / (count + peer_count)
+    left = jnp.transpose(info_ref[...])
+    came_right = info_ref[0:1, columns] * (1.0 / LEVELS**2)
+    step_right = info_ref[2:3, columns] * weight
+    for index in range(half // block):
+        rows = slice(index * block, (index + 1) * block)
+        mine = chosen_block(True, left, index, block)
+        came = from_levels(chosen_block(True, came_ref, index, block))
+        keep_ref[rows, :] = (
+            kept_ref[rows, :] + came * (mine[:, 0:1] * came_right) + mine[:, 1:2] * step_right
+        )
+
+
+def sent_zero_kernel(counts_ref, features_ref, stats_ref, _, *refs):
+    gram_half(counts_ref, features_ref, stats_ref, refs[:-1], refs[-1], False, False)
+
+
+def kept_zero_kernel(counts_ref, features_ref, stats_ref, _, kept_ref, right_ref):
     gram_half(counts_ref, features_ref, stats_ref, [kept_ref], right_ref, True, False)
 
 
@@ -276,53 +364,27 @@
     )(*operands, *after)
 
 
-def near_kernel(counts_ref, kept_ref, info_ref, *refs, lagged, block, parts):
-    came_refs, keep_ref, sent_ref = refs[:parts], refs[parts], refs[parts + 1]
-    near = lax.axis_index("dp") % 2
+def near_zero_kernel(counts_ref, kept_ref, info_ref, *refs, own, block):
+    came_refs, out_ref = refs[:-1], refs[-1]
     feats, half = kept_ref.shape
-    part = feats // parts
+    part = feats // len(came_refs)
     columns = side_columns(half, True)
     count, peer_count = live_of(counts_ref, [0]), live_of(counts_ref, [1])
-    if lagged:
-        stats_ref, info_ref = info_ref, refs[-1]
-        sums = (stats_ref[0:1, :], stats_ref[1:2, :])
-        tail = came_refs[0][feats : feats + TAIL, :]
-        pool(info_ref, sums, stats_ref[2:3, :], count, tail, peer_count)
-        sent_ref[half : half + TAIL, :] = pooled_code(info_ref)
     weight = count * peer_count / (count + peer_count)
     left = jnp.transpose(info_ref[...])
     came_right = info_ref[0:1, columns] * (1.0 / LEVELS**2)
-    step_right = info_ref[2 if lagged else 1 : 3 if lagged else 2, columns] * weight
+    step_right = info_ref[1:2, columns] * weight
     sent_right = lax.rsqrt(info_ref[3:4, columns])
-    for start in range(0, feats, 2 * block):
-        totals = []
-        for rows in (slice(start, start + block), slice(start + block, start + 2 * block)):
-            first = rows.start % part
-            came = from_levels(came_refs[rows.start // part][first : first + block, :])
-            total = kept_ref[rows, :] + came * (left[rows, 0:1] * came_right)
-            totals.append(total + left[rows, 1:2] * step_right)
-        target = slice(start // 2, start // 2 + block)
-        keep_ref[target, :] = jnp.where(near == 0, totals[0], totals[1])
-        other = jnp.where(near == 0, totals[1], totals[0])
-        even = left[start : start + block, 3:4]
-        odd = left[start + block : start + 2 * block, 3:4]
-        spread = jnp.where(near == 0, odd, even)
-        sent_ref[target, :] = to_levels(other * (lax.rsqrt(spread) * sent_right))
-
-
-def near_call(counts, kept, info, came, block, lagged):
-    feats, half = kept.shape
-    outs = [shape((half, half)), shape((half + (TAIL if lagged else 0), half), jnp.int16)]
-    if lagged:
-        outs.append(shape((8, feats)))
-    return pl.pallas_call(
-        functools.partial(near_kernel, lagged=lagged, block=block, parts=len(came)),
-        in_specs=[WHOLE] * (3 + len(came)),
-        out_specs=[WHOLE] * len(outs),
-        out_shape=outs,
-        compiler_params=params(),
-        name="near_lag" if lagged else "near_zero",
-    )(counts, kept, info, *came)
+    for index in range(half // block):
+        mine = chosen_block(own, left, index, block)
+        kept = chosen_block(own, kept_ref, index, block)
+        came_ref, inside = came_refs[2 * index * block // part], 2 * index * block % part
+        even, odd = came_ref[inside : inside + block, :], came_ref[inside + block : inside + 2 * block, :]
+        came = from_levels(chosen(own, even, odd))
+        total = kept + came * (mine[:, 0:1] * came_right) + mine[:, 1:2] * step_right
+        if not own:
+            total = to_levels(total * (lax.rsqrt(mine[:, 3:4]) * sent_right))
+        out_ref[index * block : (index + 1) * block, :] = total
 
 
 def far_kernel(counts_ref, keep_ref, came_ref, info_ref, *refs, lagged, block, far):
@@ -489,19 +551,51 @@
     half = feats // 2
     kept_shape = shape((feats, half))
     came_lag = swap(sent_lag, "tile", 1)
-    (kept_lag,) = gram_call(kept_lag_kernel, common, [sent_lag], [kept_shape], depth, LONG)
-    keep_lag, sent_lag, chip = near_call(counts, kept_lag, stats, [came_lag], block, True)
-    came_lag = swap(sent_lag, "dp", 1)
-    *sent_zero, kept_zero = gram_call(
-        zero_kernel,
+    square = shape((half, half))
+    kept_other, right = part_call(
+        other_lag_kernel,
         common,
         [sent_lag],
-        [shape((feats // SPLIT, half), jnp.int16)] * SPLIT + [kept_shape],
-        depth,
+        [square, shape((depth, half), jnp.bfloat16)],
+        block,
+        LONG,
+        "kept_lag_other",
+    )
+    sent_shape = shape((half + TAIL, half), jnp.int16)
+    sent_lag, chip = part_call(
+        near_other_kernel,
+        [counts, kept_other, stats, came_lag],
+        [],
+        [sent_shape, shape((8, feats))],
+        block,
         SHORT,
-    )
+        "near_lag_other",
+    )
+    own_came = came_lag
+    came_lag = swap(sent_lag, "dp", 1)
+    (kept_own,) = part_call(
+        own_lag_kernel, common + [right], [sent_lag], [square], block, SHORT, "kept_lag_own"
+    )
+    (keep_lag,) = part_call(
+        near_own_kernel, [counts, kept_own, chip, own_came], [], [square], block, SHORT, "near_lag_own"
+    )
+    part_shape = shape((feats // SPLIT, half), jnp.int16)
+    sent_zero = gram_call(sent_zero_kernel, common, [keep_lag], [part_shape] * SPLIT, depth, SHORT)
+    (kept_zero,) = gram_call(kept_zero_kernel, common, sent_zero[:1], [kept_shape], depth, SHORT)
     came_zero = [swap(part, "tile", 1) for part in sent_zero]
-    keep_zero, sent_zero = near_call(counts, kept_zero, chip, came_zero, block, False)
+    near_zero = [counts, kept_zero, chip] + came_zero
+    (sent_zero,) = part_call(
+        functools.partial(near_zero_kernel, own=False),
+        near_zero,
+        [],
+        [shape((half, half), jnp.int16)],
+        block,
+        SHORT,
+        "near_zero_other",
+    )
+    (keep_zero,) = part_call(
+        functools.partial(near_zero_kernel, own=True), near_zero, [], [square], block, SHORT, "near_zero_own"
+    )
     came_zero = swap(sent_zero, "dp", 1)
 
     kept_lag, *sent_lag, pair = far_call(counts, keep_lag, came_lag, chip, block, True)

time: 64.4 us -> 63 us (0.978)
  waiting for transfers between devices: 18.7 us -> 14.7 us
  Pallas kernels: 31 us -> 34 us
    pallas_call x2 -> x6, Pallas kernels: 2.71 us -> 7.82 us  [part_call(): pl.pallas_call(functools.partial(body, block=block), in_specs=[WHOLE] * l...]
    ppermute x13, waiting for transfers between devices: 18.7 us -> 14.7 us  [swap(): return lax.ppermute(array, axis, exclusive(lax.axis_size(axis), distance))]
    pallas_call x2, Pallas kernels: 8.74 us -> 6.43 us  [gram_call(): pl.pallas_call(body, in_specs=[WHOLE] * len(operands) + [pl.BlockSpec(mem...]
  transfers between devices with their start and end apart: 13 -> 13, of which waited for: 7 -> 4; matrix products, arithmetic and copies ran while one was open for 0% -> 0% of each run, Pallas kernels for 22% -> 28%
where the time goes in v6:
time: 63 us; the launch traced here: 62.7 us
  Pallas kernels  34 us (54%)
  waiting for transfers between devices  14.7 us (23%)
  starting transfers between devices  13.3 us (21%)
  between operations  0.76 us (1%)
    pallas_call x1, Pallas kernels, contacts_call(): pl.pallas_call(contacts_kernel, grid=(rows // FRAME_TILE,), in_specs=[SCA...  14.7 us
    ppermute x13, waiting for transfers between devices, swap(): return lax.ppermute(array, axis, exclusive(lax.axis_size(axis), distance))  14.7 us
    ppermute x13, starting transfers between devices, swap(): return lax.ppermute(array, axis, exclusive(lax.axis_size(axis), distance))  13.3 us
    pallas_call x6, Pallas kernels, part_call(): pl.pallas_call(functools.partial(body, block=block), in_specs=[WHOLE] * l...  7.82 us
    pallas_call x2, Pallas kernels, gram_call(): pl.pallas_call(body, in_specs=[WHOLE] * len(operands) + [pl.BlockSpec(mem...  6.43 us
    pallas_call x2, Pallas kernels, far_call(): pl.pallas_call(functools.partial(far_kernel, lagged=lagged, block=block,...  2.27 us
    pallas_call x1, Pallas kernels, finish_lag(): pl.pallas_call(functools.partial(finish_lag_kernel, far=far), in_specs=[W...  1.8 us
  transfers between devices with their start and end apart: 13, of which 4 were waited for; matrix products, arithmetic and copies ran while one was open for 0% of the time, Pallas kernels for 28%

profile of v6, /device:TPU:0, one launch (start us, length us, event | category | flops | bytes accessed | tf_op | source)
XLA Modules:
  0.0 62.7 jit_solution(4696673614269434068)
XLA Ops:
  0.6 14.7 %contacts_sent_lag.1 = (bf16[2560,1024]{1,0:T(8,128)(2,1)S(1)}, f32[8,1024]{1,0:T(8,128)S(1)}, s16[1040,512]{1,0:T(8,128)(2,1)S(1)}, f32[8,128]{1,0:T(8,128)S(1)}) custom-call(s32[16]{0:T(128)} %lengths_ref.1, s32[2,1024]{1,0:T(2,128)} %pairs_ref.1, bf16[3,2516,256]{2,1,0:T(8,128)(2,1)} %bitcast.1), custom_call_target="tpu_custom_call" | custom-call | tf_op jit(solution)/shard_map/contacts_sent_lag/pallas_call | solution.py:208
  15.4 0.5 collective-permute-start
  15.9 2.4 %kept_lag_other.1 = (f32[512,512]{1,0:T(8,128)S(1)}, bf16[2048,512]{1,0:T(8,128)(2,1)S(1)}) custom-call(f32[8,128]{1,0:T(8,128)S(1)} %get-tuple-element.27.counts_ref, bf16[2560,1024]{1,0:T(8,128)(2,1)S(1)} %get-tuple-element.28.features_ref, f32[8,1024]{1,0:T(8,128)S(1)} %get-tuple-element.29.stats_ref, s16[1040,512]{1,0:T(8,128)(2,1)S(1)} %get-tuple-element.30._), custom_call_target="tpu_custom_call" | custom-call | flops 17179869184 | bytes 16777216 | tf_op jit(solution)/shard_map/kept_lag_other/pallas_call | solution.py:295
  18.2 0.0 collective-permute-done.came_ref
  18.3 1.0 %near_lag_other.1 = (s16[528,512]{1,0:T(8,128)(2,1)S(1)}, f32[8,1024]{1,0:T(8,128)S(1)}) custom-call(f32[8,128]{1,0:T(8,128)S(1)} %get-tuple-element.27.counts_ref, f32[512,512]{1,0:T(8,128)S(1)} %get-tuple-element.32.kept_ref, f32[8,1024]{1,0:T(8,128)S(1)} %get-tuple-element.29.stats_ref, s16[1040,512]{1,0:T(8,128)(2,1)S(1)} %collective-permute-done.came_ref), custom_call_target="tpu_custom_call" | custom-call | flops 1048576 | bytes 1024 | tf_op jit(solution)/shard_map/near_lag_other/pallas_call | solution.py:295
  19.3 2.9 %collective-permute-start.1 = (s16[528,512]{1,0:T(8,128)(2,1)S(1)}, s16[528,512]{1,0:T(8,128)(2,1)S(1)}, u32[]{:S(2)}, u32[]{:S(2)}) collective-permute-start(s16[528,512]{1,0:T(8,128)(2,1)S(1)} %get-tuple-element.33._), channel_id=1, source_target_pairs={{0,2},{2,0},{4,6},{6,4},{8,10},{10,8},{12,14},{14,12},{1,3},{3,1},... | collective-permute-start | bytes 1622024 | tf_op jit(solution)/shard_map/ppermute | solution.py:544
  22.2 2.3 %kept_lag_own.1.kept_ref = f32[512,512]{1,0:T(8,128)S(1)} custom-call(f32[8,128]{1,0:T(8,128)S(1)} %get-tuple-element.27.counts_ref, bf16[2560,1024]{1,0:T(8,128)(2,1)S(1)} %get-tuple-element.28.features_ref, f32[8,1024]{1,0:T(8,128)S(1)} %get-tuple-element.29.stats_ref, bf16[2048,512]{1,0:T(8,128)(2,1)S(1)} %get-tuple-element.31.right_ref, ...), custom_call_target="tpu_custom_call" | custom-call | flops 1048576 | bytes 1024 | tf_op jit(solution)/shard_map/kept_lag_own/pallas_call | solution.py:295
  24.5 0.6 near_lag_own.1.keep_ref._
  25.1 3.3 %sent_zero.1 = (s16[256,512]{1,0:T(8,128)(2,1)S(1)}, s16[256,512]{1,0:T(8,128)(2,1)S(1)}, s16[256,512]{1,0:T(8,128)(2,1)S(1)}, s16[256,512]{1,0:T(8,128)(2,1)S(1)}) custom-call(f32[8,128]{1,0:T(8,128)S(1)} %get-tuple-element.27.counts_ref, bf16[2560,1024]{1,0:T(8,128)(2,1)S(1)} %get-tuple-element.28.features_ref, f32[8,1024]{1,0:T(8,128)S(1)} %get-tuple-element.29.stats_ref, ...), custom_call_target="tpu_custom_call" | custom-call | flops 1048576 | bytes 1024 | tf_op jit(solution)/shard_map/sent_zero/pallas_call | solution.py:354
  28.4 0.1 collective-permute-start.6
  28.5 0.5 collective-permute-start.7
  29.0 0.1 collective-permute-start.8
  29.1 0.4 collective-permute-start.5
  29.5 3.1 %kept_zero.1.kept_ref = f32[1024,512]{1,0:T(8,128)S(1)} custom-call(f32[8,128]{1,0:T(8,128)S(1)} %get-tuple-element.27.counts_ref, bf16[2560,1024]{1,0:T(8,128)(2,1)S(1)} %get-tuple-element.28.features_ref, f32[8,1024]{1,0:T(8,128)S(1)} %get-tuple-element.29.stats_ref, s16[256,512]{1,0:T(8,128)(2,1)S(1)} %get-tuple-element.43._), custom_call_target="tpu_custom_call" | custom-call | flops 1048576 | bytes 1024 | tf_op jit(solution)/shard_map/kept_zero/pallas_call | solution.py:354
  32.6 0.0 collective-permute-done.6.refs_1_
  32.7 0.0 collective-permute-done.7.refs_2_
  32.7 0.0 collective-permute-done.8.refs_3_
  32.7 0.0 collective-permute-done.5.refs_0_
  32.7 0.9 %near_zero_other.1 = s16[512,512]{1,0:T(8,128)(2,1)S(1)} custom-call(f32[8,128]{1,0:T(8,128)S(1)} %get-tuple-element.27.counts_ref, f32[1024,512]{1,0:T(8,128)S(1)} %kept_zero.1.kept_ref, f32[8,1024]{1,0:T(8,128)S(1)} %get-tuple-element.34.info_ref, s16[256,512]{1,0:T(8,128)(2,1)S(1)} %collective-permute-done.5.refs_0_, ...), custom_call_target="tpu_custom_call" | custom-call | flops 1048576 | bytes 1024 | tf_op jit(solution)/shard_map/near_zero_other/pallas_call | solution.py:295
  33.6 0.1 collective-permute-start.9
  33.7 1.1 %collective-permute-done.1.came_ref = s16[528,512]{1,0:T(8,128)(2,1)S(1)} collective-permute-done((s16[528,512]{1,0:T(8,128)(2,1)S(1)}, s16[528,512]{1,0:T(8,128)(2,1)S(1)}, u32[]{:S(2)}, u32[]{:S(2)}) %collective-permute-start.1) | collective-permute-done | bytes 540704 | tf_op jit(solution)/shard_map/ppermute | solution.py:544
  34.8 1.3 %far_lag.1 = (f32[128,512]{1,0:T(8,128)S(1)}, s16[144,512]{1,0:T(8,128)(2,1)S(1)}, s16[144,512]{1,0:T(8,128)(2,1)S(1)}, s16[144,512]{1,0:T(8,128)(2,1)S(1)}, f32[8,1024]{1,0:T(8,128)S(1)}) custom-call(f32[8,128]{1,0:T(8,128)S(1)} %get-tuple-element.27.counts_ref, f32[512,512]{1,0:T(8,128)S(1)} %near_lag_own.1.keep_ref._, ...), custom_call_target="tpu_custom_call" | custom-call | flops 17179869184 | bytes 16777216 | tf_op jit(solution)/shard_map/far_lag/pallas_call | solution.py:432
  36.2 2.9 %collective-permute-start.2 = (s16[144,512]{1,0:T(8,128)(2,1)S(1)}, s16[144,512]{1,0:T(8,128)(2,1)S(1)}, u32[]{:S(2)}, u32[]{:S(2)}) collective-permute-start(s16[144,512]{1,0:T(8,128)(2,1)S(1)} %get-tuple-element.37), channel_id=1, source_target_pairs={{0,8},{2,10},{4,12},{6,14},{8,0},{10,2},{12,4},{14,6},{1,9},{3,11}... | collective-permute-start | bytes 442376 | tf_op jit(solution)/shard_map/ppermute | solution.py:544
  39.1 1.3 %collective-permute-start.3 = (s16[144,512]{1,0:T(8,128)(2,1)S(1)}, s16[144,512]{1,0:T(8,128)(2,1)S(1)}, u32[]{:S(2)}, u32[]{:S(2)}) collective-permute-start(s16[144,512]{1,0:T(8,128)(2,1)S(1)} %get-tuple-element.38), channel_id=1, source_target_pairs={{0,12},{2,14},{4,8},{6,10},{8,4},{10,6},{12,0},{14,2},{1,13},{3,15... | collective-permute-start | bytes 442376 | tf_op jit(solution)/shard_map/ppermute | solution.py:544
  40.4 0.2 collective-permute-start.4
  40.6 0.6 %near_zero_own.1.keep_ref = f32[512,512]{1,0:T(8,128)S(1)} custom-call(f32[8,128]{1,0:T(8,128)S(1)} %get-tuple-element.27.counts_ref, f32[1024,512]{1,0:T(8,128)S(1)} %kept_zero.1.kept_ref, f32[8,1024]{1,0:T(8,128)S(1)} %get-tuple-element.34.info_ref, s16[256,512]{1,0:T(8,128)(2,1)S(1)} %collective-permute-done.5.refs_0_, ...), custom_call_target="tpu_custom_call" | custom-call | flops 1048576 | bytes 1024 | tf_op jit(solution)/shard_map/near_zero_own/pallas_call | solution.py:295
  41.3 6.3 %collective-permute-done.9.came_ref = s16[512,512]{1,0:T(8,128)(2,1)S(1)} collective-permute-done((s16[512,512]{1,0:T(8,128)(2,1)S(1)}, s16[512,512]{1,0:T(8,128)(2,1)S(1)}, u32[]{:S(2)}, u32[]{:S(2)}) %collective-permute-start.9) | collective-permute-done | bytes 524320 | tf_op jit(solution)/shard_map/ppermute | solution.py:544
  47.6 0.9 %far_zero.1 = (f32[128,512]{1,0:T(8,128)S(1)}, s16[128,512]{1,0:T(8,128)(2,1)S(1)}, s16[128,512]{1,0:T(8,128)(2,1)S(1)}, s16[128,512]{1,0:T(8,128)(2,1)S(1)}) custom-call(f32[8,128]{1,0:T(8,128)S(1)} %get-tuple-element.27.counts_ref, f32[512,512]{1,0:T(8,128)S(1)} %near_zero_own.1.keep_ref, s16[512,512]{1,0:T(8,128)(2,1)S(1)} %collective-permute-done.9.came_ref, ...), custom_call_target="tpu_custom_call" | custom-call | flops 1048576 | bytes 1024 | tf_op jit(solution)/shard_map/far_zero/pallas_call | solution.py:432
  48.6 2.7 %collective-permute-start.10 = (s16[128,512]{1,0:T(8,128)(2,1)S(1)}, s16[128,512]{1,0:T(8,128)(2,1)S(1)}, u32[]{:S(2)}, u32[]{:S(2)}) collective-permute-start(s16[128,512]{1,0:T(8,128)(2,1)S(1)} %get-tuple-element.48), channel_id=1, source_target_pairs={{0,8},{2,10},{4,12},{6,14},{8,0},{10,2},{12,4},{14,6},{1,9},{3,11}... | collective-permute-start | bytes 393224 | tf_op jit(solution)/shard_map/ppermute | solution.py:544
  51.2 1.3 %collective-permute-start.11 = (s16[128,512]{1,0:T(8,128)(2,1)S(1)}, s16[128,512]{1,0:T(8,128)(2,1)S(1)}, u32[]{:S(2)}, u32[]{:S(2)}) collective-permute-start(s16[128,512]{1,0:T(8,128)(2,1)S(1)} %get-tuple-element.49), channel_id=1, source_target_pairs={{0,12},{2,14},{4,8},{6,10},{8,4},{10,6},{12,0},{14,2},{1,13},{3,15... | collective-permute-start | bytes 393224 | tf_op jit(solution)/shard_map/ppermute | solution.py:544
  52.6 0.0 collective-permute-done.2.refs_0_
  52.6 0.2 collective-permute-start.12
  52.8 0.0 collective-permute-done.3.refs_1_
  52.8 0.0 collective-permute-done.4.refs_2_
  52.8 1.8 %finish_lag.1 = (f32[128,512]{1,0:T(8,128)}, f32[128,512]{1,0:T(8,128)S(1)}, f32[16,1024]{1,0:T(8,128)S(1)}, f32[128,16]{1,0:T(8,128)S(1)}) custom-call(f32[8,128]{1,0:T(8,128)S(1)} %get-tuple-element.27.counts_ref, f32[8,1024]{1,0:T(8,128)S(1)} %get-tuple-element.35.info_ref, f32[128,512]{1,0:T(8,128)S(1)} %get-tuple-element.36.kept_ref, ...), custom_call_target="tpu_custom_call" | custom-call | tf_op jit(solution)/shard_map/finish_lag/pallas_call | solution.py:501
  54.6 6.5 %collective-permute-done.10.refs_0_ = s16[128,512]{1,0:T(8,128)(2,1)S(1)} collective-permute-done((s16[128,512]{1,0:T(8,128)(2,1)S(1)}, s16[128,512]{1,0:T(8,128)(2,1)S(1)}, u32[]{:S(2)}, u32[]{:S(2)}) %collective-permute-start.10) | collective-permute-done | bytes 131104 | tf_op jit(solution)/shard_map/ppermute | solution.py:544
  61.1 0.0 collective-permute-done.11.refs_1_
  61.1 0.7 %collective-permute-done.12.refs_2_ = s16[128,512]{1,0:T(8,128)(2,1)S(1)} collective-permute-done((s16[128,512]{1,0:T(8,128)(2,1)S(1)}, s16[128,512]{1,0:T(8,128)(2,1)S(1)}, u32[]{:S(2)}, u32[]{:S(2)}) %collective-permute-start.12) | collective-permute-done | bytes 131104 | tf_op jit(solution)/shard_map/ppermute | solution.py:544
  61.8 0.9 %finish_zero.1 = f32[128,512]{1,0:T(8,128)} custom-call(f32[8,128]{1,0:T(8,128)S(1)} %get-tuple-element.27.counts_ref, f32[16,1024]{1,0:T(8,128)S(1)} %get-tuple-element.40.rows_ref, f32[128,16]{1,0:T(8,128)S(1)} %get-tuple-element.41.left_ref, f32[128,512]{1,0:T(8,128)S(1)} %get-tuple-element.42.between_ref, f32[128,512]{1,0:T(8,128)S(1)} %get-tuple-element.47.kept_ref, ...), custom_call_target="tpu_custom_call" | custom-call | tf_op jit(solution)/shard_map/finish_zero/pallas_call | solution.py:520
Async XLA Ops:
  15.4 2.9 %collective-permute-start = (s16[1040,512]{1,0:T(8,128)(2,1)S(1)}, s16[1040,512]{1,0:T(8,128)(2,1)S(1)}, u32[]{:S(2)}, u32[]{:S(2)}) collective-permute-start(s16[1040,512]{1,0:T(8,128)(2,1)S(1)} %get-tuple-element.30._), channel_id=1, source_target_pairs={{0,1},{1,0},{2,3},{3,2},{4,5},{5,4},{6,7},{7,6},{8,9},{9,8},{10,11... | collective-permute-start | bytes 3194888 | tf_op jit(solution)/shard_map/ppermute | solution.py:544
  19.3 15.5 %collective-permute-start.1 = (s16[528,512]{1,0:T(8,128)(2,1)S(1)}, s16[528,512]{1,0:T(8,128)(2,1)S(1)}, u32[]{:S(2)}, u32[]{:S(2)}) collective-permute-start(s16[528,512]{1,0:T(8,128)(2,1)S(1)} %get-tuple-element.33._), channel_id=1, source_target_pairs={{0,2},{2,0},{4,6},{6,4},{8,10},{10,8},{12,14},{14,12},{1,3},{3,1},... | collective-permute-start | bytes 1622024 | tf_op jit(solution)/shard_map/ppermute | solution.py:544
  28.4 4.2 %collective-permute-start.6 = (s16[256,512]{1,0:T(8,128)(2,1)S(1)}, s16[256,512]{1,0:T(8,128)(2,1)S(1)}, u32[]{:S(2)}, u32[]{:S(2)}) collective-permute-start(s16[256,512]{1,0:T(8,128)(2,1)S(1)} %get-tuple-element.44), channel_id=1, source_target_pairs={{0,1},{1,0},{2,3},{3,2},{4,5},{5,4},{6,7},{7,6},{8,9},{9,8},{10,11... | collective-permute-start | bytes 786440 | tf_op jit(solution)/shard_map/ppermute | solution.py:544
  28.5 4.2 %collective-permute-start.7 = (s16[256,512]{1,0:T(8,128)(2,1)S(1)}, s16[256,512]{1,0:T(8,128)(2,1)S(1)}, u32[]{:S(2)}, u32[]{:S(2)}) collective-permute-start(s16[256,512]{1,0:T(8,128)(2,1)S(1)} %get-tuple-element.45), channel_id=1, source_target_pairs={{0,1},{1,0},{2,3},{3,2},{4,5},{5,4},{6,7},{7,6},{8,9},{9,8},{10,11... | collective-permute-start | bytes 786440 | tf_op jit(solution)/shard_map/ppermute | solution.py:544
  29.0 3.7 %collective-permute-start.8 = (s16[256,512]{1,0:T(8,128)(2,1)S(1)}, s16[256,512]{1,0:T(8,128)(2,1)S(1)}, u32[]{:S(2)}, u32[]{:S(2)}) collective-permute-start(s16[256,512]{1,0:T(8,128)(2,1)S(1)} %get-tuple-element.46), channel_id=1, source_target_pairs={{0,1},{1,0},{2,3},{3,2},{4,5},{5,4},{6,7},{7,6},{8,9},{9,8},{10,11... | collective-permute-start | bytes 786440 | tf_op jit(solution)/shard_map/ppermute | solution.py:544
  29.1 3.6 %collective-permute-start.5 = (s16[256,512]{1,0:T(8,128)(2,1)S(1)}, s16[256,512]{1,0:T(8,128)(2,1)S(1)}, u32[]{:S(2)}, u32[]{:S(2)}) collective-permute-start(s16[256,512]{1,0:T(8,128)(2,1)S(1)} %get-tuple-element.43._), channel_id=1, source_target_pairs={{0,1},{1,0},{2,3},{3,2},{4,5},{5,4},{6,7},{7,6},{8,9},{9,8},{10,11... | collective-permute-start | bytes 786440 | tf_op jit(solution)/shard_map/ppermute | solution.py:544
  33.6 14.0 %collective-permute-start.9 = (s16[512,512]{1,0:T(8,128)(2,1)S(1)}, s16[512,512]{1,0:T(8,128)(2,1)S(1)}, u32[]{:S(2)}, u32[]{:S(2)}) collective-permute-start(s16[512,512]{1,0:T(8,128)(2,1)S(1)} %near_zero_other.1), channel_id=1, source_target_pairs={{0,2},{2,0},{4,6},{6,4},{8,10},{10,8},{12,14},{14,12},{1,3},{3,1},... | collective-permute-start | bytes 1572872 | tf_op jit(solution)/shard_map/ppermute | solution.py:544
  36.2 16.4 %collective-permute-start.2 = (s16[144,512]{1,0:T(8,128)(2,1)S(1)}, s16[144,512]{1,0:T(8,128)(2,1)S(1)}, u32[]{:S(2)}, u32[]{:S(2)}) collective-permute-start(s16[144,512]{1,0:T(8,128)(2,1)S(1)} %get-tuple-element.37), channel_id=1, source_target_pairs={{0,8},{2,10},{4,12},{6,14},{8,0},{10,2},{12,4},{14,6},{1,9},{3,11}... | collective-permute-start | bytes 442376 | tf_op jit(solution)/shard_map/ppermute | solution.py:544
  39.1 13.7 %collective-permute-start.3 = (s16[144,512]{1,0:T(8,128)(2,1)S(1)}, s16[144,512]{1,0:T(8,128)(2,1)S(1)}, u32[]{:S(2)}, u32[]{:S(2)}) collective-permute-start(s16[144,512]{1,0:T(8,128)(2,1)S(1)} %get-tuple-element.38), channel_id=1, source_target_pairs={{0,12},{2,14},{4,8},{6,10},{8,4},{10,6},{12,0},{14,2},{1,13},{3,15... | collective-permute-start | bytes 442376 | tf_op jit(solution)/shard_map/ppermute | solution.py:544
  40.4 12.4 %collective-permute-start.4 = (s16[144,512]{1,0:T(8,128)(2,1)S(1)}, s16[144,512]{1,0:T(8,128)(2,1)S(1)}, u32[]{:S(2)}, u32[]{:S(2)}) collective-permute-start(s16[144,512]{1,0:T(8,128)(2,1)S(1)} %get-tuple-element.39), channel_id=1, source_target_pairs={{0,4},{2,6},{4,0},{6,2},{8,12},{10,14},{12,8},{14,10},{1,5},{3,7},... | collective-permute-start | bytes 442376 | tf_op jit(solution)/shard_map/ppermute | solution.py:544
  48.6 12.5 %collective-permute-start.10 = (s16[128,512]{1,0:T(8,128)(2,1)S(1)}, s16[128,512]{1,0:T(8,128)(2,1)S(1)}, u32[]{:S(2)}, u32[]{:S(2)}) collective-permute-start(s16[128,512]{1,0:T(8,128)(2,1)S(1)} %get-tuple-element.48), channel_id=1, source_target_pairs={{0,8},{2,10},{4,12},{6,14},{8,0},{10,2},{12,4},{14,6},{1,9},{3,11}... | collective-permute-start | bytes 393224 | tf_op jit(solution)/shard_map/ppermute | solution.py:544
  51.2 9.9 %collective-permute-start.11 = (s16[128,512]{1,0:T(8,128)(2,1)S(1)}, s16[128,512]{1,0:T(8,128)(2,1)S(1)}, u32[]{:S(2)}, u32[]{:S(2)}) collective-permute-start(s16[128,512]{1,0:T(8,128)(2,1)S(1)} %get-tuple-element.49), channel_id=1, source_target_pairs={{0,12},{2,14},{4,8},{6,10},{8,4},{10,6},{12,0},{14,2},{1,13},{3,15... | collective-permute-start | bytes 393224 | tf_op jit(solution)/shard_map/ppermute | solution.py:544
  52.6 9.2 %collective-permute-start.12 = (s16[128,512]{1,0:T(8,128)(2,1)S(1)}, s16[128,512]{1,0:T(8,128)(2,1)S(1)}, u32[]{:S(2)}, u32[]{:S(2)}) collective-permute-start(s16[128,512]{1,0:T(8,128)(2,1)S(1)} %get-tuple-element.50), channel_id=1, source_target_pairs={{0,4},{2,6},{4,0},{6,2},{8,12},{10,14},{12,8},{14,10},{1,5},{3,7},... | collective-permute-start | bytes 393224 | tf_op jit(solution)/shard_map/ppermute | solution.py:544

commit v7 on v6

--- a/solution.py
+++ b/solution.py
@@ -8,7 +8,7 @@
 from jax.sharding import PartitionSpec as P
 
 LAG = 500
-FRAME_TILE = 512
+FRAME_TILE = 640
 FEATURE_TILE = 256
 DEPTH_UNIT = 256
 SLOPE = 6.0 * 1.4426950408889634
@@ -21,7 +21,7 @@
 LANES = 128
 LONG = 1 << 34
 SHORT = 1 << 20
-SPLIT = 4
+SPLIT = 2
 VMEM = 12 * 1024 * 1024
 WHOLE = pl.BlockSpec(memory_space=pltpu.VMEM)
 SCALARS = pl.BlockSpec(memory_space=pltpu.SMEM)

time: 63 us -> 62.8 us (level)
    ppermute x13 -> x11, starting transfers between devices: 13.3 us -> 12.7 us  [swap(): return lax.ppermute(array, axis, exclusive(lax.axis_size(axis), distance))]
    ppermute x13 -> x11, waiting for transfers between devices: 14.7 us -> 15 us  [swap(): return lax.ppermute(array, axis, exclusive(lax.axis_size(axis), distance))]
  transfers between devices with their start and end apart: 13 -> 11, of which waited for: 4 -> 3; matrix products, arithmetic and copies ran while one was open for 0% -> 0% of each run, Pallas kernels for 28% -> 28%
where the time goes in v7:
time: 62.8 us; the launch traced here: 62.3 us
  Pallas kernels  33.8 us (54%)
  waiting for transfers between devices  15 us (24%)
  starting transfers between devices  12.7 us (20%)
  between operations  0.75 us (1%)
    ppermute x11, waiting for transfers between devices, swap(): return lax.ppermute(array, axis, exclusive(lax.axis_size(axis), distance))  15 us
    pallas_call x1, Pallas kernels, contacts_call(): pl.pallas_call(contacts_kernel, grid=(rows // FRAME_TILE,), in_specs=[SCA...  14.6 us
    ppermute x11, starting transfers between devices, swap(): return lax.ppermute(array, axis, exclusive(lax.axis_size(axis), distance))  12.7 us
    pallas_call x6, Pallas kernels, part_call(): pl.pallas_call(functools.partial(body, block=block), in_specs=[WHOLE] * l...  7.81 us
    pallas_call x2, Pallas kernels, gram_call(): pl.pallas_call(body, in_specs=[WHOLE] * len(operands) + [pl.BlockSpec(mem...  6.44 us
    pallas_call x2, Pallas kernels, far_call(): pl.pallas_call(functools.partial(far_kernel, lagged=lagged, block=block,...  2.27 us
    pallas_call x1, Pallas kernels, finish_lag(): pl.pallas_call(functools.partial(finish_lag_kernel, far=far), in_specs=[W...  1.8 us
  transfers between devices with their start and end apart: 11, of which 3 were waited for; matrix products, arithmetic and copies ran while one was open for 0% of the time, Pallas kernels for 28%

profile of v7, /device:TPU:0, one launch (start us, length us, event | category | flops | bytes accessed | tf_op | source)
XLA Modules:
  0.0 62.3 jit_solution(14245749810051886300)
XLA Ops:
  0.6 14.6 %contacts_sent_lag.1 = (bf16[2560,1024]{1,0:T(8,128)(2,1)S(1)}, f32[8,1024]{1,0:T(8,128)S(1)}, s16[1040,512]{1,0:T(8,128)(2,1)S(1)}, f32[8,128]{1,0:T(8,128)S(1)}) custom-call(s32[16]{0:T(128)} %lengths_ref.1, s32[2,1024]{1,0:T(2,128)} %pairs_ref.1, bf16[3,2516,256]{2,1,0:T(8,128)(2,1)} %bitcast.1), custom_call_target="tpu_custom_call" | custom-call | tf_op jit(solution)/shard_map/contacts_sent_lag/pallas_call | solution.py:208
  15.2 0.5 collective-permute-start
  15.7 2.3 %kept_lag_other.1 = (f32[512,512]{1,0:T(8,128)S(1)}, bf16[2048,512]{1,0:T(8,128)(2,1)S(1)}) custom-call(f32[8,128]{1,0:T(8,128)S(1)} %get-tuple-element.25.counts_ref, bf16[2560,1024]{1,0:T(8,128)(2,1)S(1)} %get-tuple-element.26.features_ref, f32[8,1024]{1,0:T(8,128)S(1)} %get-tuple-element.27.stats_ref, s16[1040,512]{1,0:T(8,128)(2,1)S(1)} %get-tuple-element.28._), custom_call_target="tpu_custom_call" | custom-call | flops 17179869184 | bytes 16777216 | tf_op jit(solution)/shard_map/kept_lag_other/pallas_call | solution.py:295
  18.1 0.0 collective-permute-done.came_ref
  18.1 1.0 %near_lag_other.1 = (s16[528,512]{1,0:T(8,128)(2,1)S(1)}, f32[8,1024]{1,0:T(8,128)S(1)}) custom-call(f32[8,128]{1,0:T(8,128)S(1)} %get-tuple-element.25.counts_ref, f32[512,512]{1,0:T(8,128)S(1)} %get-tuple-element.30.kept_ref, f32[8,1024]{1,0:T(8,128)S(1)} %get-tuple-element.27.stats_ref, s16[1040,512]{1,0:T(8,128)(2,1)S(1)} %collective-permute-done.came_ref), custom_call_target="tpu_custom_call" | custom-call | flops 1048576 | bytes 1024 | tf_op jit(solution)/shard_map/near_lag_other/pallas_call | solution.py:295
  19.1 2.9 %collective-permute-start.1 = (s16[528,512]{1,0:T(8,128)(2,1)S(1)}, s16[528,512]{1,0:T(8,128)(2,1)S(1)}, u32[]{:S(2)}, u32[]{:S(2)}) collective-permute-start(s16[528,512]{1,0:T(8,128)(2,1)S(1)} %get-tuple-element.31._), channel_id=1, source_target_pairs={{0,2},{2,0},{4,6},{6,4},{8,10},{10,8},{12,14},{14,12},{1,3},{3,1},... | collective-permute-start | bytes 1622024 | tf_op jit(solution)/shard_map/ppermute | solution.py:544
  22.0 2.3 %kept_lag_own.1.kept_ref = f32[512,512]{1,0:T(8,128)S(1)} custom-call(f32[8,128]{1,0:T(8,128)S(1)} %get-tuple-element.25.counts_ref, bf16[2560,1024]{1,0:T(8,128)(2,1)S(1)} %get-tuple-element.26.features_ref, f32[8,1024]{1,0:T(8,128)S(1)} %get-tuple-element.27.stats_ref, bf16[2048,512]{1,0:T(8,128)(2,1)S(1)} %get-tuple-element.29.right_ref, ...), custom_call_target="tpu_custom_call" | custom-call | flops 1048576 | bytes 1024 | tf_op jit(solution)/shard_map/kept_lag_own/pallas_call | solution.py:295
  24.4 0.6 near_lag_own.1.keep_ref._
  24.9 3.3 %sent_zero.1 = (s16[512,512]{1,0:T(8,128)(2,1)S(1)}, s16[512,512]{1,0:T(8,128)(2,1)S(1)}) custom-call(f32[8,128]{1,0:T(8,128)S(1)} %get-tuple-element.25.counts_ref, bf16[2560,1024]{1,0:T(8,128)(2,1)S(1)} %get-tuple-element.26.features_ref, f32[8,1024]{1,0:T(8,128)S(1)} %get-tuple-element.27.stats_ref, f32[512,512]{1,0:T(8,128)S(1)} %near_lag_own.1.keep_ref._), custom_call_target="tpu_custom_call" | custom-call | flops 1048576 | bytes 1024 | tf_op jit(solution)/shard_map/sent_zero/pallas_call | solution.py:354
  28.3 0.1 collective-permute-start.6
  28.3 0.5 collective-permute-start.5
  28.8 3.1 %kept_zero.1.kept_ref = f32[1024,512]{1,0:T(8,128)S(1)} custom-call(f32[8,128]{1,0:T(8,128)S(1)} %get-tuple-element.25.counts_ref, bf16[2560,1024]{1,0:T(8,128)(2,1)S(1)} %get-tuple-element.26.features_ref, f32[8,1024]{1,0:T(8,128)S(1)} %get-tuple-element.27.stats_ref, s16[512,512]{1,0:T(8,128)(2,1)S(1)} %get-tuple-element.41._), custom_call_target="tpu_custom_call" | custom-call | flops 1048576 | bytes 1024 | tf_op jit(solution)/shard_map/kept_zero/pallas_call | solution.py:354
  32.0 0.0 collective-permute-done.6.refs_1_
  32.0 0.0 collective-permute-done.5.refs_0_
  32.0 0.9 %near_zero_other.1 = s16[512,512]{1,0:T(8,128)(2,1)S(1)} custom-call(f32[8,128]{1,0:T(8,128)S(1)} %get-tuple-element.25.counts_ref, f32[1024,512]{1,0:T(8,128)S(1)} %kept_zero.1.kept_ref, f32[8,1024]{1,0:T(8,128)S(1)} %get-tuple-element.32.info_ref, s16[512,512]{1,0:T(8,128)(2,1)S(1)} %collective-permute-done.5.refs_0_, ...), custom_call_target="tpu_custom_call" | custom-call | flops 1048576 | bytes 1024 | tf_op jit(solution)/shard_map/near_zero_other/pallas_call | solution.py:295
  32.9 0.1 collective-permute-start.7
  33.0 1.7 %collective-permute-done.1.came_ref = s16[528,512]{1,0:T(8,128)(2,1)S(1)} collective-permute-done((s16[528,512]{1,0:T(8,128)(2,1)S(1)}, s16[528,512]{1,0:T(8,128)(2,1)S(1)}, u32[]{:S(2)}, u32[]{:S(2)}) %collective-permute-start.1) | collective-permute-done | bytes 540704 | tf_op jit(solution)/shard_map/ppermute | solution.py:544
  34.7 1.3 %far_lag.1 = (f32[128,512]{1,0:T(8,128)S(1)}, s16[144,512]{1,0:T(8,128)(2,1)S(1)}, s16[144,512]{1,0:T(8,128)(2,1)S(1)}, s16[144,512]{1,0:T(8,128)(2,1)S(1)}, f32[8,1024]{1,0:T(8,128)S(1)}) custom-call(f32[8,128]{1,0:T(8,128)S(1)} %get-tuple-element.25.counts_ref, f32[512,512]{1,0:T(8,128)S(1)} %near_lag_own.1.keep_ref._, ...), custom_call_target="tpu_custom_call" | custom-call | flops 17179869184 | bytes 16777216 | tf_op jit(solution)/shard_map/far_lag/pallas_call | solution.py:432
  36.0 2.9 %collective-permute-start.2 = (s16[144,512]{1,0:T(8,128)(2,1)S(1)}, s16[144,512]{1,0:T(8,128)(2,1)S(1)}, u32[]{:S(2)}, u32[]{:S(2)}) collective-permute-start(s16[144,512]{1,0:T(8,128)(2,1)S(1)} %get-tuple-element.35), channel_id=1, source_target_pairs={{0,8},{2,10},{4,12},{6,14},{8,0},{10,2},{12,4},{14,6},{1,9},{3,11}... | collective-permute-start | bytes 442376 | tf_op jit(solution)/shard_map/ppermute | solution.py:544
  38.9 1.3 %collective-permute-start.3 = (s16[144,512]{1,0:T(8,128)(2,1)S(1)}, s16[144,512]{1,0:T(8,128)(2,1)S(1)}, u32[]{:S(2)}, u32[]{:S(2)}) collective-permute-start(s16[144,512]{1,0:T(8,128)(2,1)S(1)} %get-tuple-element.36), channel_id=1, source_target_pairs={{0,12},{2,14},{4,8},{6,10},{8,4},{10,6},{12,0},{14,2},{1,13},{3,15... | collective-permute-start | bytes 442376 | tf_op jit(solution)/shard_map/ppermute | solution.py:544
  40.2 0.2 collective-permute-start.4
  40.5 0.6 %near_zero_own.1.keep_ref = f32[512,512]{1,0:T(8,128)S(1)} custom-call(f32[8,128]{1,0:T(8,128)S(1)} %get-tuple-element.25.counts_ref, f32[1024,512]{1,0:T(8,128)S(1)} %kept_zero.1.kept_ref, f32[8,1024]{1,0:T(8,128)S(1)} %get-tuple-element.32.info_ref, s16[512,512]{1,0:T(8,128)(2,1)S(1)} %collective-permute-done.5.refs_0_, ...), custom_call_target="tpu_custom_call" | custom-call | flops 1048576 | bytes 1024 | tf_op jit(solution)/shard_map/near_zero_own/pallas_call | solution.py:295
  41.1 5.8 %collective-permute-done.7.came_ref = s16[512,512]{1,0:T(8,128)(2,1)S(1)} collective-permute-done((s16[512,512]{1,0:T(8,128)(2,1)S(1)}, s16[512,512]{1,0:T(8,128)(2,1)S(1)}, u32[]{:S(2)}, u32[]{:S(2)}) %collective-permute-start.7) | collective-permute-done | bytes 524320 | tf_op jit(solution)/shard_map/ppermute | solution.py:544
  46.9 0.9 %far_zero.1 = (f32[128,512]{1,0:T(8,128)S(1)}, s16[128,512]{1,0:T(8,128)(2,1)S(1)}, s16[128,512]{1,0:T(8,128)(2,1)S(1)}, s16[128,512]{1,0:T(8,128)(2,1)S(1)}) custom-call(f32[8,128]{1,0:T(8,128)S(1)} %get-tuple-element.25.counts_ref, f32[512,512]{1,0:T(8,128)S(1)} %near_zero_own.1.keep_ref, s16[512,512]{1,0:T(8,128)(2,1)S(1)} %collective-permute-done.7.came_ref, ...), custom_call_target="tpu_custom_call" | custom-call | flops 1048576 | bytes 1024 | tf_op jit(solution)/shard_map/far_zero/pallas_call | solution.py:432
  47.9 2.6 %collective-permute-start.8 = (s16[128,512]{1,0:T(8,128)(2,1)S(1)}, s16[128,512]{1,0:T(8,128)(2,1)S(1)}, u32[]{:S(2)}, u32[]{:S(2)}) collective-permute-start(s16[128,512]{1,0:T(8,128)(2,1)S(1)} %get-tuple-element.44), channel_id=1, source_target_pairs={{0,8},{2,10},{4,12},{6,14},{8,0},{10,2},{12,4},{14,6},{1,9},{3,11}... | collective-permute-start | bytes 393224 | tf_op jit(solution)/shard_map/ppermute | solution.py:544
  50.5 1.3 %collective-permute-start.9 = (s16[128,512]{1,0:T(8,128)(2,1)S(1)}, s16[128,512]{1,0:T(8,128)(2,1)S(1)}, u32[]{:S(2)}, u32[]{:S(2)}) collective-permute-start(s16[128,512]{1,0:T(8,128)(2,1)S(1)} %get-tuple-element.45), channel_id=1, source_target_pairs={{0,12},{2,14},{4,8},{6,10},{8,4},{10,6},{12,0},{14,2},{1,13},{3,15... | collective-permute-start | bytes 393224 | tf_op jit(solution)/shard_map/ppermute | solution.py:544
  51.8 0.0 collective-permute-done.2.refs_0_
  51.8 0.2 collective-permute-start.10
  52.1 0.0 collective-permute-done.3.refs_1_
  52.1 0.0 collective-permute-done.4.refs_2_
  52.1 1.8 %finish_lag.1 = (f32[128,512]{1,0:T(8,128)}, f32[128,512]{1,0:T(8,128)S(1)}, f32[16,1024]{1,0:T(8,128)S(1)}, f32[128,16]{1,0:T(8,128)S(1)}) custom-call(f32[8,128]{1,0:T(8,128)S(1)} %get-tuple-element.25.counts_ref, f32[8,1024]{1,0:T(8,128)S(1)} %get-tuple-element.33.info_ref, f32[128,512]{1,0:T(8,128)S(1)} %get-tuple-element.34.kept_ref, ...), custom_call_target="tpu_custom_call" | custom-call | tf_op jit(solution)/shard_map/finish_lag/pallas_call | solution.py:501
  53.9 7.5 %collective-permute-done.8.refs_0_ = s16[128,512]{1,0:T(8,128)(2,1)S(1)} collective-permute-done((s16[128,512]{1,0:T(8,128)(2,1)S(1)}, s16[128,512]{1,0:T(8,128)(2,1)S(1)}, u32[]{:S(2)}, u32[]{:S(2)}) %collective-permute-start.8) | collective-permute-done | bytes 131104 | tf_op jit(solution)/shard_map/ppermute | solution.py:544
  61.4 0.0 collective-permute-done.9.refs_1_
  61.4 0.0 collective-permute-done.10.refs_2_
  61.4 0.9 %finish_zero.1 = f32[128,512]{1,0:T(8,128)} custom-call(f32[8,128]{1,0:T(8,128)S(1)} %get-tuple-element.25.counts_ref, f32[16,1024]{1,0:T(8,128)S(1)} %get-tuple-element.38.rows_ref, f32[128,16]{1,0:T(8,128)S(1)} %get-tuple-element.39.left_ref, f32[128,512]{1,0:T(8,128)S(1)} %get-tuple-element.40.between_ref, f32[128,512]{1,0:T(8,128)S(1)} %get-tuple-element.43.kept_ref, ...), custom_call_target="tpu_custom_call" | custom-call | tf_op jit(solution)/shard_map/finish_zero/pallas_call | solution.py:520
Async XLA Ops:
  15.2 2.9 %collective-permute-start = (s16[1040,512]{1,0:T(8,128)(2,1)S(1)}, s16[1040,512]{1,0:T(8,128)(2,1)S(1)}, u32[]{:S(2)}, u32[]{:S(2)}) collective-permute-start(s16[1040,512]{1,0:T(8,128)(2,1)S(1)} %get-tuple-element.28._), channel_id=1, source_target_pairs={{0,1},{1,0},{2,3},{3,2},{4,5},{5,4},{6,7},{7,6},{8,9},{9,8},{10,11... | collective-permute-start | bytes 3194888 | tf_op jit(solution)/shard_map/ppermute | solution.py:544
  19.1 15.5 %collective-permute-start.1 = (s16[528,512]{1,0:T(8,128)(2,1)S(1)}, s16[528,512]{1,0:T(8,128)(2,1)S(1)}, u32[]{:S(2)}, u32[]{:S(2)}) collective-permute-start(s16[528,512]{1,0:T(8,128)(2,1)S(1)} %get-tuple-element.31._), channel_id=1, source_target_pairs={{0,2},{2,0},{4,6},{6,4},{8,10},{10,8},{12,14},{14,12},{1,3},{3,1},... | collective-permute-start | bytes 1622024 | tf_op jit(solution)/shard_map/ppermute | solution.py:544
  28.3 3.7 %collective-permute-start.6 = (s16[512,512]{1,0:T(8,128)(2,1)S(1)}, s16[512,512]{1,0:T(8,128)(2,1)S(1)}, u32[]{:S(2)}, u32[]{:S(2)}) collective-permute-start(s16[512,512]{1,0:T(8,128)(2,1)S(1)} %get-tuple-element.42), channel_id=1, source_target_pairs={{0,1},{1,0},{2,3},{3,2},{4,5},{5,4},{6,7},{7,6},{8,9},{9,8},{10,11... | collective-permute-start | bytes 1572872 | tf_op jit(solution)/shard_map/ppermute | solution.py:544
  28.3 3.7 %collective-permute-start.5 = (s16[512,512]{1,0:T(8,128)(2,1)S(1)}, s16[512,512]{1,0:T(8,128)(2,1)S(1)}, u32[]{:S(2)}, u32[]{:S(2)}) collective-permute-start(s16[512,512]{1,0:T(8,128)(2,1)S(1)} %get-tuple-element.41._), channel_id=1, source_target_pairs={{0,1},{1,0},{2,3},{3,2},{4,5},{5,4},{6,7},{7,6},{8,9},{9,8},{10,11... | collective-permute-start | bytes 1572872 | tf_op jit(solution)/shard_map/ppermute | solution.py:544
  32.9 14.0 %collective-permute-start.7 = (s16[512,512]{1,0:T(8,128)(2,1)S(1)}, s16[512,512]{1,0:T(8,128)(2,1)S(1)}, u32[]{:S(2)}, u32[]{:S(2)}) collective-permute-start(s16[512,512]{1,0:T(8,128)(2,1)S(1)} %near_zero_other.1), channel_id=1, source_target_pairs={{0,2},{2,0},{4,6},{6,4},{8,10},{10,8},{12,14},{14,12},{1,3},{3,1},... | collective-permute-start | bytes 1572872 | tf_op jit(solution)/shard_map/ppermute | solution.py:544
  36.0 15.8 %collective-permute-start.2 = (s16[144,512]{1,0:T(8,128)(2,1)S(1)}, s16[144,512]{1,0:T(8,128)(2,1)S(1)}, u32[]{:S(2)}, u32[]{:S(2)}) collective-permute-start(s16[144,512]{1,0:T(8,128)(2,1)S(1)} %get-tuple-element.35), channel_id=1, source_target_pairs={{0,8},{2,10},{4,12},{6,14},{8,0},{10,2},{12,4},{14,6},{1,9},{3,11}... | collective-permute-start | bytes 442376 | tf_op jit(solution)/shard_map/ppermute | solution.py:544
  38.9 13.2 %collective-permute-start.3 = (s16[144,512]{1,0:T(8,128)(2,1)S(1)}, s16[144,512]{1,0:T(8,128)(2,1)S(1)}, u32[]{:S(2)}, u32[]{:S(2)}) collective-permute-start(s16[144,512]{1,0:T(8,128)(2,1)S(1)} %get-tuple-element.36), channel_id=1, source_target_pairs={{0,12},{2,14},{4,8},{6,10},{8,4},{10,6},{12,0},{14,2},{1,13},{3,15... | collective-permute-start | bytes 442376 | tf_op jit(solution)/shard_map/ppermute | solution.py:544
  40.2 11.9 %collective-permute-start.4 = (s16[144,512]{1,0:T(8,128)(2,1)S(1)}, s16[144,512]{1,0:T(8,128)(2,1)S(1)}, u32[]{:S(2)}, u32[]{:S(2)}) collective-permute-start(s16[144,512]{1,0:T(8,128)(2,1)S(1)} %get-tuple-element.37), channel_id=1, source_target_pairs={{0,4},{2,6},{4,0},{6,2},{8,12},{10,14},{12,8},{14,10},{1,5},{3,7},... | collective-permute-start | bytes 442376 | tf_op jit(solution)/shard_map/ppermute | solution.py:544
  47.9 13.5 %collective-permute-start.8 = (s16[128,512]{1,0:T(8,128)(2,1)S(1)}, s16[128,512]{1,0:T(8,128)(2,1)S(1)}, u32[]{:S(2)}, u32[]{:S(2)}) collective-permute-start(s16[128,512]{1,0:T(8,128)(2,1)S(1)} %get-tuple-element.44), channel_id=1, source_target_pairs={{0,8},{2,10},{4,12},{6,14},{8,0},{10,2},{12,4},{14,6},{1,9},{3,11}... | collective-permute-start | bytes 393224 | tf_op jit(solution)/shard_map/ppermute | solution.py:544
  50.5 10.9 %collective-permute-start.9 = (s16[128,512]{1,0:T(8,128)(2,1)S(1)}, s16[128,512]{1,0:T(8,128)(2,1)S(1)}, u32[]{:S(2)}, u32[]{:S(2)}) collective-permute-start(s16[128,512]{1,0:T(8,128)(2,1)S(1)} %get-tuple-element.45), channel_id=1, source_target_pairs={{0,12},{2,14},{4,8},{6,10},{8,4},{10,6},{12,0},{14,2},{1,13},{3,15... | collective-permute-start | bytes 393224 | tf_op jit(solution)/shard_map/ppermute | solution.py:544
  51.8 9.5 %collective-permute-start.10 = (s16[128,512]{1,0:T(8,128)(2,1)S(1)}, s16[128,512]{1,0:T(8,128)(2,1)S(1)}, u32[]{:S(2)}, u32[]{:S(2)}) collective-permute-start(s16[128,512]{1,0:T(8,128)(2,1)S(1)} %get-tuple-element.46), channel_id=1, source_target_pairs={{0,4},{2,6},{4,0},{6,2},{8,12},{10,14},{12,8},{14,10},{1,5},{3,7},... | collective-permute-start | bytes 393224 | tf_op jit(solution)/shard_map/ppermute | solution.py:544

commit v8 on v7

--- a/solution.py
+++ b/solution.py
@@ -23,6 +23,7 @@
 SHORT = 1 << 20
 SPLIT = 2
 VMEM = 12 * 1024 * 1024
+CONTACTS_VMEM = 20 * 1024 * 1024
 WHOLE = pl.BlockSpec(memory_space=pltpu.VMEM)
 SCALARS = pl.BlockSpec(memory_space=pltpu.SMEM)
 
@@ -138,23 +139,9 @@
     )
 
 
-def contacts_kernel(
-    lengths_ref, pairs_ref, coords_ref, features_ref, stats_ref, sent_ref, counts_ref, table_ref, right_ref
-):
-    step = pl.program_id(0)
-    atoms, feats = table_ref.shape
-    tile = coords_ref.shape[1]
-
-    @pl.when(step == 0)
-    def _():
-        atom_ids = lax.broadcasted_iota(jnp.int32, (atoms, feats), 0)
-        first_hit = (atom_ids == pairs_ref[0:1, :]).astype(jnp.float32)
-        second_hit = (atom_ids == pairs_ref[1:2, :]).astype(jnp.float32)
-        table_ref[...] = (first_hit - second_hit).astype(jnp.bfloat16)
-        stats_ref[...] = jnp.zeros_like(stats_ref)
-        count_pairs(lengths_ref, counts_ref)
-
-    live = lengths_ref[own_place()] - LAG
+def contacts_chunk(step, live, frames_ref, table_ref, features_ref, stats_ref):
+    tile = frames_ref.shape[2]
+    feats = table_ref.shape[1]
     frame = step * tile + lax.broadcasted_iota(jnp.int32, (tile, 1), 0)
     used = (frame < live) | ((frame >= LAG) & (frame < live + LAG))
     leads = (step * tile + tile <= live).astype(jnp.float32)
@@ -164,7 +151,7 @@
         weights = table_ref[:, columns]
         squared = None
         for axis in range(3):
-            separation = jnp.dot(coords_ref[axis], weights, preferred_element_type=jnp.float32)
+            separation = jnp.dot(frames_ref[step, axis], weights, preferred_element_type=jnp.float32)
             square = separation * separation
             squared = square if squared is None else squared + square
         squared = jnp.maximum(squared, 1e-30)
@@ -183,35 +170,67 @@
         value = jnp.where(frame < live, features_ref[target, :], 0.0).astype(jnp.float32)
         stats_ref[0:1, :] += jnp.sum(value, axis=0, keepdims=True)
 
-    @pl.when(step == 0)
-    def _():
-        value = features_ref[0:LAG, :].astype(jnp.float32)
-        stats_ref[1:2, :] = -jnp.sum(value, axis=0, keepdims=True)
-
-    @pl.when(step == pl.num_programs(0) - 1)
-    def _():
-        count = live + jnp.minimum(live, LAG)
-        total = stats_ref[2:3, :]
-        squares = stats_ref[3:4, :]
-        stats_ref[1:2, :] += total
-        spread = squares - total * total / count.astype(jnp.float32)
-        stats_ref[2:3, :] = jnp.maximum(spread, 0.0) + (SLACK * squares + FLOOR)
-        gram_half(counts_ref, features_ref, stats_ref, [sent_ref], right_ref, False, True)
-        sent_ref[feats : feats + TAIL, :] = encode(
-            [stats_ref[0:1, :], stats_ref[1:2, :], jnp.sqrt(stats_ref[2:3, :])]
-        )
+
+def contacts_kernel(
+    lengths_ref, pairs_ref, coords_ref, tail_ref, features_ref, stats_ref, sent_ref, counts_ref,
+    table_ref, right_ref, frames_ref, arrived
+):
+    atoms, feats = table_ref.shape
+    chunks, _, tile, _ = frames_ref.shape
+    whole = chunks - 1
+
+    def chunk_copy(step):
+        rows = pl.ds(pl.multiple_of(step * tile, tile), tile)
+        return pltpu.make_async_copy(coords_ref.at[:, rows, :], frames_ref.at[step], arrived.at[step])
+
+    for step in range(whole):
+        chunk_copy(step).start()
+    atom_ids = lax.broadcasted_iota(jnp.int32, (atoms, feats), 0)
+    first_hit = (atom_ids == pairs_ref[0:1, :]).astype(jnp.float32)
+    second_hit = (atom_ids == pairs_ref[1:2, :]).astype(jnp.float32)
+    table_ref[...] = (first_hit - second_hit).astype(jnp.bfloat16)
+    stats_ref[...] = jnp.zeros_like(stats_ref)
+    count_pairs(lengths_ref, counts_ref)
+    frames_ref[whole] = tail_ref[...]
+    live = lengths_ref[own_place()] - LAG
+
+    def one_chunk(index, carry):
+        step = lax.rem(index + whole, chunks)
+
+        @pl.when(index > 0)
+        def _():
+            chunk_copy(step).wait()
+
+        contacts_chunk(step, live, frames_ref, table_ref, features_ref, stats_ref)
+        return carry
+
+    lax.fori_loop(0, chunks, one_chunk, 0)
+    head = jnp.sum(features_ref[0:LAG, :].astype(jnp.float32), axis=0, keepdims=True)
+    count = live + jnp.minimum(live, LAG)
+    total = stats_ref[2:3, :]
+    squares = stats_ref[3:4, :]
+    stats_ref[1:2, :] = total - head
+    spread = squares - total * total / count.astype(jnp.float32)
+    stats_ref[2:3, :] = jnp.maximum(spread, 0.0) + (SLACK * squares + FLOOR)
+    gram_half(counts_ref, features_ref, stats_ref, [sent_ref], right_ref, False, True)
+    sent_ref[feats : feats + TAIL, :] = encode(
+        [stats_ref[0:1, :], stats_ref[1:2, :], jnp.sqrt(stats_ref[2:3, :])]
+    )
 
 
 def contacts_call(coords, lengths, atom_pairs, rows, depth):
     atoms = coords.shape[2]
     feats = atom_pairs.shape[1]
+    chunks = rows // FRAME_TILE
+    assert (chunks - 1) * FRAME_TILE < coords.shape[1] <= rows
     return pl.pallas_call(
         contacts_kernel,
-        grid=(rows // FRAME_TILE,),
+        grid=(1,),
         in_specs=[
             SCALARS,
             pl.BlockSpec((2, feats), lambda i: (0, 0)),
-            pl.BlockSpec((3, FRAME_TILE, atoms), lambda i: (0, i, 0)),
+            pl.BlockSpec(memory_space=pl.ANY),
+            pl.BlockSpec((3, FRAME_TILE, atoms), lambda i: (0, chunks - 1, 0)),
         ],
         out_specs=[WHOLE] * 4,
         out_shape=[
@@ -223,10 +242,12 @@
         scratch_shapes=[
             pltpu.VMEM((atoms, feats), jnp.bfloat16),
             pltpu.VMEM((depth, feats // 2), jnp.bfloat16),
+            pltpu.VMEM((chunks, 3, FRAME_TILE, atoms), jnp.bfloat16),
+            pltpu.SemaphoreType.DMA((chunks,)),
         ],
-        compiler_params=params(),
+        compiler_params=pltpu.CompilerParams(vmem_limit_bytes=CONTACTS_VMEM),
         name="contacts_sent_lag",
-    )(lengths, atom_pairs, coords)
+    )(lengths, atom_pairs, coords, coords)
 
 
 def gram_half(counts_ref, features_ref, stats_ref, out_refs, right_ref, kept, lagged):

time: 62.8 us -> 62.5 us (level)
  transfers between devices with their start and end apart: 11 -> 11, of which waited for: 3 -> 4; matrix products, arithmetic and copies ran while one was open for 0% -> 0% of each run, Pallas kernels for 28% -> 28%
where the time goes in v8:
time: 62.5 us; the launch traced here: 62.1 us
  Pallas kernels  33.7 us (54%)
  waiting for transfers between devices  14.9 us (24%)
  starting transfers between devices  12.7 us (20%)
  between operations  0.75 us (1%)
    ppermute x11, waiting for transfers between devices, swap(): return lax.ppermute(array, axis, exclusive(lax.axis_size(axis), distance))  14.9 us
    pallas_call x1, Pallas kernels, contacts_call(): pl.pallas_call(contacts_kernel, grid=(1,), in_specs=[SCALARS, pl.BlockSpe...  14.4 us
    ppermute x11, starting transfers between devices, swap(): return lax.ppermute(array, axis, exclusive(lax.axis_size(axis), distance))  12.7 us
    pallas_call x6, Pallas kernels, part_call(): pl.pallas_call(functools.partial(body, block=block), in_specs=[WHOLE] * l...  7.83 us
    pallas_call x2, Pallas kernels, gram_call(): pl.pallas_call(body, in_specs=[WHOLE] * len(operands) + [pl.BlockSpec(mem...  6.67 us
    pallas_call x2, Pallas kernels, far_call(): pl.pallas_call(functools.partial(far_kernel, lagged=lagged, block=block,...  2.05 us
    pallas_call x1, Pallas kernels, finish_lag(): pl.pallas_call(functools.partial(finish_lag_kernel, far=far), in_specs=[W...  1.8 us
  transfers between devices with their start and end apart: 11, of which 4 were waited for; matrix products, arithmetic and copies ran while one was open for 0% of the time, Pallas kernels for 28%

profile of v8, /device:TPU:0, one launch (start us, length us, event | category | flops | bytes accessed | tf_op | source)
XLA Modules:
  0.0 62.1 jit_solution(4401315369495273346)
XLA Ops:
  0.6 14.4 %contacts_sent_lag.1 = (bf16[2560,1024]{1,0:T(8,128)(2,1)S(1)}, f32[8,1024]{1,0:T(8,128)S(1)}, s16[1040,512]{1,0:T(8,128)(2,1)S(1)}, f32[8,128]{1,0:T(8,128)S(1)}) custom-call(s32[16]{0:T(128)} %lengths_ref.1, s32[2,1024]{1,0:T(2,128)} %pairs_ref.1, bf16[3,2516,256]{2,1,0:T(8,128)(2,1)} %bitcast.1, bf16[3,2516,256]{2,1,0:T(8,128)(2,1)} %bitcast.2), custom_call_target="tpu_custom_call" | custom-call | tf_op jit(solution)/shard_map/contacts_sent_lag/pallas_call | solution.py:226
  15.0 0.5 collective-permute-start
  15.6 2.4 %kept_lag_other.1 = (f32[512,512]{1,0:T(8,128)S(1)}, bf16[2048,512]{1,0:T(8,128)(2,1)S(1)}) custom-call(f32[8,128]{1,0:T(8,128)S(1)} %get-tuple-element.25.counts_ref, bf16[2560,1024]{1,0:T(8,128)(2,1)S(1)} %get-tuple-element.26.features_ref, f32[8,1024]{1,0:T(8,128)S(1)} %get-tuple-element.27.stats_ref, s16[1040,512]{1,0:T(8,128)(2,1)S(1)} %get-tuple-element.28._), custom_call_target="tpu_custom_call" | custom-call | flops 17179869184 | bytes 16777216 | tf_op jit(solution)/shard_map/kept_lag_other/pallas_call | solution.py:316
  17.9 0.0 collective-permute-done.came_ref
  17.9 1.0 %near_lag_other.1 = (s16[528,512]{1,0:T(8,128)(2,1)S(1)}, f32[8,1024]{1,0:T(8,128)S(1)}) custom-call(f32[8,128]{1,0:T(8,128)S(1)} %get-tuple-element.25.counts_ref, f32[512,512]{1,0:T(8,128)S(1)} %get-tuple-element.30.kept_ref, f32[8,1024]{1,0:T(8,128)S(1)} %get-tuple-element.27.stats_ref, s16[1040,512]{1,0:T(8,128)(2,1)S(1)} %collective-permute-done.came_ref), custom_call_target="tpu_custom_call" | custom-call | flops 1048576 | bytes 1024 | tf_op jit(solution)/shard_map/near_lag_other/pallas_call | solution.py:316
  19.0 2.9 %collective-permute-start.1 = (s16[528,512]{1,0:T(8,128)(2,1)S(1)}, s16[528,512]{1,0:T(8,128)(2,1)S(1)}, u32[]{:S(2)}, u32[]{:S(2)}) collective-permute-start(s16[528,512]{1,0:T(8,128)(2,1)S(1)} %get-tuple-element.31._), channel_id=1, source_target_pairs={{0,2},{2,0},{4,6},{6,4},{8,10},{10,8},{12,14},{14,12},{1,3},{3,1},... | collective-permute-start | bytes 1622024 | tf_op jit(solution)/shard_map/ppermute | solution.py:565
  21.9 2.3 %kept_lag_own.1.kept_ref = f32[512,512]{1,0:T(8,128)S(1)} custom-call(f32[8,128]{1,0:T(8,128)S(1)} %get-tuple-element.25.counts_ref, bf16[2560,1024]{1,0:T(8,128)(2,1)S(1)} %get-tuple-element.26.features_ref, f32[8,1024]{1,0:T(8,128)S(1)} %get-tuple-element.27.stats_ref, bf16[2048,512]{1,0:T(8,128)(2,1)S(1)} %get-tuple-element.29.right_ref, ...), custom_call_target="tpu_custom_call" | custom-call | flops 1048576 | bytes 1024 | tf_op jit(solution)/shard_map/kept_lag_own/pallas_call | solution.py:316
  24.2 0.6 near_lag_own.1.keep_ref._
  24.8 3.3 %sent_zero.1 = (s16[512,512]{1,0:T(8,128)(2,1)S(1)}, s16[512,512]{1,0:T(8,128)(2,1)S(1)}) custom-call(f32[8,128]{1,0:T(8,128)S(1)} %get-tuple-element.25.counts_ref, bf16[2560,1024]{1,0:T(8,128)(2,1)S(1)} %get-tuple-element.26.features_ref, f32[8,1024]{1,0:T(8,128)S(1)} %get-tuple-element.27.stats_ref, f32[512,512]{1,0:T(8,128)S(1)} %near_lag_own.1.keep_ref._), custom_call_target="tpu_custom_call" | custom-call | flops 1048576 | bytes 1024 | tf_op jit(solution)/shard_map/sent_zero/pallas_call | solution.py:375
  28.1 0.1 collective-permute-start.6
  28.2 0.5 collective-permute-start.5
  28.7 3.4 %kept_zero.1.kept_ref = f32[1024,512]{1,0:T(8,128)S(1)} custom-call(f32[8,128]{1,0:T(8,128)S(1)} %get-tuple-element.25.counts_ref, bf16[2560,1024]{1,0:T(8,128)(2,1)S(1)} %get-tuple-element.26.features_ref, f32[8,1024]{1,0:T(8,128)S(1)} %get-tuple-element.27.stats_ref, s16[512,512]{1,0:T(8,128)(2,1)S(1)} %get-tuple-element.41._), custom_call_target="tpu_custom_call" | custom-call | flops 1048576 | bytes 1024 | tf_op jit(solution)/shard_map/kept_zero/pallas_call | solution.py:375
  32.0 0.0 collective-permute-done.6.refs_1_
  32.1 0.0 collective-permute-done.5.refs_0_
  32.1 0.9 %near_zero_other.1 = s16[512,512]{1,0:T(8,128)(2,1)S(1)} custom-call(f32[8,128]{1,0:T(8,128)S(1)} %get-tuple-element.25.counts_ref, f32[1024,512]{1,0:T(8,128)S(1)} %kept_zero.1.kept_ref, f32[8,1024]{1,0:T(8,128)S(1)} %get-tuple-element.32.info_ref, s16[512,512]{1,0:T(8,128)(2,1)S(1)} %collective-permute-done.5.refs_0_, ...), custom_call_target="tpu_custom_call" | custom-call | flops 1048576 | bytes 1024 | tf_op jit(solution)/shard_map/near_zero_other/pallas_call | solution.py:316
  33.0 0.1 collective-permute-start.7
  33.1 1.4 %collective-permute-done.1.came_ref = s16[528,512]{1,0:T(8,128)(2,1)S(1)} collective-permute-done((s16[528,512]{1,0:T(8,128)(2,1)S(1)}, s16[528,512]{1,0:T(8,128)(2,1)S(1)}, u32[]{:S(2)}, u32[]{:S(2)}) %collective-permute-start.1) | collective-permute-done | bytes 540704 | tf_op jit(solution)/shard_map/ppermute | solution.py:565
  34.5 1.1 %far_lag.1 = (f32[128,512]{1,0:T(8,128)S(1)}, s16[144,512]{1,0:T(8,128)(2,1)S(1)}, s16[144,512]{1,0:T(8,128)(2,1)S(1)}, s16[144,512]{1,0:T(8,128)(2,1)S(1)}, f32[8,1024]{1,0:T(8,128)S(1)}) custom-call(f32[8,128]{1,0:T(8,128)S(1)} %get-tuple-element.25.counts_ref, f32[512,512]{1,0:T(8,128)S(1)} %near_lag_own.1.keep_ref._, ...), custom_call_target="tpu_custom_call" | custom-call | flops 17179869184 | bytes 16777216 | tf_op jit(solution)/shard_map/far_lag/pallas_call | solution.py:453
  35.6 2.9 %collective-permute-start.2 = (s16[144,512]{1,0:T(8,128)(2,1)S(1)}, s16[144,512]{1,0:T(8,128)(2,1)S(1)}, u32[]{:S(2)}, u32[]{:S(2)}) collective-permute-start(s16[144,512]{1,0:T(8,128)(2,1)S(1)} %get-tuple-element.35), channel_id=1, source_target_pairs={{0,8},{2,10},{4,12},{6,14},{8,0},{10,2},{12,4},{14,6},{1,9},{3,11}... | collective-permute-start | bytes 442376 | tf_op jit(solution)/shard_map/ppermute | solution.py:565
  38.5 1.3 %collective-permute-start.3 = (s16[144,512]{1,0:T(8,128)(2,1)S(1)}, s16[144,512]{1,0:T(8,128)(2,1)S(1)}, u32[]{:S(2)}, u32[]{:S(2)}) collective-permute-start(s16[144,512]{1,0:T(8,128)(2,1)S(1)} %get-tuple-element.36), channel_id=1, source_target_pairs={{0,12},{2,14},{4,8},{6,10},{8,4},{10,6},{12,0},{14,2},{1,13},{3,15... | collective-permute-start | bytes 442376 | tf_op jit(solution)/shard_map/ppermute | solution.py:565
  39.9 0.2 collective-permute-start.4
  40.1 0.6 %near_zero_own.1.keep_ref = f32[512,512]{1,0:T(8,128)S(1)} custom-call(f32[8,128]{1,0:T(8,128)S(1)} %get-tuple-element.25.counts_ref, f32[1024,512]{1,0:T(8,128)S(1)} %kept_zero.1.kept_ref, f32[8,1024]{1,0:T(8,128)S(1)} %get-tuple-element.32.info_ref, s16[512,512]{1,0:T(8,128)(2,1)S(1)} %collective-permute-done.5.refs_0_, ...), custom_call_target="tpu_custom_call" | custom-call | flops 1048576 | bytes 1024 | tf_op jit(solution)/shard_map/near_zero_own/pallas_call | solution.py:316
  40.7 6.3 %collective-permute-done.7.came_ref = s16[512,512]{1,0:T(8,128)(2,1)S(1)} collective-permute-done((s16[512,512]{1,0:T(8,128)(2,1)S(1)}, s16[512,512]{1,0:T(8,128)(2,1)S(1)}, u32[]{:S(2)}, u32[]{:S(2)}) %collective-permute-start.7) | collective-permute-done | bytes 524320 | tf_op jit(solution)/shard_map/ppermute | solution.py:565
  47.0 0.9 %far_zero.1 = (f32[128,512]{1,0:T(8,128)S(1)}, s16[128,512]{1,0:T(8,128)(2,1)S(1)}, s16[128,512]{1,0:T(8,128)(2,1)S(1)}, s16[128,512]{1,0:T(8,128)(2,1)S(1)}) custom-call(f32[8,128]{1,0:T(8,128)S(1)} %get-tuple-element.25.counts_ref, f32[512,512]{1,0:T(8,128)S(1)} %near_zero_own.1.keep_ref, s16[512,512]{1,0:T(8,128)(2,1)S(1)} %collective-permute-done.7.came_ref, ...), custom_call_target="tpu_custom_call" | custom-call | flops 1048576 | bytes 1024 | tf_op jit(solution)/shard_map/far_zero/pallas_call | solution.py:453
  47.9 2.6 %collective-permute-start.8 = (s16[128,512]{1,0:T(8,128)(2,1)S(1)}, s16[128,512]{1,0:T(8,128)(2,1)S(1)}, u32[]{:S(2)}, u32[]{:S(2)}) collective-permute-start(s16[128,512]{1,0:T(8,128)(2,1)S(1)} %get-tuple-element.44), channel_id=1, source_target_pairs={{0,8},{2,10},{4,12},{6,14},{8,0},{10,2},{12,4},{14,6},{1,9},{3,11}... | collective-permute-start | bytes 393224 | tf_op jit(solution)/shard_map/ppermute | solution.py:565
  50.6 1.4 %collective-permute-start.9 = (s16[128,512]{1,0:T(8,128)(2,1)S(1)}, s16[128,512]{1,0:T(8,128)(2,1)S(1)}, u32[]{:S(2)}, u32[]{:S(2)}) collective-permute-start(s16[128,512]{1,0:T(8,128)(2,1)S(1)} %get-tuple-element.45), channel_id=1, source_target_pairs={{0,12},{2,14},{4,8},{6,10},{8,4},{10,6},{12,0},{14,2},{1,13},{3,15... | collective-permute-start | bytes 393224 | tf_op jit(solution)/shard_map/ppermute | solution.py:565
  51.9 0.0 collective-permute-done.2.refs_0_
  51.9 0.2 collective-permute-start.10
  52.1 0.0 collective-permute-done.3.refs_1_
  52.2 0.0 collective-permute-done.4.refs_2_
  52.2 1.8 %finish_lag.1 = (f32[128,512]{1,0:T(8,128)}, f32[128,512]{1,0:T(8,128)S(1)}, f32[16,1024]{1,0:T(8,128)S(1)}, f32[128,16]{1,0:T(8,128)S(1)}) custom-call(f32[8,128]{1,0:T(8,128)S(1)} %get-tuple-element.25.counts_ref, f32[8,1024]{1,0:T(8,128)S(1)} %get-tuple-element.33.info_ref, f32[128,512]{1,0:T(8,128)S(1)} %get-tuple-element.34.kept_ref, ...), custom_call_target="tpu_custom_call" | custom-call | tf_op jit(solution)/shard_map/finish_lag/pallas_call | solution.py:522
  54.0 6.7 %collective-permute-done.8.refs_0_ = s16[128,512]{1,0:T(8,128)(2,1)S(1)} collective-permute-done((s16[128,512]{1,0:T(8,128)(2,1)S(1)}, s16[128,512]{1,0:T(8,128)(2,1)S(1)}, u32[]{:S(2)}, u32[]{:S(2)}) %collective-permute-start.8) | collective-permute-done | bytes 131104 | tf_op jit(solution)/shard_map/ppermute | solution.py:565
  60.6 0.0 collective-permute-done.9.refs_1_
  60.6 0.5 collective-permute-done.10.refs_2_
  61.1 0.9 %finish_zero.1 = f32[128,512]{1,0:T(8,128)} custom-call(f32[8,128]{1,0:T(8,128)S(1)} %get-tuple-element.25.counts_ref, f32[16,1024]{1,0:T(8,128)S(1)} %get-tuple-element.38.rows_ref, f32[128,16]{1,0:T(8,128)S(1)} %get-tuple-element.39.left_ref, f32[128,512]{1,0:T(8,128)S(1)} %get-tuple-element.40.between_ref, f32[128,512]{1,0:T(8,128)S(1)} %get-tuple-element.43.kept_ref, ...), custom_call_target="tpu_custom_call" | custom-call | tf_op jit(solution)/shard_map/finish_zero/pallas_call | solution.py:541
Async XLA Ops:
  15.0 2.9 %collective-permute-start = (s16[1040,512]{1,0:T(8,128)(2,1)S(1)}, s16[1040,512]{1,0:T(8,128)(2,1)S(1)}, u32[]{:S(2)}, u32[]{:S(2)}) collective-permute-start(s16[1040,512]{1,0:T(8,128)(2,1)S(1)} %get-tuple-element.28._), channel_id=1, source_target_pairs={{0,1},{1,0},{2,3},{3,2},{4,5},{5,4},{6,7},{7,6},{8,9},{9,8},{10,11... | collective-permute-start | bytes 3194888 | tf_op jit(solution)/shard_map/ppermute | solution.py:565
  19.0 15.5 %collective-permute-start.1 = (s16[528,512]{1,0:T(8,128)(2,1)S(1)}, s16[528,512]{1,0:T(8,128)(2,1)S(1)}, u32[]{:S(2)}, u32[]{:S(2)}) collective-permute-start(s16[528,512]{1,0:T(8,128)(2,1)S(1)} %get-tuple-element.31._), channel_id=1, source_target_pairs={{0,2},{2,0},{4,6},{6,4},{8,10},{10,8},{12,14},{14,12},{1,3},{3,1},... | collective-permute-start | bytes 1622024 | tf_op jit(solution)/shard_map/ppermute | solution.py:565
  28.1 3.9 %collective-permute-start.6 = (s16[512,512]{1,0:T(8,128)(2,1)S(1)}, s16[512,512]{1,0:T(8,128)(2,1)S(1)}, u32[]{:S(2)}, u32[]{:S(2)}) collective-permute-start(s16[512,512]{1,0:T(8,128)(2,1)S(1)} %get-tuple-element.42), channel_id=1, source_target_pairs={{0,1},{1,0},{2,3},{3,2},{4,5},{5,4},{6,7},{7,6},{8,9},{9,8},{10,11... | collective-permute-start | bytes 1572872 | tf_op jit(solution)/shard_map/ppermute | solution.py:565
  28.2 3.9 %collective-permute-start.5 = (s16[512,512]{1,0:T(8,128)(2,1)S(1)}, s16[512,512]{1,0:T(8,128)(2,1)S(1)}, u32[]{:S(2)}, u32[]{:S(2)}) collective-permute-start(s16[512,512]{1,0:T(8,128)(2,1)S(1)} %get-tuple-element.41._), channel_id=1, source_target_pairs={{0,1},{1,0},{2,3},{3,2},{4,5},{5,4},{6,7},{7,6},{8,9},{9,8},{10,11... | collective-permute-start | bytes 1572872 | tf_op jit(solution)/shard_map/ppermute | solution.py:565
  33.0 14.0 %collective-permute-start.7 = (s16[512,512]{1,0:T(8,128)(2,1)S(1)}, s16[512,512]{1,0:T(8,128)(2,1)S(1)}, u32[]{:S(2)}, u32[]{:S(2)}) collective-permute-start(s16[512,512]{1,0:T(8,128)(2,1)S(1)} %near_zero_other.1), channel_id=1, source_target_pairs={{0,2},{2,0},{4,6},{6,4},{8,10},{10,8},{12,14},{14,12},{1,3},{3,1},... | collective-permute-start | bytes 1572872 | tf_op jit(solution)/shard_map/ppermute | solution.py:565
  35.6 16.3 %collective-permute-start.2 = (s16[144,512]{1,0:T(8,128)(2,1)S(1)}, s16[144,512]{1,0:T(8,128)(2,1)S(1)}, u32[]{:S(2)}, u32[]{:S(2)}) collective-permute-start(s16[144,512]{1,0:T(8,128)(2,1)S(1)} %get-tuple-element.35), channel_id=1, source_target_pairs={{0,8},{2,10},{4,12},{6,14},{8,0},{10,2},{12,4},{14,6},{1,9},{3,11}... | collective-permute-start | bytes 442376 | tf_op jit(solution)/shard_map/ppermute | solution.py:565
  38.5 13.6 %collective-permute-start.3 = (s16[144,512]{1,0:T(8,128)(2,1)S(1)}, s16[144,512]{1,0:T(8,128)(2,1)S(1)}, u32[]{:S(2)}, u32[]{:S(2)}) collective-permute-start(s16[144,512]{1,0:T(8,128)(2,1)S(1)} %get-tuple-element.36), channel_id=1, source_target_pairs={{0,12},{2,14},{4,8},{6,10},{8,4},{10,6},{12,0},{14,2},{1,13},{3,15... | collective-permute-start | bytes 442376 | tf_op jit(solution)/shard_map/ppermute | solution.py:565
  39.9 12.3 %collective-permute-start.4 = (s16[144,512]{1,0:T(8,128)(2,1)S(1)}, s16[144,512]{1,0:T(8,128)(2,1)S(1)}, u32[]{:S(2)}, u32[]{:S(2)}) collective-permute-start(s16[144,512]{1,0:T(8,128)(2,1)S(1)} %get-tuple-element.37), channel_id=1, source_target_pairs={{0,4},{2,6},{4,0},{6,2},{8,12},{10,14},{12,8},{14,10},{1,5},{3,7},... | collective-permute-start | bytes 442376 | tf_op jit(solution)/shard_map/ppermute | solution.py:565
  47.9 12.7 %collective-permute-start.8 = (s16[128,512]{1,0:T(8,128)(2,1)S(1)}, s16[128,512]{1,0:T(8,128)(2,1)S(1)}, u32[]{:S(2)}, u32[]{:S(2)}) collective-permute-start(s16[128,512]{1,0:T(8,128)(2,1)S(1)} %get-tuple-element.44), channel_id=1, source_target_pairs={{0,8},{2,10},{4,12},{6,14},{8,0},{10,2},{12,4},{14,6},{1,9},{3,11}... | collective-permute-start | bytes 393224 | tf_op jit(solution)/shard_map/ppermute | solution.py:565
  50.6 10.1 %collective-permute-start.9 = (s16[128,512]{1,0:T(8,128)(2,1)S(1)}, s16[128,512]{1,0:T(8,128)(2,1)S(1)}, u32[]{:S(2)}, u32[]{:S(2)}) collective-permute-start(s16[128,512]{1,0:T(8,128)(2,1)S(1)} %get-tuple-element.45), channel_id=1, source_target_pairs={{0,12},{2,14},{4,8},{6,10},{8,4},{10,6},{12,0},{14,2},{1,13},{3,15... | collective-permute-start | bytes 393224 | tf_op jit(solution)/shard_map/ppermute | solution.py:565
  51.9 9.2 %collective-permute-start.10 = (s16[128,512]{1,0:T(8,128)(2,1)S(1)}, s16[128,512]{1,0:T(8,128)(2,1)S(1)}, u32[]{:S(2)}, u32[]{:S(2)}) collective-permute-start(s16[128,512]{1,0:T(8,128)(2,1)S(1)} %get-tuple-element.46), channel_id=1, source_target_pairs={{0,4},{2,6},{4,0},{6,2},{8,12},{10,14},{12,8},{14,10},{1,5},{3,7},... | collective-permute-start | bytes 393224 | tf_op jit(solution)/shard_map/ppermute | solution.py:565
